TPU v7x, 32 devices: a whole 2x2x4 slice. The times are simulated.
32 devices in a mesh: grp: 4 (over y, core), blk: 8 (over z, x).
Axes of the slice: x: 2, y: 2, z: 4, core: 2. Of those that a mesh axis runs over, the one named last changes fastest.
Arguments:
- pooled: bfloat16 [8192, 1536], P(('grp', 'blk')), may hold values from -6 to 6
- img_weight: bfloat16 [1536, 1152], P(('grp', 'blk')), may hold values from -0.0048828125 to 0.0048828125
- img_label: int32 [8192], P(('grp', 'blk')), may hold values from 0 to 255, as said below
- text_raw: bfloat16 [256, 1152], P('blk'), may hold values from -0.19921875 to 0.19921875
Outputs:
- grad_weight: float32 [1536, 1152], P(('grp', 'blk'))
- grad_text: float32 [256, 1152], P('blk')
Inputs may be any that keep to these rules, and one draw needn't show every extreme that they name: `img_label`: every text sample is the positive of exactly 32 images.
All inputs are finite; a program needn't handle non-finite values.
Results may differ from a plain program's by a relative error of at most 0.0049.
Values may be sent and summed in bfloat16 or wider, within the bound.
No kernel may reach another device: no remote copies, remote signals or barrier semaphores. Data moves between devices by JAX's collectives and lax.ppermute only.
A program may use at most 64 MiB of HBM per device.

v0:
```python
import jax
import jax.numpy as jnp
from jax import lax
from jax.sharding import PartitionSpec as P

epsilon = 1e-06
logit_scale = 10.0
logit_bias = -5.0


def from_behind(array, axis, by):
    count = lax.axis_size(axis)
    return lax.ppermute(array, axis, [(i, (i + by) % count) for i in range(count)])


def unit_rows(raw_rows):
    inverse = lax.rsqrt(jnp.sum(raw_rows * raw_rows, axis=1, keepdims=True) + epsilon)
    return (raw_rows * inverse, inverse)


def pair_terms(embedded, labels, text_piece, first_row, text_rows):
    logits = (
        logit_scale
        * lax.dot_general(
            embedded, text_piece, (((1,), (1,)), ((), ())), preferred_element_type=jnp.float32
        )
        + logit_bias
    )
    columns = first_row + jnp.arange(text_piece.shape[0], dtype=jnp.int32)
    polarity = jnp.where(labels[:, None] == columns[None, :], 1.0, -1.0).astype(jnp.float32)
    pair_slope = (
        -polarity * jax.nn.sigmoid(-polarity * logits) * (logit_scale / text_rows)
    ).astype(jnp.bfloat16)
    grad_embed = jnp.dot(pair_slope, text_piece, preferred_element_type=jnp.float32)
    grad_piece = lax.dot_general(
        pair_slope, embedded, (((0,), (0,)), ((), ())), preferred_element_type=jnp.float32
    )
    return (grad_embed, grad_piece)


def shards(pooled, img_weight, img_label, text_raw):
    image_rows = pooled.shape[0]
    embed_width = img_weight.shape[1]
    text_rows = text_raw.shape[0]
    window = pooled
    projected = jnp.dot(
        window,
        lax.all_gather(img_weight, ("grp", "blk"), axis=0, tiled=True),
        preferred_element_type=jnp.float32,
    )
    embed_float, inverse = unit_rows(projected)
    embedded = embed_float.astype(jnp.bfloat16)
    text_float, text_inverse = unit_rows(text_raw.astype(jnp.float32))
    text_unit = text_float.astype(jnp.bfloat16)
    cycle_size = lax.axis_size("blk")
    position = lax.axis_index("blk")
    embed_zero = jnp.zeros((image_rows, embed_width), jnp.float32)

    def cycle_turn(turn_index, carried):
        text_piece, piece_sum, grad_embed = carried
        anchor = (position - turn_index) % cycle_size
        piece_embed, piece_grad = pair_terms(
            embedded, img_label, text_piece, anchor * text_rows, text_rows
        )
        piece_sum = from_behind(piece_sum + piece_grad, "blk", 1)
        text_piece = from_behind(text_piece, "blk", 1)
        return (text_piece, piece_sum, grad_embed + piece_embed)

    start_sum = jnp.zeros((text_rows, embed_width), jnp.float32)
    carried = lax.fori_loop(0, cycle_size, cycle_turn, (text_unit, start_sum, embed_zero))
    grad_home = carried[1]
    grad_embed = carried[2]
    grad_unit = lax.psum(grad_home, "grp")
    grad_text = text_inverse * (
        grad_unit - text_float * jnp.sum(grad_unit * text_float, axis=1, keepdims=True)
    )
    grad_proj = (
        inverse
        * (grad_embed - embed_float * jnp.sum(grad_embed * embed_float, axis=1, keepdims=True))
    ).astype(jnp.bfloat16)
    window = pooled
    grad_weight = lax.psum_scatter(
        lax.dot_general(
            window, grad_proj, (((0,), (0,)), ((), ())), preferred_element_type=jnp.float32
        ),
        ("grp", "blk"),
        scatter_dimension=0,
        tiled=True,
    )
    return (grad_weight, grad_text)


def solution(mesh):
    return jax.shard_map(
        shards,
        mesh=mesh,
        in_specs=(
            P(("grp", "blk"), None),
            P(("grp", "blk"), None),
            P(("grp", "blk")),
            P("blk", None),
        ),
        out_specs=(P(("grp", "blk"), None), P("blk", None)),
        check_vma=False,
    )
```

profile of v0, /device:TPU:0, one launch (start us, length us, event | category | flops | bytes accessed | tf_op | source)
XLA Modules:
  0.0 316.5 jit_solution(11519692439100315899)
XLA Ops:
  7.2 0.7 all-gather.2.cloned.1.call-update
  8.0 1.0 fusion.17
  9.0 1.0 fusion.13
  10.0 64.0 %all-gather.2.cloned.1.call-done = bf16[1536,1152]{1,0:T(8,128)(2,1)} async-done(((bf16[48,1152]{1,0:T(8,128)(2,1)}), bf16[1536,1152]{1,0:T(8,128)(2,1)}) %all-gather.2.cloned.1.call-update) | async-done | bytes 3538960 | tf_op jit(solution)/shard_map/all_gather | solution.py:48
  73.9 3.3 %multiply_reduce_fusion.1 = (f32[256]{0:T(256)S(1)}, f32[256,1152]{1,0:T(8,128)S(1)}) fusion(bf16[256,1536]{1,0:T(8,128)(2,1)S(1)} %copy-done, bf16[1536,1152]{1,0:T(8,128)(2,1)} %all-gather.2.cloned.1.call-done), kind=kOutput, calls=%fused_computation.16 | convolution fusion | flops 906559232 | bytes 5506048 | tf_op jit(solution)/shard_map/dot_general | solution.py:46
  77.2 1.0 copy-done.1
  78.2 0.1 multiply_convert_fusion.1
  78.4 74.8 %while.20 = (s32[]{:T(128)}, bf16[32,1152]{1,0:T(8,128)(2,1)S(1)}, f32[32,1152]{1,0:T(8,128)S(1)}, f32[256,1152]{1,0:T(8,128)S(1)}, s32[256]{0:T(256)S(1)}, /*in...) while((s32[]{:T(128)}, bf16[32,1152]{1,0:T(8,128)(2,1)S(1)}, ...), condition=%wide.region_3.4_spmd.clone, body=%wide.region_2.3_spmd.clone.sunk | while | flops 57348144 | bytes 5064280 | solution.py:70
  78.4 1.5 collective-permute-start
  79.9 0.3 fusion.40
  80.2 0.2 convolution_add_fusion.4
  80.4 1.0 collective-permute-start.1
  81.4 0.5 convolution_add_fusion.5
  82.0 3.6 %collective-permute-done = bf16[32,1152]{1,0:T(8,128)(2,1)S(1)} collective-permute-done((bf16[32,1152]{1,0:T(8,128)(2,1)S(1)}, bf16[32,1152]{1,0:T(8,128)(2,1)S(1)}, u32[]{:S(2)}, u32[]{:S(2)}) %collective-permute-start) | collective-permute-done | bytes 73760 | tf_op jit(solution)/shard_map/while/body/eval_jaxpr/ppermute | solution.py:13
  85.6 3.3 %collective-permute-done.1 = f32[32,1152]{1,0:T(8,128)S(1)} collective-permute-done((f32[32,1152]{1,0:T(8,128)S(1)}, f32[32,1152]{1,0:T(8,128)S(1)}, u32[]{:S(2)}, u32[]{:S(2)}) %collective-permute-start.1) | collective-permute-done | bytes 147488 | tf_op jit(solution)/shard_map/while/body/eval_jaxpr/ppermute | solution.py:13
  88.9 0.3 fusion.40
  89.3 0.2 convolution_add_fusion.4
  89.5 0.6 collective-permute-start.1
  90.1 0.5 convolution_add_fusion.5
  90.6 5.9 %collective-permute-done = bf16[32,1152]{1,0:T(8,128)(2,1)S(1)} collective-permute-done((bf16[32,1152]{1,0:T(8,128)(2,1)S(1)}, bf16[32,1152]{1,0:T(8,128)(2,1)S(1)}, u32[]{:S(2)}, u32[]{:S(2)}) %collective-permute-start) | collective-permute-done | bytes 73760 | tf_op jit(solution)/shard_map/while/body/eval_jaxpr/ppermute | solution.py:13
  96.5 1.6 collective-permute-done.1
  98.1 0.3 fusion.40
  98.4 0.2 convolution_add_fusion.4
  98.7 0.1 collective-permute-start.1
  98.7 0.5 convolution_add_fusion.5
  99.3 5.9 %collective-permute-done = bf16[32,1152]{1,0:T(8,128)(2,1)S(1)} collective-permute-done((bf16[32,1152]{1,0:T(8,128)(2,1)S(1)}, bf16[32,1152]{1,0:T(8,128)(2,1)S(1)}, u32[]{:S(2)}, u32[]{:S(2)}) %collective-permute-start) | collective-permute-done | bytes 73760 | tf_op jit(solution)/shard_map/while/body/eval_jaxpr/ppermute | solution.py:13
  105.1 1.6 collective-permute-done.1
  106.8 0.3 fusion.40
  107.1 0.2 convolution_add_fusion.4
  107.3 0.1 collective-permute-start.1
  107.4 0.5 convolution_add_fusion.5
  107.9 5.9 %collective-permute-done = bf16[32,1152]{1,0:T(8,128)(2,1)S(1)} collective-permute-done((bf16[32,1152]{1,0:T(8,128)(2,1)S(1)}, bf16[32,1152]{1,0:T(8,128)(2,1)S(1)}, u32[]{:S(2)}, u32[]{:S(2)}) %collective-permute-start) | collective-permute-done | bytes 73760 | tf_op jit(solution)/shard_map/while/body/eval_jaxpr/ppermute | solution.py:13
  113.8 1.6 collective-permute-done.1
  115.4 0.3 fusion.40
  115.7 0.2 convolution_add_fusion.4
  115.9 0.1 collective-permute-start.1
  116.0 0.5 convolution_add_fusion.5
  116.5 5.9 %collective-permute-done = bf16[32,1152]{1,0:T(8,128)(2,1)S(1)} collective-permute-done((bf16[32,1152]{1,0:T(8,128)(2,1)S(1)}, bf16[32,1152]{1,0:T(8,128)(2,1)S(1)}, u32[]{:S(2)}, u32[]{:S(2)}) %collective-permute-start) | collective-permute-done | bytes 73760 | tf_op jit(solution)/shard_map/while/body/eval_jaxpr/ppermute | solution.py:13
  122.4 1.6 collective-permute-done.1
  124.0 0.3 fusion.40
  124.4 0.2 convolution_add_fusion.4
  124.6 0.1 collective-permute-start.1
  124.6 0.5 convolution_add_fusion.5
  125.2 5.9 %collective-permute-done = bf16[32,1152]{1,0:T(8,128)(2,1)S(1)} collective-permute-done((bf16[32,1152]{1,0:T(8,128)(2,1)S(1)}, bf16[32,1152]{1,0:T(8,128)(2,1)S(1)}, u32[]{:S(2)}, u32[]{:S(2)}) %collective-permute-start) | collective-permute-done | bytes 73760 | tf_op jit(solution)/shard_map/while/body/eval_jaxpr/ppermute | solution.py:13
  131.0 2.6 collective-permute-done.1
  133.7 0.3 fusion.40
  134.0 0.2 convolution_add_fusion.4
  134.2 0.1 collective-permute-start.1
  134.3 0.5 convolution_add_fusion.5
  134.9 6.5 %collective-permute-done = bf16[32,1152]{1,0:T(8,128)(2,1)S(1)} collective-permute-done((bf16[32,1152]{1,0:T(8,128)(2,1)S(1)}, bf16[32,1152]{1,0:T(8,128)(2,1)S(1)}, u32[]{:S(2)}, u32[]{:S(2)}) %collective-permute-start) | collective-permute-done | bytes 73760 | tf_op jit(solution)/shard_map/while/body/eval_jaxpr/ppermute | solution.py:13
  141.3 3.2 collective-permute-done.1
  144.5 0.3 fusion.40
  144.9 0.2 convolution_add_fusion.4
  145.2 0.5 convolution_add_fusion.5
  145.7 5.9 %collective-permute-done = bf16[32,1152]{1,0:T(8,128)(2,1)S(1)} collective-permute-done((bf16[32,1152]{1,0:T(8,128)(2,1)S(1)}, bf16[32,1152]{1,0:T(8,128)(2,1)S(1)}, u32[]{:S(2)}, u32[]{:S(2)}) %collective-permute-start) | collective-permute-done | bytes 73760 | tf_op jit(solution)/shard_map/while/body/eval_jaxpr/ppermute | solution.py:13
  151.6 1.6 collective-permute-done.1
  153.1 0.7 copy-done.3
  153.9 1.7 multiply_reduce_fusion
  155.6 4.3 %convolution_bitcast_fusion = f32[1536,1152]{0,1:T(8,128)} fusion(bf16[256,1536]{1,0:T(8,128)(2,1)S(1)} %copy-done, f32[256,1152]{1,0:T(8,128)S(1)} %get-tuple-element.180, f32[256,1152]{1,0:T(8,128)S(1)} %copy-done.2, f32[256]{0:T(256)S(1)} %multiply_reduce_fusion, f32[256]{0:T(256)S(1)} %add_rsqrt_fusion), kind=kOutput, calls=%fused_computation.13 | convolution fusion | flops 907444224 | bytes 10225664 | tf_op jit(solution)/shard_map/dot_general | solution.py:83
  159.8 8.1 %copy.8 = f32[1536,1152]{1,0:T(8,128)} copy(f32[1536,1152]{0,1:T(8,128)} %convolution_bitcast_fusion) | data formatting | bytes 14155776
  167.9 14.8 %all-reduce.2.cloned.1.call-done = f32[32,1152]{1,0:T(8,128)} async-done(((f32[32,1152]{1,0:T(8,128)}), f32[32,1152]{1,0:T(8,128)}) %all-reduce.2.cloned.1.call-update) | async-done | bytes 147472 | tf_op jit(solution)/shard_map/psum | solution.py:73
  182.7 1.1 fusion.14
  183.9 1.7 fusion.16
  185.5 124.4 %reduce-scatter.4.cloned.1.call-done = f32[48,1152]{1,0:T(8,128)} async-done(((f32[1536,1152]{1,0:T(8,128)}), f32[48,1152]{1,0:T(8,128)}) %reduce-scatter.4.cloned.1.call-update) | async-done | bytes 221200
  (43 shorter events, 0.3 us)
Async XLA Ops:
  7.2 66.8 %copy-start = (bf16[256,1536]{1,0:T(8,128)(2,1)S(1)}, bf16[256,1536]{1,0:T(8,128)(2,1)}, u32[]{:S(2)}) copy-start(bf16[256,1536]{1,0:T(8,128)(2,1)} %param.6) | copy-start | bytes 2359300
  7.2 66.7 %all-gather.2.cloned.1.call-start = ((), (), s32[]{:S(2)}) async-start(), calls=%async_computation.1 | async-start | bytes 3649536 | tf_op jit(solution)/shard_map/all_gather | solution.py:48
  7.9 174.8 %all-reduce.2.cloned.1.call-start = ((), (), s32[]{:S(2)}) async-start(), calls=%async_computation.2 | async-start | bytes 294912 | tf_op jit(solution)/shard_map/psum | solution.py:73
  77.2 1.0 copy-start.1
  77.2 1.2 copy-start.5
  78.4 7.2 %collective-permute-start = (bf16[32,1152]{1,0:T(8,128)(2,1)S(1)}, bf16[32,1152]{1,0:T(8,128)(2,1)S(1)}, u32[]{:S(2)}, u32[]{:S(2)}) collective-permute-start(bf16[32,1152]{1,0:T(8,128)(2,1)S(1)} %copy.15), channel_id=1, source_target_pairs={{0,1},{1,2},{2,3},{3,4},{4,5},{5,6},{6,7},{7,0},{8,9},{9,10},{10,1... | collective-permute-start | bytes 221192 | tf_op jit(solution)/shard_map/while/body/eval_jaxpr/ppermute | solution.py:13
  80.4 8.5 %collective-permute-start.1 = (f32[32,1152]{1,0:T(8,128)S(1)}, f32[32,1152]{1,0:T(8,128)S(1)}, u32[]{:S(2)}, u32[]{:S(2)}) collective-permute-start(f32[32,1152]{1,0:T(8,128)S(1)} %convolution_add_fusion.4), channel_id=1, source_target_pairs={{0,1},{1,2},{2,3},{3,4},{4,5},{5,6},{6,7},{7,0},{8,9},{9,10},{10,1... | collective-permute-start | bytes 442376 | tf_op jit(solution)/shard_map/while/body/eval_jaxpr/ppermute | solution.py:13
  88.9 7.6 %collective-permute-start = (bf16[32,1152]{1,0:T(8,128)(2,1)S(1)}, bf16[32,1152]{1,0:T(8,128)(2,1)S(1)}, u32[]{:S(2)}, u32[]{:S(2)}) collective-permute-start(bf16[32,1152]{1,0:T(8,128)(2,1)S(1)} %copy.15), channel_id=1, source_target_pairs={{0,1},{1,2},{2,3},{3,4},{4,5},{5,6},{6,7},{7,0},{8,9},{9,10},{10,1... | collective-permute-start | bytes 221192 | tf_op jit(solution)/shard_map/while/body/eval_jaxpr/ppermute | solution.py:13
  89.5 8.6 %collective-permute-start.1 = (f32[32,1152]{1,0:T(8,128)S(1)}, f32[32,1152]{1,0:T(8,128)S(1)}, u32[]{:S(2)}, u32[]{:S(2)}) collective-permute-start(f32[32,1152]{1,0:T(8,128)S(1)} %convolution_add_fusion.4), channel_id=1, source_target_pairs={{0,1},{1,2},{2,3},{3,4},{4,5},{5,6},{6,7},{7,0},{8,9},{9,10},{10,1... | collective-permute-start | bytes 442376 | tf_op jit(solution)/shard_map/while/body/eval_jaxpr/ppermute | solution.py:13
  98.1 7.0 %collective-permute-start = (bf16[32,1152]{1,0:T(8,128)(2,1)S(1)}, bf16[32,1152]{1,0:T(8,128)(2,1)S(1)}, u32[]{:S(2)}, u32[]{:S(2)}) collective-permute-start(bf16[32,1152]{1,0:T(8,128)(2,1)S(1)} %copy.15), channel_id=1, source_target_pairs={{0,1},{1,2},{2,3},{3,4},{4,5},{5,6},{6,7},{7,0},{8,9},{9,10},{10,1... | collective-permute-start | bytes 221192 | tf_op jit(solution)/shard_map/while/body/eval_jaxpr/ppermute | solution.py:13
  98.7 8.1 %collective-permute-start.1 = (f32[32,1152]{1,0:T(8,128)S(1)}, f32[32,1152]{1,0:T(8,128)S(1)}, u32[]{:S(2)}, u32[]{:S(2)}) collective-permute-start(f32[32,1152]{1,0:T(8,128)S(1)} %convolution_add_fusion.4), channel_id=1, source_target_pairs={{0,1},{1,2},{2,3},{3,4},{4,5},{5,6},{6,7},{7,0},{8,9},{9,10},{10,1... | collective-permute-start | bytes 442376 | tf_op jit(solution)/shard_map/while/body/eval_jaxpr/ppermute | solution.py:13
  106.7 7.0 %collective-permute-start = (bf16[32,1152]{1,0:T(8,128)(2,1)S(1)}, bf16[32,1152]{1,0:T(8,128)(2,1)S(1)}, u32[]{:S(2)}, u32[]{:S(2)}) collective-permute-start(bf16[32,1152]{1,0:T(8,128)(2,1)S(1)} %copy.15), channel_id=1, source_target_pairs={{0,1},{1,2},{2,3},{3,4},{4,5},{5,6},{6,7},{7,0},{8,9},{9,10},{10,1... | collective-permute-start | bytes 221192 | tf_op jit(solution)/shard_map/while/body/eval_jaxpr/ppermute | solution.py:13
  107.3 8.1 %collective-permute-start.1 = (f32[32,1152]{1,0:T(8,128)S(1)}, f32[32,1152]{1,0:T(8,128)S(1)}, u32[]{:S(2)}, u32[]{:S(2)}) collective-permute-start(f32[32,1152]{1,0:T(8,128)S(1)} %convolution_add_fusion.4), channel_id=1, source_target_pairs={{0,1},{1,2},{2,3},{3,4},{4,5},{5,6},{6,7},{7,0},{8,9},{9,10},{10,1... | collective-permute-start | bytes 442376 | tf_op jit(solution)/shard_map/while/body/eval_jaxpr/ppermute | solution.py:13
  115.4 7.0 %collective-permute-start = (bf16[32,1152]{1,0:T(8,128)(2,1)S(1)}, bf16[32,1152]{1,0:T(8,128)(2,1)S(1)}, u32[]{:S(2)}, u32[]{:S(2)}) collective-permute-start(bf16[32,1152]{1,0:T(8,128)(2,1)S(1)} %copy.15), channel_id=1, source_target_pairs={{0,1},{1,2},{2,3},{3,4},{4,5},{5,6},{6,7},{7,0},{8,9},{9,10},{10,1... | collective-permute-start | bytes 221192 | tf_op jit(solution)/shard_map/while/body/eval_jaxpr/ppermute | solution.py:13
  115.9 8.1 %collective-permute-start.1 = (f32[32,1152]{1,0:T(8,128)S(1)}, f32[32,1152]{1,0:T(8,128)S(1)}, u32[]{:S(2)}, u32[]{:S(2)}) collective-permute-start(f32[32,1152]{1,0:T(8,128)S(1)} %convolution_add_fusion.4), channel_id=1, source_target_pairs={{0,1},{1,2},{2,3},{3,4},{4,5},{5,6},{6,7},{7,0},{8,9},{9,10},{10,1... | collective-permute-start | bytes 442376 | tf_op jit(solution)/shard_map/while/body/eval_jaxpr/ppermute | solution.py:13
  124.0 7.0 %collective-permute-start = (bf16[32,1152]{1,0:T(8,128)(2,1)S(1)}, bf16[32,1152]{1,0:T(8,128)(2,1)S(1)}, u32[]{:S(2)}, u32[]{:S(2)}) collective-permute-start(bf16[32,1152]{1,0:T(8,128)(2,1)S(1)} %copy.15), channel_id=1, source_target_pairs={{0,1},{1,2},{2,3},{3,4},{4,5},{5,6},{6,7},{7,0},{8,9},{9,10},{10,1... | collective-permute-start | bytes 221192 | tf_op jit(solution)/shard_map/while/body/eval_jaxpr/ppermute | solution.py:13
  124.6 9.1 %collective-permute-start.1 = (f32[32,1152]{1,0:T(8,128)S(1)}, f32[32,1152]{1,0:T(8,128)S(1)}, u32[]{:S(2)}, u32[]{:S(2)}) collective-permute-start(f32[32,1152]{1,0:T(8,128)S(1)} %convolution_add_fusion.4), channel_id=1, source_target_pairs={{0,1},{1,2},{2,3},{3,4},{4,5},{5,6},{6,7},{7,0},{8,9},{9,10},{10,1... | collective-permute-start | bytes 442376 | tf_op jit(solution)/shard_map/while/body/eval_jaxpr/ppermute | solution.py:13
  133.7 7.7 %collective-permute-start = (bf16[32,1152]{1,0:T(8,128)(2,1)S(1)}, bf16[32,1152]{1,0:T(8,128)(2,1)S(1)}, u32[]{:S(2)}, u32[]{:S(2)}) collective-permute-start(bf16[32,1152]{1,0:T(8,128)(2,1)S(1)} %copy.15), channel_id=1, source_target_pairs={{0,1},{1,2},{2,3},{3,4},{4,5},{5,6},{6,7},{7,0},{8,9},{9,10},{10,1... | collective-permute-start | bytes 221192 | tf_op jit(solution)/shard_map/while/body/eval_jaxpr/ppermute | solution.py:13
  134.2 10.3 %collective-permute-start.1 = (f32[32,1152]{1,0:T(8,128)S(1)}, f32[32,1152]{1,0:T(8,128)S(1)}, u32[]{:S(2)}, u32[]{:S(2)}) collective-permute-start(f32[32,1152]{1,0:T(8,128)S(1)} %convolution_add_fusion.4), channel_id=1, source_target_pairs={{0,1},{1,2},{2,3},{3,4},{4,5},{5,6},{6,7},{7,0},{8,9},{9,10},{10,1... | collective-permute-start | bytes 442376 | tf_op jit(solution)/shard_map/while/body/eval_jaxpr/ppermute | solution.py:13
  144.5 7.0 %collective-permute-start = (bf16[32,1152]{1,0:T(8,128)(2,1)S(1)}, bf16[32,1152]{1,0:T(8,128)(2,1)S(1)}, u32[]{:S(2)}, u32[]{:S(2)}) collective-permute-start(bf16[32,1152]{1,0:T(8,128)(2,1)S(1)} %copy.15), channel_id=1, source_target_pairs={{0,1},{1,2},{2,3},{3,4},{4,5},{5,6},{6,7},{7,0},{8,9},{9,10},{10,1... | collective-permute-start | bytes 221192 | tf_op jit(solution)/shard_map/while/body/eval_jaxpr/ppermute | solution.py:13
  145.1 8.0 %collective-permute-start.1 = (f32[32,1152]{1,0:T(8,128)S(1)}, f32[32,1152]{1,0:T(8,128)S(1)}, u32[]{:S(2)}, u32[]{:S(2)}) collective-permute-start(f32[32,1152]{1,0:T(8,128)S(1)} %convolution_add_fusion.4), channel_id=1, source_target_pairs={{0,1},{1,2},{2,3},{3,4},{4,5},{5,6},{6,7},{7,0},{8,9},{9,10},{10,1... | collective-permute-start | bytes 442376 | tf_op jit(solution)/shard_map/while/body/eval_jaxpr/ppermute | solution.py:13
  153.1 0.7 copy-start.3
  153.8 156.1 %reduce-scatter.4.cloned.1.call-start = ((), (), s32[]{:S(2)}) async-start(), calls=%async_computation.3 | async-start | bytes 7299072
  153.9 1.7 copy-start.2
  167.9 14.9 %copy-start.4 = (bf16[32,1152]{1,0:T(8,128)(2,1)S(1)}, bf16[32,1152]{1,0:T(8,128)(2,1)}, u32[]{:S(2)}) copy-start(bf16[32,1152]{1,0:T(8,128)(2,1)} %param.9) | copy-start | bytes 221188
Sparse Core Ops, SparseCore 0:
  11.0 62.8 all-gather.1
  153.9 28.7 all-reduce.1
  190.0 119.9 reduce-scatter.3
where the time goes:
time: 317 us; the launch traced here: 316 us
  waiting for transfers between devices  266 us (84%)
  matrix products  15.9 us (5%)
  between operations  13.8 us (4%)
  local copies, waits for them, and re-layouts  9.8 us (3%)
  other arithmetic  6.59 us (2%)
  starting transfers between devices  3.6 us (1%)
    unnamed x4, waiting for transfers between devices  125 us
    all_gather x1, waiting for transfers between devices, shards(): lax.all_gather(img_weight, ('grp', 'blk'), axis=0, tiled=True)  64 us
    ppermute x16, waiting for transfers between devices, from_behind(): lax.ppermute(array, axis, [(i, (i + by) % count) for i in range(count)])  62.3 us
    psum x1, waiting for transfers between devices, shards(): grad_unit = lax.psum(grad_home, 'grp')  14.8 us
    unnamed x13, local copies, waits for them, and re-layouts  9.74 us
  transfers between devices with their start and end apart: 19, of which 19 were waited for; matrix products, arithmetic and copies ran while one was open for 9% of the time, Pallas kernels for 0%

commit v1 on v0

v1 whole, which is shorter than its diff:
```python
import jax
import jax.numpy as jnp
from jax import lax
from jax.sharding import PartitionSpec as P

epsilon = 1e-06
logit_scale = 10.0
logit_bias = -5.0
axes = ("grp", "blk")


def unit_rows(raw_rows):
    inverse = lax.rsqrt(jnp.sum(raw_rows * raw_rows, axis=1, keepdims=True) + epsilon)
    return (raw_rows * inverse, inverse)


def make_shards(grp_size, blk_size):
    devices = grp_size * blk_size
    core_mask, y_mask, x_mask = blk_size, 2 * blk_size, 1
    depth = blk_size // 2
    y_size = grp_size // 2
    assert grp_size == 4 and blk_size & (blk_size - 1) == 0 and blk_size >= 2

    def swap(array, mask):
        return lax.ppermute(array, axes, [(i, i ^ mask) for i in range(devices)])

    def shards(pooled, img_weight, img_label, text_raw):
        images, width = pooled.shape
        rows, embed = img_weight.shape
        texts = text_raw.shape[0]
        half = texts // 2
        grp, blk = lax.axis_index("grp"), lax.axis_index("blk")
        core = grp % 2
        place = grp * blk_size + blk

        text_float, text_inverse = unit_rows(text_raw.astype(jnp.float32))
        text_unit = text_float.astype(jnp.bfloat16)
        own_half = lax.dynamic_slice_in_dim(text_unit, core * half, half, 0)

        own = jnp.concatenate([img_weight, own_half], axis=0)
        by_z = [own] + [None] * (depth - 1)
        for kz in range(depth - 1, 0, -1):
            by_z[kz] = swap(own, 2 * kz)
        quads, text_pairs = [], []
        for kz in range(depth):
            block = by_z[kz][:rows]
            if kz % 2 == 0:
                other = swap(by_z[kz], x_mask)
                text_other = other[rows:]
                pair = jnp.concatenate([block, other[:rows]], axis=0)
                far = swap(pair, y_mask)
                quad = jnp.concatenate([pair, far], axis=0)
            else:
                other = swap(block, y_mask)
                pair = jnp.concatenate([block, other, by_z[kz][rows:]], axis=0)
                far = swap(pair, x_mask)
                text_other = far[2 * rows :]
                quad = jnp.concatenate([block, far[:rows], other, far[rows : 2 * rows]], axis=0)
            quads.append(quad)
            text_pairs.append(jnp.concatenate([by_z[kz][rows:], text_other], axis=0))
        gathered = [jnp.concatenate([q, swap(q, core_mask)], axis=0) for q in quads]
        text_mine = jnp.concatenate(text_pairs, axis=0)
        text_all = jnp.concatenate([text_mine, swap(text_mine, core_mask)], axis=0)

        order = jnp.asarray(
            [
                ky * y_mask + kc * core_mask + kz * 2 + kx
                for kz in range(depth)
                for kc in range(2)
                for ky in range(y_size)
                for kx in range(2)
            ],
            dtype=jnp.int32,
        )
        columns = jnp.take(pooled.T.reshape(devices, rows, images), place ^ order, axis=0)
        quad_rows = 2 * y_size * rows
        columns = columns.reshape(depth, 2, quad_rows, images)
        mine = columns[:, 0].reshape(depth * quad_rows, images)
        theirs = swap(columns[:, 1].reshape(depth * quad_rows, images), core_mask)

        projected = sum(
            lax.dot_general(
                columns[kz].reshape(2 * quad_rows, images),
                gathered[kz],
                (((0,), (0,)), ((), ())),
                preferred_element_type=jnp.float32,
            )
            for kz in range(depth)
        )
        embed_float, inverse = unit_rows(projected)
        embedded = embed_float.astype(jnp.bfloat16)

        text_place = blk ^ jnp.arange(blk_size, dtype=jnp.int32)
        halves = core ^ jnp.arange(2, dtype=jnp.int32)
        text_ids = (
            text_place[None, :, None] * texts
            + halves[:, None, None] * half
            + jnp.arange(half, dtype=jnp.int32)[None, None, :]
        ).reshape(-1)
        logits = (
            logit_scale
            * lax.dot_general(
                embedded, text_all, (((1,), (1,)), ((), ())), preferred_element_type=jnp.float32
            )
            + logit_bias
        )
        polarity = jnp.where(img_label[:, None] == text_ids[None, :], 1.0, -1.0).astype(jnp.float32)
        pair_slope = (
            -polarity * jax.nn.sigmoid(-polarity * logits) * (logit_scale / texts)
        ).astype(jnp.bfloat16)
        grad_embed = jnp.dot(pair_slope, text_all, preferred_element_type=jnp.float32)
        grad_unit = lax.dot_general(
            pair_slope, embedded, (((0,), (0,)), ((), ())), preferred_element_type=jnp.float32
        )
        grad_proj = (
            inverse
            * (grad_embed - embed_float * jnp.sum(grad_embed * embed_float, axis=1, keepdims=True))
        ).astype(jnp.bfloat16)

        class_rows = blk_size * half
        grad_unit = grad_unit[:class_rows] + swap(
            grad_unit[class_rows:].astype(jnp.bfloat16), core_mask
        ).astype(jnp.float32)
        grad_unit = grad_unit.reshape(depth, 2, half, embed)
        grad_unit = grad_unit[:, 0] + swap(
            grad_unit[:, 1].astype(jnp.bfloat16), x_mask
        ).astype(jnp.float32)
        grad_unit = grad_unit + swap(grad_unit.astype(jnp.bfloat16), y_mask).astype(jnp.float32)

        grad_both = jnp.concatenate([grad_proj, swap(grad_proj, core_mask)], axis=0)
        both = jnp.concatenate([mine, theirs], axis=1).reshape(
            depth, quad_rows, 2 * images
        )
        total = None
        for kz in list(range(2, depth)) + list(range(min(2, depth))):
            part = jnp.dot(both[kz], grad_both, preferred_element_type=jnp.float32)
            part = part.reshape(y_size, 2, rows, embed)
            if kz % 2 == 0:
                part = part[0] + swap(part[1].astype(jnp.bfloat16), y_mask).astype(jnp.float32)
                part = part[0] + swap(part[1].astype(jnp.bfloat16), x_mask).astype(jnp.float32)
            else:
                part = part[:, 0] + swap(part[:, 1].astype(jnp.bfloat16), x_mask).astype(jnp.float32)
                part = part[0] + swap(part[1].astype(jnp.bfloat16), y_mask).astype(jnp.float32)
            part = jnp.concatenate([part, grad_unit[kz]], axis=0)
            if kz:
                part = swap(part.astype(jnp.bfloat16), 2 * kz).astype(jnp.float32)
            total = part if total is None else total + part
        grad_weight = total[:rows]
        half_mine = total[rows:]
        half_theirs = swap(half_mine, core_mask)
        grad_unit = jnp.where(
            core == 0,
            jnp.concatenate([half_mine, half_theirs], axis=0),
            jnp.concatenate([half_theirs, half_mine], axis=0),
        )
        grad_text = text_inverse * (
            grad_unit - text_float * jnp.sum(grad_unit * text_float, axis=1, keepdims=True)
        )
        return (grad_weight, grad_text)

    return shards


def solution(mesh):
    return jax.shard_map(
        make_shards(mesh.shape["grp"], mesh.shape["blk"]),
        mesh=mesh,
        in_specs=(
            P(("grp", "blk"), None),
            P(("grp", "blk"), None),
            P(("grp", "blk")),
            P("blk", None),
        ),
        out_specs=(P(("grp", "blk"), None), P("blk", None)),
        check_vma=False,
    )
```

time: 317 us -> 92.2 us (0.29)
  waiting for transfers between devices: 266 us -> 41 us
  starting transfers between devices: 3.6 us -> 33.8 us
  between operations: 13.8 us -> 1.34 us
  matrix products: 15.9 us -> 5.27 us
  local copies, waits for them, and re-layouts: 9.8 us -> 4.97 us
    unnamed x4 -> x0, waiting for transfers between devices: 125 us -> none
    all_gather x1 -> x0, waiting for transfers between devices: 64 us -> none  [shards(): lax.all_gather(img_weight, ('grp', 'blk'), axis=0, tiled=True)]
    ppermute x16 -> x33, starting transfers between devices: 3.48 us -> 33.8 us  [swap(): return lax.ppermute(array, axes, [(i, i ^ mask) for i in range(devices)])]
    ppermute x16 -> x33, waiting for transfers between devices: 62.3 us -> 41 us  [swap(): return lax.ppermute(array, axes, [(i, i ^ mask) for i in range(devices)])]
    psum x1 -> x0, waiting for transfers between devices: 14.8 us -> none  [shards(): grad_unit = lax.psum(grad_home, 'grp')]
    dot_general x26 -> x11, matrix products: 15.9 us -> 5.27 us  [the longest x4 2.28 us: shards(): lax.dot_general(columns[kz].reshape(2 * quad_rows, images), gathered[kz],...]
    unnamed x13 -> x29, local copies, waits for them, and re-layouts: 9.74 us -> 2.72 us
  transfers between devices with their start and end apart: 19 -> 33, of which waited for: 19 -> 15; matrix products, arithmetic and copies ran while one was open for 9% -> 12% of each run, Pallas kernels for 0% -> 0%
where the time goes in v1:
time: 92.2 us; the launch traced here: 91.9 us
  waiting for transfers between devices  41 us (44%)
  starting transfers between devices  33.8 us (37%)
  other arithmetic  5.5 us (6%)
  matrix products  5.27 us (6%)
  local copies, waits for them, and re-layouts  4.97 us (5%)
  between operations  1.34 us (1%)
    ppermute x33, waiting for transfers between devices, swap(): return lax.ppermute(array, axes, [(i, i ^ mask) for i in range(devices)])  41 us
    ppermute x33, starting transfers between devices, swap(): return lax.ppermute(array, axes, [(i, i ^ mask) for i in range(devices)])  33.8 us
    unnamed x29, local copies, waits for them, and re-layouts  2.72 us
    dot_general x4, matrix products, shards(): lax.dot_general(columns[kz].reshape(2 * quad_rows, images), gathered[kz],...  2.28 us
  transfers between devices with their start and end apart: 33, of which 15 were waited for; matrix products, arithmetic and copies ran while one was open for 12% of the time, Pallas kernels for 0%

profile of v1, /device:TPU:0, one launch (start us, length us, event | category | flops | bytes accessed | tf_op | source)
XLA Modules:
  0.0 91.9 jit_solution(10314523183518799352)
XLA Ops:
  0.7 1.0 %fusion.52 = f32[32]{0:T(128)S(1)} fusion(bf16[32,1152]{1,0:T(8,128)(2,1)} %param.8), kind=kLoop, calls=%fused_computation.99 | loop fusion | flops 110560 | bytes 73856 | tf_op jit(solution)/shard_map/reduce_sum | solution.py:13
  1.7 1.0 %convert_multiply_fusion = bf16[32,1152]{1,0:T(8,128)(2,1)S(1)} fusion(bf16[32,1152]{1,0:T(8,128)(2,1)} %param.8, f32[32]{0:T(128)S(1)} %add_rsqrt_fusion.1), kind=kLoop, calls=%fused_computation.97 | loop fusion | flops 110592 | bytes 147584 | tf_op jit(solution)/shard_map/mul | solution.py:14
  2.7 0.6 constant_dynamic-update-slice_fusion.17
  3.3 0.9 pad_maximum_fusion.10
  4.2 3.0 %collective-permute-start.1 = (bf16[64,1152]{1,0:T(8,128)(2,1)S(1)}, bf16[64,1152]{1,0:T(8,128)(2,1)S(1)}, u32[]{:S(2)}, u32[]{:S(2)}) collective-permute-start(bf16[64,1152]{1,0:T(8,128)(2,1)S(1)} %pad_maximum_fusion.10), channel_id=1, source_target_pairs={{0,1},{1,0},{2,3},{3,2},{4,5},{5,4},{6,7},{7,6},{8,9},{9,8},{10,11... | collective-permute-start | bytes 442376 | tf_op jit(solution)/shard_map/ppermute | solution.py:25
  7.2 1.6 %collective-permute-start.4 = (bf16[64,1152]{1,0:T(8,128)(2,1)S(1)}, bf16[64,1152]{1,0:T(8,128)(2,1)S(1)}, u32[]{:S(2)}, u32[]{:S(2)}) collective-permute-start(bf16[64,1152]{1,0:T(8,128)(2,1)S(1)} %pad_maximum_fusion.10), channel_id=1, source_target_pairs={{0,2},{1,3},{2,0},{3,1},{4,6},{5,7},{6,4},{7,5},{8,10},{9,11},{10,... | collective-permute-start | bytes 442376 | tf_op jit(solution)/shard_map/ppermute | solution.py:25
  8.8 2.6 %collective-permute-start.8 = (bf16[64,1152]{1,0:T(8,128)(2,1)S(1)}, bf16[64,1152]{1,0:T(8,128)(2,1)S(1)}, u32[]{:S(2)}, u32[]{:S(2)}) collective-permute-start(bf16[64,1152]{1,0:T(8,128)(2,1)S(1)} %pad_maximum_fusion.10), channel_id=1, source_target_pairs={{0,4},{1,5},{2,6},{3,7},{4,0},{5,1},{6,2},{7,3},{8,12},{9,13},{10,... | collective-permute-start | bytes 442376 | tf_op jit(solution)/shard_map/ppermute | solution.py:25
  11.4 0.2 collective-permute-start.12
  11.6 1.4 %copy.22 = bf16[256,1536]{0,1:T(8,128)(2,1)S(1)} copy(bf16[256,1536]{1,0:T(8,128)(2,1)} %param.5) | data formatting | bytes 1572864 | tf_op args[0]
  13.3 0.6 gather_fusion
  13.9 0.3 broadcast_select_fusion.1
  14.9 1.6 %collective-permute-start.5 = (bf16[48,1152]{1,0:T(8,128)(2,1)S(1)}, bf16[48,1152]{1,0:T(8,128)(2,1)S(1)}, u32[]{:S(2)}, u32[]{:S(2)}) collective-permute-start(bf16[48,1152]{1,0:T(8,128)(2,1)S(1)} %get-tuple-element.30), channel_id=1, source_target_pairs={{0,16},{1,17},{2,18},{3,19},{4,20},{5,21},{6,22},{7,23},{8,24},{9,... | collective-permute-start | bytes 331784 | tf_op jit(solution)/shard_map/ppermute | solution.py:25
  16.5 4.5 %collective-permute-done.12 = bf16[64,1152]{1,0:T(8,128)(2,1)S(1)} collective-permute-done((bf16[64,1152]{1,0:T(8,128)(2,1)S(1)}, bf16[64,1152]{1,0:T(8,128)(2,1)S(1)}, u32[]{:S(2)}, u32[]{:S(2)}) %collective-permute-start.12) | collective-permute-done | bytes 147488 | tf_op jit(solution)/shard_map/ppermute | solution.py:25
  21.0 1.6 %collective-permute-start.13 = (bf16[48,1152]{1,0:T(8,128)(2,1)S(1)}, bf16[48,1152]{1,0:T(8,128)(2,1)S(1)}, u32[]{:S(2)}, u32[]{:S(2)}) collective-permute-start(bf16[48,1152]{1,0:T(8,128)(2,1)S(1)} %get-tuple-element.32), channel_id=1, source_target_pairs={{0,16},{1,17},{2,18},{3,19},{4,20},{5,21},{6,22},{7,23},{8,24},{9,... | collective-permute-start | bytes 331784 | tf_op jit(solution)/shard_map/ppermute | solution.py:25
  22.6 0.6 collective-permute-start.2
  23.2 0.5 collective-permute-start.9
  23.8 1.6 %collective-permute-start.6 = (bf16[112,1152]{1,0:T(8,128)(2,1)S(1)}, bf16[112,1152]{1,0:T(8,128)(2,1)S(1)}, u32[]{:S(2)}, u32[]{:S(2)}) collective-permute-start(bf16[112,1152]{1,0:T(8,128)(2,1)S(1)} %pad_maximum_fusion.5), channel_id=1, source_target_pairs={{0,1},{1,0},{2,3},{3,2},{4,5},{5,4},{6,7},{7,6},{8,9},{9,8},{10,11... | collective-permute-start | bytes 774152 | tf_op jit(solution)/shard_map/ppermute | solution.py:25
  25.4 4.4 %collective-permute-done.9 = bf16[64,1152]{1,0:T(8,128)(2,1)S(1)} collective-permute-done((bf16[64,1152]{1,0:T(8,128)(2,1)S(1)}, bf16[64,1152]{1,0:T(8,128)(2,1)S(1)}, u32[]{:S(2)}, u32[]{:S(2)}) %collective-permute-start.9) | collective-permute-done | bytes 147488 | tf_op jit(solution)/shard_map/ppermute | solution.py:25
  29.8 1.6 %collective-permute-start.10 = (bf16[96,1152]{1,0:T(8,128)(2,1)S(1)}, bf16[96,1152]{1,0:T(8,128)(2,1)S(1)}, u32[]{:S(2)}, u32[]{:S(2)}) collective-permute-start(bf16[96,1152]{1,0:T(8,128)(2,1)S(1)} %pad_maximum_fusion.8), channel_id=1, source_target_pairs={{0,16},{1,17},{2,18},{3,19},{4,20},{5,21},{6,22},{7,23},{8,24},{9,... | collective-permute-start | bytes 663560 | tf_op jit(solution)/shard_map/ppermute | solution.py:25
  31.5 1.0 %collective-permute-done.6 = bf16[112,1152]{1,0:T(8,128)(2,1)S(1)} collective-permute-done((bf16[112,1152]{1,0:T(8,128)(2,1)S(1)}, bf16[112,1152]{1,0:T(8,128)(2,1)S(1)}, u32[]{:S(2)}, u32[]{:S(2)}) %collective-permute-start.6) | collective-permute-done | bytes 258080 | tf_op jit(solution)/shard_map/ppermute | solution.py:25
  32.6 0.6 collective-permute-start.14
  33.2 2.6 %collective-permute-done.10 = bf16[96,1152]{1,0:T(8,128)(2,1)S(1)} collective-permute-done((bf16[96,1152]{1,0:T(8,128)(2,1)S(1)}, bf16[96,1152]{1,0:T(8,128)(2,1)S(1)}, u32[]{:S(2)}, u32[]{:S(2)}) %collective-permute-start.10) | collective-permute-done | bytes 221216 | tf_op jit(solution)/shard_map/ppermute | solution.py:25
  36.0 0.6 collective-permute-start.7
  36.6 3.7 %collective-permute-done.14 = bf16[112,1152]{1,0:T(8,128)(2,1)S(1)} collective-permute-done((bf16[112,1152]{1,0:T(8,128)(2,1)S(1)}, bf16[112,1152]{1,0:T(8,128)(2,1)S(1)}, u32[]{:S(2)}, u32[]{:S(2)}) %collective-permute-start.14) | collective-permute-done | bytes 258080 | tf_op jit(solution)/shard_map/ppermute | solution.py:25
  40.5 0.6 collective-permute-start.15
  41.1 0.5 fusion.68
  41.6 0.5 fusion.22
  42.2 0.4 collective-permute-done.15
  42.6 0.5 fusion.69
  43.2 0.8 multiply_reduce_fusion.1
  43.9 0.4 fusion.14
  44.4 0.4 fusion.62
  44.9 0.4 collective-permute-start.20
  45.2 0.4 multiply_reduce_fusion
  45.6 0.9 collective-permute-done.20
  46.6 0.6 collective-permute-start.21
  47.2 0.2 multiply_convert_fusion
  47.6 5.1 %collective-permute-done.21 = bf16[4,16,1152]{2,1,0:T(8,128)(2,1)S(1)} collective-permute-done((bf16[4,16,1152]{2,1,0:T(8,128)(2,1)S(1)}, bf16[4,16,1152]{2,1,0:T(8,128)(2,1)S(1)}, u32[]{:S(2)}, u32[]{:S(2)}) %collective-permute-start.21) | collective-permute-done | bytes 147488 | tf_op jit(solution)/shard_map/ppermute | solution.py:25
  52.7 0.6 collective-permute-start.22
  53.3 0.4 fusion.44
  53.8 0.4 fusion.47
  54.2 0.5 copy-done.1
  54.7 1.5 %collective-permute-start.27 = (bf16[2,48,1152]{2,1,0:T(8,128)(2,1)S(1)}, bf16[2,48,1152]{2,1,0:T(8,128)(2,1)S(1)}, u32[]{:S(2)}, u32[]{:S(2)}) collective-permute-start(bf16[2,48,1152]{2,1,0:T(8,128)(2,1)S(1)} %bitcast.115), channel_id=1, source_target_pairs={{0,16},{1,17},{2,18},{3,19},{4,20},{5,21},{6,22},{7,23},{8,24},{9,... | collective-permute-start | bytes 663560 | tf_op jit(solution)/shard_map/ppermute | solution.py:25
  56.3 0.4 fusion.4
  56.8 0.6 collective-permute-start.29
  57.4 0.4 fusion.2
  57.8 1.6 %collective-permute-start.24 = (bf16[2,48,1152]{2,1,0:T(8,128)(2,1)S(1)}, bf16[2,48,1152]{2,1,0:T(8,128)(2,1)S(1)}, u32[]{:S(2)}, u32[]{:S(2)}) collective-permute-start(bf16[2,48,1152]{2,1,0:T(8,128)(2,1)S(1)} %fusion.34), channel_id=1, source_target_pairs={{0,1},{1,0},{2,3},{3,2},{4,5},{5,4},{6,7},{7,6},{8,9},{9,8},{10,11... | collective-permute-start | bytes 663560 | tf_op jit(solution)/shard_map/ppermute | solution.py:25
  59.4 0.6 collective-permute-start.18
  60.1 4.1 %collective-permute-done.27 = bf16[2,48,1152]{2,1,0:T(8,128)(2,1)S(1)} collective-permute-done((bf16[2,48,1152]{2,1,0:T(8,128)(2,1)S(1)}, bf16[2,48,1152]{2,1,0:T(8,128)(2,1)S(1)}, u32[]{:S(2)}, u32[]{:S(2)}) %collective-permute-start.27) | collective-permute-done | bytes 221216 | tf_op jit(solution)/shard_map/ppermute | solution.py:25
  64.3 0.6 collective-permute-start.28
  64.8 0.4 collective-permute-done.29
  65.3 0.6 collective-permute-start.30
  65.9 3.1 %collective-permute-done.24 = bf16[2,48,1152]{2,1,0:T(8,128)(2,1)S(1)} collective-permute-done((bf16[2,48,1152]{2,1,0:T(8,128)(2,1)S(1)}, bf16[2,48,1152]{2,1,0:T(8,128)(2,1)S(1)}, u32[]{:S(2)}, u32[]{:S(2)}) %collective-permute-start.24) | collective-permute-done | bytes 221216 | tf_op jit(solution)/shard_map/ppermute | solution.py:25
  69.1 0.7 collective-permute-start.25
  69.9 0.6 collective-permute-start.19
  70.5 0.6 collective-permute-done.30
  71.1 3.5 %collective-permute-start.31 = (bf16[64,1152]{1,0:T(8,128)(2,1)S(1)}, bf16[64,1152]{1,0:T(8,128)(2,1)S(1)}, u32[]{:S(2)}, u32[]{:S(2)}) collective-permute-start(bf16[64,1152]{1,0:T(8,128)(2,1)S(1)} %pad_maximum_fusion.13), channel_id=1, source_target_pairs={{0,2},{1,3},{2,0},{3,1},{4,6},{5,7},{6,4},{7,5},{8,10},{9,11},{10,... | collective-permute-start | bytes 442376 | tf_op jit(solution)/shard_map/ppermute | solution.py:25
  74.7 3.1 %collective-permute-start.26 = (bf16[64,1152]{1,0:T(8,128)(2,1)S(1)}, bf16[64,1152]{1,0:T(8,128)(2,1)S(1)}, u32[]{:S(2)}, u32[]{:S(2)}) collective-permute-start(bf16[64,1152]{1,0:T(8,128)(2,1)S(1)} %pad_maximum_fusion.12), channel_id=1, source_target_pairs={{0,6},{1,7},{2,4},{3,5},{4,2},{5,3},{6,0},{7,1},{8,14},{9,15},{10,... | collective-permute-start | bytes 442376 | tf_op jit(solution)/shard_map/ppermute | solution.py:25
  77.8 2.0 %collective-permute-start.23 = (bf16[64,1152]{1,0:T(8,128)(2,1)S(1)}, bf16[64,1152]{1,0:T(8,128)(2,1)S(1)}, u32[]{:S(2)}, u32[]{:S(2)}) collective-permute-start(bf16[64,1152]{1,0:T(8,128)(2,1)S(1)} %pad_maximum_fusion.11), channel_id=1, source_target_pairs={{0,4},{1,5},{2,6},{3,7},{4,0},{5,1},{6,2},{7,3},{8,12},{9,13},{10,... | collective-permute-start | bytes 442376 | tf_op jit(solution)/shard_map/ppermute | solution.py:25
  79.9 4.0 %collective-permute-done.26 = bf16[64,1152]{1,0:T(8,128)(2,1)S(1)} collective-permute-done((bf16[64,1152]{1,0:T(8,128)(2,1)S(1)}, bf16[64,1152]{1,0:T(8,128)(2,1)S(1)}, u32[]{:S(2)}, u32[]{:S(2)}) %collective-permute-start.26) | collective-permute-done | bytes 147488 | tf_op jit(solution)/shard_map/ppermute | solution.py:25
  83.9 5.6 %collective-permute-done.23 = bf16[64,1152]{1,0:T(8,128)(2,1)S(1)} collective-permute-done((bf16[64,1152]{1,0:T(8,128)(2,1)S(1)}, bf16[64,1152]{1,0:T(8,128)(2,1)S(1)}, u32[]{:S(2)}, u32[]{:S(2)}) %collective-permute-start.23) | collective-permute-done | bytes 147488 | tf_op jit(solution)/shard_map/ppermute | solution.py:25
  89.7 0.7 slice.289
  90.4 0.5 collective-permute-done.32
  91.2 0.8 subtract_multiply_fusion
  (118 shorter events, 3.0 us)
Async XLA Ops:
  0.6 12.4 %copy-start.5 = (s32[32]{0:T(128)S(1)}, s32[32]{0:T(128)}, u32[]{:S(2)}) copy-start(s32[32]{0:T(128)} %constant.62.clone) | copy-start | bytes 388
  4.2 18.4 %collective-permute-start.1 = (bf16[64,1152]{1,0:T(8,128)(2,1)S(1)}, bf16[64,1152]{1,0:T(8,128)(2,1)S(1)}, u32[]{:S(2)}, u32[]{:S(2)}) collective-permute-start(bf16[64,1152]{1,0:T(8,128)(2,1)S(1)} %pad_maximum_fusion.10), channel_id=1, source_target_pairs={{0,1},{1,0},{2,3},{3,2},{4,5},{5,4},{6,7},{7,6},{8,9},{9,8},{10,11... | collective-permute-start | bytes 442376 | tf_op jit(solution)/shard_map/ppermute | solution.py:25
  7.2 7.6 %collective-permute-start.4 = (bf16[64,1152]{1,0:T(8,128)(2,1)S(1)}, bf16[64,1152]{1,0:T(8,128)(2,1)S(1)}, u32[]{:S(2)}, u32[]{:S(2)}) collective-permute-start(bf16[64,1152]{1,0:T(8,128)(2,1)S(1)} %pad_maximum_fusion.10), channel_id=1, source_target_pairs={{0,2},{1,3},{2,0},{3,1},{4,6},{5,7},{6,4},{7,5},{8,10},{9,11},{10,... | collective-permute-start | bytes 442376 | tf_op jit(solution)/shard_map/ppermute | solution.py:25
  8.8 14.4 %collective-permute-start.8 = (bf16[64,1152]{1,0:T(8,128)(2,1)S(1)}, bf16[64,1152]{1,0:T(8,128)(2,1)S(1)}, u32[]{:S(2)}, u32[]{:S(2)}) collective-permute-start(bf16[64,1152]{1,0:T(8,128)(2,1)S(1)} %pad_maximum_fusion.10), channel_id=1, source_target_pairs={{0,4},{1,5},{2,6},{3,7},{4,0},{5,1},{6,2},{7,3},{8,12},{9,13},{10,... | collective-permute-start | bytes 442376 | tf_op jit(solution)/shard_map/ppermute | solution.py:25
  11.4 9.6 %collective-permute-start.12 = (bf16[64,1152]{1,0:T(8,128)(2,1)S(1)}, bf16[64,1152]{1,0:T(8,128)(2,1)S(1)}, u32[]{:S(2)}, u32[]{:S(2)}) collective-permute-start(bf16[64,1152]{1,0:T(8,128)(2,1)S(1)} %pad_maximum_fusion.10), channel_id=1, source_target_pairs={{0,6},{1,7},{2,4},{3,5},{4,2},{5,3},{6,0},{7,1},{8,14},{9,15},{10,... | collective-permute-start | bytes 442376 | tf_op jit(solution)/shard_map/ppermute | solution.py:25
  14.3 33.2 %collective-permute-start = (bf16[768,256]{1,0:T(8,128)(2,1)S(1)}, bf16[768,256]{1,0:T(8,128)(2,1)S(1)}, u32[]{:S(2)}, u32[]{:S(2)}) collective-permute-start(bf16[768,256]{1,0:T(8,128)(2,1)S(1)} %bitcast.113), channel_id=1, source_target_pairs={{0,8},{1,9},{2,10},{3,11},{4,12},{5,13},{6,14},{7,15},{8,0},{9,1},... | collective-permute-start | bytes 1179656 | tf_op jit(solution)/shard_map/ppermute | solution.py:25
  14.8 7.8 %copy-start.2 = (bf16[48,1152]{1,0:T(8,128)(2,1)S(1)}, bf16[48,1152]{1,0:T(8,128)(2,1)}, u32[]{:S(2)}) copy-start(bf16[48,1152]{1,0:T(8,128)(2,1)} %param.6) | copy-start | bytes 331780
  14.8 9.0 %copy-start.4 = (bf16[128,1152]{1,0:T(8,128)(2,1)S(1)}, bf16[128,1152]{1,0:T(8,128)(2,1)}, u32[]{:S(2)}) copy-start(bf16[128,1152]{1,0:T(8,128)(2,1)} %get-tuple-element.6) | copy-start | bytes 884740
  14.9 8.9 %collective-permute-start.5 = (bf16[48,1152]{1,0:T(8,128)(2,1)S(1)}, bf16[48,1152]{1,0:T(8,128)(2,1)S(1)}, u32[]{:S(2)}, u32[]{:S(2)}) collective-permute-start(bf16[48,1152]{1,0:T(8,128)(2,1)S(1)} %get-tuple-element.30), channel_id=1, source_target_pairs={{0,16},{1,17},{2,18},{3,19},{4,20},{5,21},{6,22},{7,23},{8,24},{9,... | collective-permute-start | bytes 331784 | tf_op jit(solution)/shard_map/ppermute | solution.py:25
  21.0 11.6 %collective-permute-start.13 = (bf16[48,1152]{1,0:T(8,128)(2,1)S(1)}, bf16[48,1152]{1,0:T(8,128)(2,1)S(1)}, u32[]{:S(2)}, u32[]{:S(2)}) collective-permute-start(bf16[48,1152]{1,0:T(8,128)(2,1)S(1)} %get-tuple-element.32), channel_id=1, source_target_pairs={{0,16},{1,17},{2,18},{3,19},{4,20},{5,21},{6,22},{7,23},{8,24},{9,... | collective-permute-start | bytes 331784 | tf_op jit(solution)/shard_map/ppermute | solution.py:25
  22.6 8.8 %collective-permute-start.2 = (bf16[96,1152]{1,0:T(8,128)(2,1)S(1)}, bf16[96,1152]{1,0:T(8,128)(2,1)S(1)}, u32[]{:S(2)}, u32[]{:S(2)}) collective-permute-start(bf16[96,1152]{1,0:T(8,128)(2,1)S(1)} %pad_maximum_fusion.7), channel_id=1, source_target_pairs={{0,16},{1,17},{2,18},{3,19},{4,20},{5,21},{6,22},{7,23},{8,24},{9,... | collective-permute-start | bytes 663560 | tf_op jit(solution)/shard_map/ppermute | solution.py:25
  23.2 6.5 %collective-permute-start.9 = (bf16[64,1152]{1,0:T(8,128)(2,1)S(1)}, bf16[64,1152]{1,0:T(8,128)(2,1)S(1)}, u32[]{:S(2)}, u32[]{:S(2)}) collective-permute-start(bf16[64,1152]{1,0:T(8,128)(2,1)S(1)} %collective-permute-done.8), channel_id=1, source_target_pairs={{0,1},{1,0},{2,3},{3,2},{4,5},{5,4},{6,7},{7,6},{8,9},{9,8},{10,11... | collective-permute-start | bytes 442376 | tf_op jit(solution)/shard_map/ppermute | solution.py:25
  23.8 8.7 %collective-permute-start.6 = (bf16[112,1152]{1,0:T(8,128)(2,1)S(1)}, bf16[112,1152]{1,0:T(8,128)(2,1)S(1)}, u32[]{:S(2)}, u32[]{:S(2)}) collective-permute-start(bf16[112,1152]{1,0:T(8,128)(2,1)S(1)} %pad_maximum_fusion.5), channel_id=1, source_target_pairs={{0,1},{1,0},{2,3},{3,2},{4,5},{5,4},{6,7},{7,6},{8,9},{9,8},{10,11... | collective-permute-start | bytes 774152 | tf_op jit(solution)/shard_map/ppermute | solution.py:25
  29.8 6.0 %collective-permute-start.10 = (bf16[96,1152]{1,0:T(8,128)(2,1)S(1)}, bf16[96,1152]{1,0:T(8,128)(2,1)S(1)}, u32[]{:S(2)}, u32[]{:S(2)}) collective-permute-start(bf16[96,1152]{1,0:T(8,128)(2,1)S(1)} %pad_maximum_fusion.8), channel_id=1, source_target_pairs={{0,16},{1,17},{2,18},{3,19},{4,20},{5,21},{6,22},{7,23},{8,24},{9,... | collective-permute-start | bytes 663560 | tf_op jit(solution)/shard_map/ppermute | solution.py:25
  31.4 11.7 %collective-permute-start.3 = (bf16[192,1152]{1,0:T(8,128)(2,1)S(1)}, bf16[192,1152]{1,0:T(8,128)(2,1)S(1)}, u32[]{:S(2)}, u32[]{:S(2)}) collective-permute-start(bf16[192,1152]{1,0:T(8,128)(2,1)S(1)} %pad_maximum_fusion.1), channel_id=1, source_target_pairs={{0,8},{1,9},{2,10},{3,11},{4,12},{5,13},{6,14},{7,15},{8,0},{9,1},... | collective-permute-start | bytes 1327112 | tf_op jit(solution)/shard_map/ppermute | solution.py:25
  32.6 7.7 %collective-permute-start.14 = (bf16[112,1152]{1,0:T(8,128)(2,1)S(1)}, bf16[112,1152]{1,0:T(8,128)(2,1)S(1)}, u32[]{:S(2)}, u32[]{:S(2)}) collective-permute-start(bf16[112,1152]{1,0:T(8,128)(2,1)S(1)} %pad_maximum_fusion.6), channel_id=1, source_target_pairs={{0,1},{1,0},{2,3},{3,2},{4,5},{5,4},{6,7},{7,6},{8,9},{9,8},{10,11... | collective-permute-start | bytes 774152 | tf_op jit(solution)/shard_map/ppermute | solution.py:25
  35.8 5.8 %collective-permute-start.11 = (bf16[192,1152]{1,0:T(8,128)(2,1)S(1)}, bf16[192,1152]{1,0:T(8,128)(2,1)S(1)}, u32[]{:S(2)}, u32[]{:S(2)}) collective-permute-start(bf16[192,1152]{1,0:T(8,128)(2,1)S(1)} %pad_maximum_fusion.3), channel_id=1, source_target_pairs={{0,8},{1,9},{2,10},{3,11},{4,12},{5,13},{6,14},{7,15},{8,0},{9,1},... | collective-permute-start | bytes 1327112 | tf_op jit(solution)/shard_map/ppermute | solution.py:25
  36.0 4.5 %collective-permute-start.7 = (bf16[192,1152]{1,0:T(8,128)(2,1)S(1)}, bf16[192,1152]{1,0:T(8,128)(2,1)S(1)}, u32[]{:S(2)}, u32[]{:S(2)}) collective-permute-start(bf16[192,1152]{1,0:T(8,128)(2,1)S(1)} %pad_maximum_fusion.2), channel_id=1, source_target_pairs={{0,8},{1,9},{2,10},{3,11},{4,12},{5,13},{6,14},{7,15},{8,0},{9,1},... | collective-permute-start | bytes 1327112 | tf_op jit(solution)/shard_map/ppermute | solution.py:25
  40.3 1.9 %collective-permute-start.16 = (bf16[128,1152]{1,0:T(8,128)(2,1)S(1)}, bf16[128,1152]{1,0:T(8,128)(2,1)S(1)}, u32[]{:S(2)}, u32[]{:S(2)}) collective-permute-start(bf16[128,1152]{1,0:T(8,128)(2,1)S(1)} %get-tuple-element.22), channel_id=1, source_target_pairs={{0,8},{1,9},{2,10},{3,11},{4,12},{5,13},{6,14},{7,15},{8,0},{9,1},... | collective-permute-start | bytes 884744 | tf_op jit(solution)/shard_map/ppermute | solution.py:25
  40.5 2.1 %collective-permute-start.15 = (bf16[192,1152]{1,0:T(8,128)(2,1)S(1)}, bf16[192,1152]{1,0:T(8,128)(2,1)S(1)}, u32[]{:S(2)}, u32[]{:S(2)}) collective-permute-start(bf16[192,1152]{1,0:T(8,128)(2,1)S(1)} %pad_maximum_fusion.4), channel_id=1, source_target_pairs={{0,8},{1,9},{2,10},{3,11},{4,12},{5,13},{6,14},{7,15},{8,0},{9,1},... | collective-permute-start | bytes 1327112 | tf_op jit(solution)/shard_map/ppermute | solution.py:25
  43.2 0.8 copy-start.6
  44.9 1.6 %collective-permute-start.20 = (bf16[128,1152]{1,0:T(8,128)(2,1)S(1)}, bf16[128,1152]{1,0:T(8,128)(2,1)S(1)}, u32[]{:S(2)}, u32[]{:S(2)}) collective-permute-start(bf16[128,1152]{1,0:T(8,128)(2,1)S(1)} %slice.383), channel_id=1, source_target_pairs={{0,8},{1,9},{2,10},{3,11},{4,12},{5,13},{6,14},{7,15},{8,0},{9,1},... | collective-permute-start | bytes 884744 | tf_op jit(solution)/shard_map/ppermute | solution.py:25
  46.6 6.1 %collective-permute-start.21 = (bf16[4,16,1152]{2,1,0:T(8,128)(2,1)S(1)}, bf16[4,16,1152]{2,1,0:T(8,128)(2,1)S(1)}, u32[]{:S(2)}, u32[]{:S(2)}) collective-permute-start(bf16[4,16,1152]{2,1,0:T(8,128)(2,1)S(1)} %fusion.53), channel_id=1, source_target_pairs={{0,1},{1,0},{2,3},{3,2},{4,5},{5,4},{6,7},{7,6},{8,9},{9,8},{10,11... | collective-permute-start | bytes 442376 | tf_op jit(solution)/shard_map/ppermute | solution.py:25
  47.4 5.9 %collective-permute-start.17 = (bf16[256,1152]{1,0:T(8,128)(2,1)S(1)}, bf16[256,1152]{1,0:T(8,128)(2,1)S(1)}, u32[]{:S(2)}, u32[]{:S(2)}) collective-permute-start(bf16[256,1152]{1,0:T(8,128)(2,1)S(1)} %multiply_convert_fusion), channel_id=1, source_target_pairs={{0,8},{1,9},{2,10},{3,11},{4,12},{5,13},{6,14},{7,15},{8,0},{9,1},... | collective-permute-start | bytes 1769480 | tf_op jit(solution)/shard_map/ppermute | solution.py:25
  52.7 7.2 %collective-permute-start.22 = (bf16[4,16,1152]{2,1,0:T(8,128)(2,1)S(1)}, bf16[4,16,1152]{2,1,0:T(8,128)(2,1)S(1)}, u32[]{:S(2)}, u32[]{:S(2)}) collective-permute-start(bf16[4,16,1152]{2,1,0:T(8,128)(2,1)S(1)} %fusion.51), channel_id=1, source_target_pairs={{0,16},{1,17},{2,18},{3,19},{4,20},{5,21},{6,22},{7,23},{8,24},{9,... | collective-permute-start | bytes 442376 | tf_op jit(solution)/shard_map/ppermute | solution.py:25
  53.8 0.9 %copy-start.1 = (f32[192,1152]{1,0:T(8,128)}, f32[192,1152]{1,0:T(8,128)S(1)}, u32[]{:S(2)}) copy-start(f32[192,1152]{1,0:T(8,128)S(1)} %fusion.44) | copy-start | bytes 2654212
  54.7 2.0 %copy-start = (f32[192,1152]{1,0:T(8,128)}, f32[192,1152]{1,0:T(8,128)S(1)}, u32[]{:S(2)}) copy-start(f32[192,1152]{1,0:T(8,128)S(1)} %fusion.47) | copy-start | bytes 2654212
  54.7 9.4 %collective-permute-start.27 = (bf16[2,48,1152]{2,1,0:T(8,128)(2,1)S(1)}, bf16[2,48,1152]{2,1,0:T(8,128)(2,1)S(1)}, u32[]{:S(2)}, u32[]{:S(2)}) collective-permute-start(bf16[2,48,1152]{2,1,0:T(8,128)(2,1)S(1)} %bitcast.115), channel_id=1, source_target_pairs={{0,16},{1,17},{2,18},{3,19},{4,20},{5,21},{6,22},{7,23},{8,24},{9,... | collective-permute-start | bytes 663560 | tf_op jit(solution)/shard_map/ppermute | solution.py:25
  56.8 8.4 %collective-permute-start.29 = (bf16[2,48,1152]{2,1,0:T(8,128)(2,1)S(1)}, bf16[2,48,1152]{2,1,0:T(8,128)(2,1)S(1)}, u32[]{:S(2)}, u32[]{:S(2)}) collective-permute-start(bf16[2,48,1152]{2,1,0:T(8,128)(2,1)S(1)} %fusion.35), channel_id=1, source_target_pairs={{0,1},{1,0},{2,3},{3,2},{4,5},{5,4},{6,7},{7,6},{8,9},{9,8},{10,11... | collective-permute-start | bytes 663560 | tf_op jit(solution)/shard_map/ppermute | solution.py:25
  57.8 6.4 %slice-start.1 = ((f32[192,1152]{1,0:T(8,128)}), f32[96,1152]{1,0:T(8,128)S(1)}, s32[]{:S(2)}) async-start(f32[192,1152]{1,0:T(8,128)} %copy-done.1), calls=%async_computation.1 | async-start | bytes 884736 | tf_op jit(solution)/shard_map/slice | solution.py:139
  57.8 11.2 %collective-permute-start.24 = (bf16[2,48,1152]{2,1,0:T(8,128)(2,1)S(1)}, bf16[2,48,1152]{2,1,0:T(8,128)(2,1)S(1)}, u32[]{:S(2)}, u32[]{:S(2)}) collective-permute-start(bf16[2,48,1152]{2,1,0:T(8,128)(2,1)S(1)} %fusion.34), channel_id=1, source_target_pairs={{0,1},{1,0},{2,3},{3,2},{4,5},{5,4},{6,7},{7,6},{8,9},{9,8},{10,11... | collective-permute-start | bytes 663560 | tf_op jit(solution)/shard_map/ppermute | solution.py:25
  59.4 10.4 %collective-permute-start.18 = (bf16[2,48,1152]{2,1,0:T(8,128)(2,1)S(1)}, bf16[2,48,1152]{2,1,0:T(8,128)(2,1)S(1)}, u32[]{:S(2)}, u32[]{:S(2)}) collective-permute-start(bf16[2,48,1152]{2,1,0:T(8,128)(2,1)S(1)} %bitcast.114), channel_id=1, source_target_pairs={{0,16},{1,17},{2,18},{3,19},{4,20},{5,21},{6,22},{7,23},{8,24},{9,... | collective-permute-start | bytes 663560 | tf_op jit(solution)/shard_map/ppermute | solution.py:25
  64.3 5.6 %slice-start = ((f32[192,1152]{1,0:T(8,128)}), f32[96,1152]{1,0:T(8,128)S(1)}, s32[]{:S(2)}) async-start(f32[192,1152]{1,0:T(8,128)} %copy-done), calls=%async_computation | async-start | bytes 884736 | tf_op jit(solution)/shard_map/slice | solution.py:139
  64.3 15.6 %collective-permute-start.28 = (bf16[48,1152]{1,0:T(8,128)(2,1)S(1)}, bf16[48,1152]{1,0:T(8,128)(2,1)S(1)}, u32[]{:S(2)}, u32[]{:S(2)}) collective-permute-start(bf16[48,1152]{1,0:T(8,128)(2,1)S(1)} %fusion.56), channel_id=1, source_target_pairs={{0,1},{1,0},{2,3},{3,2},{4,5},{5,4},{6,7},{7,6},{8,9},{9,8},{10,11... | collective-permute-start | bytes 331784 | tf_op jit(solution)/shard_map/ppermute | solution.py:25
  65.3 5.8 %collective-permute-start.30 = (bf16[48,1152]{1,0:T(8,128)(2,1)S(1)}, bf16[48,1152]{1,0:T(8,128)(2,1)S(1)}, u32[]{:S(2)}, u32[]{:S(2)}) collective-permute-start(bf16[48,1152]{1,0:T(8,128)(2,1)S(1)} %fusion.57), channel_id=1, source_target_pairs={{0,16},{1,17},{2,18},{3,19},{4,20},{5,21},{6,22},{7,23},{8,24},{9,... | collective-permute-start | bytes 331784 | tf_op jit(solution)/shard_map/ppermute | solution.py:25
  69.1 5.5 %collective-permute-start.25 = (bf16[48,1152]{1,0:T(8,128)(2,1)S(1)}, bf16[48,1152]{1,0:T(8,128)(2,1)S(1)}, u32[]{:S(2)}, u32[]{:S(2)}) collective-permute-start(bf16[48,1152]{1,0:T(8,128)(2,1)S(1)} %fusion.55), channel_id=1, source_target_pairs={{0,16},{1,17},{2,18},{3,19},{4,20},{5,21},{6,22},{7,23},{8,24},{9,... | collective-permute-start | bytes 331784 | tf_op jit(solution)/shard_map/ppermute | solution.py:25
  69.9 7.9 %collective-permute-start.19 = (bf16[48,1152]{1,0:T(8,128)(2,1)S(1)}, bf16[48,1152]{1,0:T(8,128)(2,1)S(1)}, u32[]{:S(2)}, u32[]{:S(2)}) collective-permute-start(bf16[48,1152]{1,0:T(8,128)(2,1)S(1)} %fusion.54), channel_id=1, source_target_pairs={{0,1},{1,0},{2,3},{3,2},{4,5},{5,4},{6,7},{7,6},{8,9},{9,8},{10,11... | collective-permute-start | bytes 331784 | tf_op jit(solution)/shard_map/ppermute | solution.py:25
  71.1 8.7 %collective-permute-start.31 = (bf16[64,1152]{1,0:T(8,128)(2,1)S(1)}, bf16[64,1152]{1,0:T(8,128)(2,1)S(1)}, u32[]{:S(2)}, u32[]{:S(2)}) collective-permute-start(bf16[64,1152]{1,0:T(8,128)(2,1)S(1)} %pad_maximum_fusion.13), channel_id=1, source_target_pairs={{0,2},{1,3},{2,0},{3,1},{4,6},{5,7},{6,4},{7,5},{8,10},{9,11},{10,... | collective-permute-start | bytes 442376 | tf_op jit(solution)/shard_map/ppermute | solution.py:25
  74.7 9.2 %collective-permute-start.26 = (bf16[64,1152]{1,0:T(8,128)(2,1)S(1)}, bf16[64,1152]{1,0:T(8,128)(2,1)S(1)}, u32[]{:S(2)}, u32[]{:S(2)}) collective-permute-start(bf16[64,1152]{1,0:T(8,128)(2,1)S(1)} %pad_maximum_fusion.12), channel_id=1, source_target_pairs={{0,6},{1,7},{2,4},{3,5},{4,2},{5,3},{6,0},{7,1},{8,14},{9,15},{10,... | collective-permute-start | bytes 442376 | tf_op jit(solution)/shard_map/ppermute | solution.py:25
  77.8 13.2 %copy-start.3 = (bf16[32,1152]{1,0:T(8,128)(2,1)S(1)}, bf16[32,1152]{1,0:T(8,128)(2,1)}, u32[]{:S(2)}) copy-start(bf16[32,1152]{1,0:T(8,128)(2,1)} %param.8) | copy-start | bytes 221188
  77.8 11.7 %collective-permute-start.23 = (bf16[64,1152]{1,0:T(8,128)(2,1)S(1)}, bf16[64,1152]{1,0:T(8,128)(2,1)S(1)}, u32[]{:S(2)}, u32[]{:S(2)}) collective-permute-start(bf16[64,1152]{1,0:T(8,128)(2,1)S(1)} %pad_maximum_fusion.11), channel_id=1, source_target_pairs={{0,4},{1,5},{2,6},{3,7},{4,0},{5,1},{6,2},{7,3},{8,12},{9,13},{10,... | collective-permute-start | bytes 442376 | tf_op jit(solution)/shard_map/ppermute | solution.py:25
  89.6 1.3 %collective-permute-start.32 = (f32[16,1152]{1,0:T(8,128)S(1)}, f32[16,1152]{1,0:T(8,128)S(1)}, u32[]{:S(2)}, u32[]{:S(2)}) collective-permute-start(f32[16,1152]{1,0:T(8,128)S(1)} %slice.290), channel_id=1, source_target_pairs={{0,8},{1,9},{2,10},{3,11},{4,12},{5,13},{6,14},{7,15},{8,0},{9,1},... | collective-permute-start | bytes 221192 | tf_op jit(solution)/shard_map/ppermute | solution.py:25

commit v2 on v1

v2 whole, which is shorter than its diff:
```python
import jax
import jax.numpy as jnp
from jax import lax
from jax.sharding import PartitionSpec as P

epsilon = 1e-06
logit_scale = 10.0
logit_bias = -5.0
axes = ("grp", "blk")


def unit_rows(raw_rows):
    inverse = lax.rsqrt(jnp.sum(raw_rows * raw_rows, axis=1, keepdims=True) + epsilon)
    return (raw_rows * inverse, inverse)


def make_shards(grp_size, blk_size):
    devices = grp_size * blk_size
    core_mask, y_mask, x_mask = blk_size, 2 * blk_size, 1
    depth = blk_size // 2
    assert grp_size == 4 and blk_size & (blk_size - 1) == 0 and depth >= 4
    chunks = [[0], list(range(1, depth - 1)), [depth - 1]]

    def swap(array, mask):
        return lax.ppermute(array, axes, [(i, i ^ mask) for i in range(devices)])

    def swap_by_core(array, masks):
        pairs = [(i, i ^ masks[1 if i & core_mask else 0]) for i in range(devices)]
        return lax.ppermute(array, axes, pairs)

    def first(array):
        return swap_by_core(array, (x_mask, y_mask))

    def second(array):
        return swap_by_core(array, (y_mask, x_mask))

    def shards(pooled, img_weight, img_label, text_raw):
        images, width = pooled.shape
        rows, embed = img_weight.shape
        texts = text_raw.shape[0]
        quarter = texts // grp_size
        grp, blk = lax.axis_index("grp"), lax.axis_index("blk")
        core, side = grp % 2, grp // 2
        place = grp * blk_size + blk

        first_mask = jnp.where(core == 0, x_mask, y_mask)
        second_mask = jnp.where(core == 0, y_mask, x_mask)
        chunk_masks = []
        for chunk in chunks:
            kz = jnp.asarray([2 * k for k in chunk], dtype=jnp.int32)
            by_core = []
            for kc in range(2):
                f, s = (first_mask, second_mask) if kc == 0 else (second_mask, first_mask)
                j = jnp.stack([0 * f, f, s, f ^ s]).astype(jnp.int32)
                by_core.append((j[:, None] ^ kz[None, :] ^ (kc * core_mask)).reshape(-1))
            chunk_masks.append(jnp.concatenate(by_core))
        sources = [place ^ m for m in chunk_masks]

        own = jnp.concatenate(
            [img_weight, lax.dynamic_slice_in_dim(text_raw, grp * quarter, quarter, 0)], axis=0
        )[None]
        by_z = [own] + [None] * (depth - 1)
        for kz in range(1, depth):
            by_z[kz] = swap(own, 2 * kz)
        gathered = []
        last = None
        for chunk in chunks:
            block = jnp.concatenate([by_z[kz] for kz in chunk], axis=0)
            if last is not None and chunk is chunks[-1]:
                block, _ = lax.optimization_barrier((block, gathered[0]))
            pair = jnp.concatenate([block, first(block)], axis=0)
            quad = jnp.concatenate([pair, second(pair)], axis=0)
            last = quad
            gathered.append(jnp.concatenate([quad, swap(quad, core_mask)], axis=0))

        turned = pooled.T.reshape(devices, rows, images)
        columns = [jnp.take(turned, s, axis=0).reshape(2, -1, images) for s in sources]
        theirs = swap(jnp.concatenate([c[1] for c in columns], axis=0), core_mask)

        text_all = jnp.concatenate([g[:, rows:].reshape(-1, embed) for g in gathered], axis=0)
        text_all = unit_rows(text_all.astype(jnp.float32))[0].astype(jnp.bfloat16)
        text_place = jnp.concatenate(sources)
        text_first = (text_place % blk_size) * texts + (text_place // blk_size) * quarter
        text_ids = (text_first[:, None] + jnp.arange(quarter, dtype=jnp.int32)[None, :]).reshape(-1)

        projected = sum(
            lax.dot_general(
                c.reshape(-1, images),
                g[:, :rows].reshape(-1, embed),
                (((0,), (0,)), ((), ())),
                preferred_element_type=jnp.float32,
            )
            for c, g in zip(columns, gathered)
        )
        embed_float, inverse = unit_rows(projected)
        embedded = embed_float.astype(jnp.bfloat16)

        logits = (
            logit_scale
            * lax.dot_general(
                embedded, text_all, (((1,), (1,)), ((), ())), preferred_element_type=jnp.float32
            )
            + logit_bias
        )
        polarity = jnp.where(img_label[:, None] == text_ids[None, :], 1.0, -1.0).astype(jnp.float32)
        pair_slope = (
            -polarity * jax.nn.sigmoid(-polarity * logits) * (logit_scale / texts)
        ).astype(jnp.bfloat16)
        grad_embed = jnp.dot(pair_slope, text_all, preferred_element_type=jnp.float32)
        grad_proj = (
            inverse
            * (grad_embed - embed_float * jnp.sum(grad_embed * embed_float, axis=1, keepdims=True))
        ).astype(jnp.bfloat16)

        grad_unit = lax.dot_general(
            pair_slope, embedded, (((0,), (0,)), ((), ())), preferred_element_type=jnp.float32
        )
        at, keep, send = 0, [], []
        for chunk in chunks:
            size = 4 * len(chunk) * quarter
            keep.append(grad_unit[at : at + size])
            send.append(grad_unit[at + size : at + 2 * size].astype(jnp.bfloat16))
            at += 2 * size
        grad_unit = jnp.concatenate(keep, axis=0) + swap(
            jnp.concatenate(send, axis=0), core_mask
        ).astype(jnp.float32)

        grad_both = jnp.concatenate([grad_proj, swap(grad_proj, core_mask)], axis=0)
        text_at = [4 * quarter * sum(len(c) for c in chunks[:i]) for i in range(len(chunks))]
        row_at = [4 * rows * sum(len(c) for c in chunks[:i]) for i in range(len(chunks))]
        total = None
        for i in (2, 1, 0):
            chunk = chunks[i]
            count = len(chunk)
            both = jnp.concatenate(
                [columns[i][0], theirs[row_at[i] : row_at[i] + 4 * count * rows]], axis=1
            )
            part = jnp.dot(both, grad_both, preferred_element_type=jnp.float32)
            text_part = grad_unit[text_at[i] : text_at[i] + 4 * count * quarter]
            part = jnp.concatenate(
                [
                    part.reshape(4, count, rows, embed),
                    text_part.reshape(4, count, quarter, embed),
                ],
                axis=2,
            )
            part = part[:2] + second(part[2:].astype(jnp.bfloat16)).astype(jnp.float32)
            part = part[0] + first(part[1].astype(jnp.bfloat16)).astype(jnp.float32)
            for k, kz in enumerate(chunk):
                piece = part[k]
                if kz:
                    piece = swap(piece.astype(jnp.bfloat16), 2 * kz).astype(jnp.float32)
                total = piece if total is None else total + piece
        grad_weight = total[:rows]

        def joined(array, mask, position):
            other = swap(array, mask)
            return jnp.where(
                position == 0,
                jnp.concatenate([array, other], axis=0),
                jnp.concatenate([other, array], axis=0),
            )

        grad_unit = joined(joined(total[rows:], core_mask, core), y_mask, side)
        text_float, text_inverse = unit_rows(text_raw.astype(jnp.float32))
        grad_text = text_inverse * (
            grad_unit - text_float * jnp.sum(grad_unit * text_float, axis=1, keepdims=True)
        )
        return (grad_weight, grad_text)

    return shards


def solution(mesh):
    return jax.shard_map(
        make_shards(mesh.shape["grp"], mesh.shape["blk"]),
        mesh=mesh,
        in_specs=(
            P(("grp", "blk"), None),
            P(("grp", "blk"), None),
            P(("grp", "blk")),
            P("blk", None),
        ),
        out_specs=(P(("grp", "blk"), None), P("blk", None)),
        check_vma=False,
    )
```

time: 92.2 us -> 88.8 us (0.963)
  starting transfers between devices: 33.8 us -> 30.1 us
  local copies, waits for them, and re-layouts: 4.97 us -> 6.37 us
    ppermute x33 -> x14, waiting for transfers between devices: 41 us -> 14.6 us  [swap(): return lax.ppermute(array, axes, [(i, i ^ mask) for i in range(devices)])]
    ppermute x0 -> x12, waiting for transfers between devices: none -> 26.2 us  [swap_by_core(): return lax.ppermute(array, axes, pairs)]
    ppermute x33 -> x14, starting transfers between devices: 33.8 us -> 12.9 us  [swap(): return lax.ppermute(array, axes, [(i, i ^ mask) for i in range(devices)])]
    ppermute x0 -> x12, starting transfers between devices: none -> 17.2 us  [swap_by_core(): return lax.ppermute(array, axes, pairs)]
    gather x1 -> x3, local copies, waits for them, and re-layouts: 0.6 us -> 1.69 us  [shards(): jnp.take(turned, s, axis=0).reshape(2, -1, images)]
    mul x3 -> x0, other arithmetic: 0.98 us -> none  [the longest x1 0.97 us: unit_rows(): return (raw_rows * inverse, inverse)]
    dot_general x8 -> x6, matrix products: 3.98 us -> 3.39 us  [the longest x3 1.84 us: shards(): lax.dot_general(c.reshape(-1, images), g[:, :rows].reshape(-1, embed), ((...]
    unnamed x29 -> x14, local copies, waits for them, and re-layouts: 2.72 us -> 2.21 us
  transfers between devices with their start and end apart: 33 -> 26, of which waited for: 15 -> 15; matrix products, arithmetic and copies ran while one was open for 12% -> 10% of each run, Pallas kernels for 0% -> 0%
where the time goes in v2:
time: 88.8 us; the launch traced here: 88.5 us
  waiting for transfers between devices  40.9 us (46%)
  starting transfers between devices  30.1 us (34%)
  local copies, waits for them, and re-layouts  6.37 us (7%)
  other arithmetic  5.12 us (6%)
  matrix products  4.85 us (5%)
  between operations  1.18 us (1%)
    ppermute x12, waiting for transfers between devices, swap_by_core(): return lax.ppermute(array, axes, pairs)  26.2 us
    ppermute x12, starting transfers between devices, swap_by_core(): return lax.ppermute(array, axes, pairs)  17.2 us
    ppermute x14, waiting for transfers between devices, swap(): return lax.ppermute(array, axes, [(i, i ^ mask) for i in range(devices)])  14.6 us
    ppermute x14, starting transfers between devices, swap(): return lax.ppermute(array, axes, [(i, i ^ mask) for i in range(devices)])  12.9 us
    unnamed x14, local copies, waits for them, and re-layouts  2.21 us
    dot_general x3, matrix products, shards(): lax.dot_general(c.reshape(-1, images), g[:, :rows].reshape(-1, embed), ((...  1.84 us
  transfers between devices with their start and end apart: 26, of which 15 were waited for; matrix products, arithmetic and copies ran while one was open for 10% of the time, Pallas kernels for 0%

profile of v2, /device:TPU:0, one launch (start us, length us, event | category | flops | bytes accessed | tf_op | source)
XLA Modules:
  0.0 88.5 jit_solution(7315146175543247020)
XLA Ops:
  0.6 0.7 constant_dynamic-slice_fusion
  1.4 0.9 %maximum_bitcast_fusion = bf16[1,56,1152]{2,1,0:T(8,128)(2,1)S(1)} fusion(bf16[8,1152]{1,0:T(8,128)(2,1)S(1)} %constant_dynamic-slice_fusion, bf16[48,1152]{1,0:T(8,128)(2,1)} %param.10), kind=kLoop, calls=%fused_computation.108 | loop fusion | flops 258048 | bytes 258048 | tf_op jit(solution)/shard_map/broadcast_in_dim | solution.py:59
  2.3 3.0 %collective-permute-start.1 = (bf16[1,56,1152]{2,1,0:T(8,128)(2,1)S(1)}, bf16[1,56,1152]{2,1,0:T(8,128)(2,1)S(1)}, u32[]{:S(2)}, u32[]{:S(2)}) collective-permute-start(bf16[1,56,1152]{2,1,0:T(8,128)(2,1)S(1)} %maximum_bitcast_fusion), channel_id=1, source_target_pairs={{0,1},{1,0},{2,3},{3,2},{4,5},{5,4},{6,7},{7,6},{8,24},{9,25},{10,... | collective-permute-start | bytes 387080 | tf_op jit(solution)/shard_map/ppermute | solution.py:29
  5.3 3.6 %collective-permute-start.9 = (bf16[1,56,1152]{2,1,0:T(8,128)(2,1)S(1)}, bf16[1,56,1152]{2,1,0:T(8,128)(2,1)S(1)}, u32[]{:S(2)}, u32[]{:S(2)}) collective-permute-start(bf16[1,56,1152]{2,1,0:T(8,128)(2,1)S(1)} %maximum_bitcast_fusion), channel_id=1, source_target_pairs={{0,6},{1,7},{2,4},{3,5},{4,2},{5,3},{6,0},{7,1},{8,14},{9,15},{10,... | collective-permute-start | bytes 387080 | tf_op jit(solution)/shard_map/ppermute | solution.py:25
  8.9 0.8 collective-permute-start.5
  9.7 0.7 broadcast_xor_fusion
  10.9 1.4 %copy.13 = bf16[256,1536]{0,1:T(8,128)(2,1)S(1)} copy(bf16[256,1536]{1,0:T(8,128)(2,1)} %param.9) | data formatting | bytes 1572864 | tf_op args[0]
  12.4 0.6 gather_fusion
  13.0 0.6 gather_fusion.2
  13.7 0.6 gather_fusion.1
  14.6 0.1 broadcast_select_fusion
  15.0 0.1 add.156
  15.1 1.6 %collective-permute-start.2 = (bf16[2,56,1152]{2,1,0:T(8,128)(2,1)S(1)}, bf16[2,56,1152]{2,1,0:T(8,128)(2,1)S(1)}, u32[]{:S(2)}, u32[]{:S(2)}) collective-permute-start(bf16[2,56,1152]{2,1,0:T(8,128)(2,1)S(1)} %pad_maximum_fusion.15), channel_id=1, source_target_pairs={{0,16},{1,17},{2,18},{3,19},{4,20},{5,21},{6,22},{7,23},{8,9},{9,8... | collective-permute-start | bytes 774152 | tf_op jit(solution)/shard_map/ppermute | solution.py:29
  16.7 2.8 %collective-permute-done.5 = bf16[1,56,1152]{2,1,0:T(8,128)(2,1)S(1)} collective-permute-done((bf16[1,56,1152]{2,1,0:T(8,128)(2,1)S(1)}, bf16[1,56,1152]{2,1,0:T(8,128)(2,1)S(1)}, u32[]{:S(2)}, u32[]{:S(2)}) %collective-permute-start.5) | collective-permute-done | bytes 129056 | tf_op jit(solution)/shard_map/ppermute | solution.py:25
  19.6 1.6 %collective-permute-start.6 = (bf16[2,56,1152]{2,1,0:T(8,128)(2,1)S(1)}, bf16[2,56,1152]{2,1,0:T(8,128)(2,1)S(1)}, u32[]{:S(2)}, u32[]{:S(2)}) collective-permute-start(bf16[2,56,1152]{2,1,0:T(8,128)(2,1)S(1)} %pad_maximum_fusion.16), channel_id=1, source_target_pairs={{0,1},{1,0},{2,3},{3,2},{4,5},{5,4},{6,7},{7,6},{8,24},{9,25},{10,... | collective-permute-start | bytes 774152 | tf_op jit(solution)/shard_map/ppermute | solution.py:29
  21.2 0.5 collective-permute-done.2
  21.8 4.2 %collective-permute-done.6 = bf16[2,56,1152]{2,1,0:T(8,128)(2,1)S(1)} collective-permute-done((bf16[2,56,1152]{2,1,0:T(8,128)(2,1)S(1)}, bf16[2,56,1152]{2,1,0:T(8,128)(2,1)S(1)}, u32[]{:S(2)}, u32[]{:S(2)}) %collective-permute-start.6) | collective-permute-done | bytes 258080 | tf_op jit(solution)/shard_map/ppermute | solution.py:29
  26.0 0.6 collective-permute-start.7
  26.7 0.1 pad_maximum_fusion.2
  26.8 0.6 copy-done.1
  27.4 1.5 %collective-permute-start.10 = (bf16[1,56,1152]{2,1,0:T(8,128)(2,1)S(1)}, bf16[1,56,1152]{2,1,0:T(8,128)(2,1)S(1)}, u32[]{:S(2)}, u32[]{:S(2)}) collective-permute-start(bf16[1,56,1152]{2,1,0:T(8,128)(2,1)S(1)} %collective-permute-done.9), channel_id=1, source_target_pairs={{0,1},{1,0},{2,3},{3,2},{4,5},{5,4},{6,7},{7,6},{8,24},{9,25},{10,... | collective-permute-start | bytes 387080 | tf_op jit(solution)/shard_map/ppermute | solution.py:29
  28.9 4.9 %collective-permute-done.10 = bf16[1,56,1152]{2,1,0:T(8,128)(2,1)S(1)} collective-permute-done((bf16[1,56,1152]{2,1,0:T(8,128)(2,1)S(1)}, bf16[1,56,1152]{2,1,0:T(8,128)(2,1)S(1)}, u32[]{:S(2)}, u32[]{:S(2)}) %collective-permute-start.10) | collective-permute-done | bytes 129056 | tf_op jit(solution)/shard_map/ppermute | solution.py:29
  33.8 1.6 %collective-permute-start.11 = (bf16[2,56,1152]{2,1,0:T(8,128)(2,1)S(1)}, bf16[2,56,1152]{2,1,0:T(8,128)(2,1)S(1)}, u32[]{:S(2)}, u32[]{:S(2)}) collective-permute-start(bf16[2,56,1152]{2,1,0:T(8,128)(2,1)S(1)} %pad_maximum_fusion.17), channel_id=1, source_target_pairs={{0,16},{1,17},{2,18},{3,19},{4,20},{5,21},{6,22},{7,23},{8,9},{9,8... | collective-permute-start | bytes 774152 | tf_op jit(solution)/shard_map/ppermute | solution.py:29
  35.4 1.1 %collective-permute-done.7 = bf16[4,56,1152]{2,1,0:T(8,128)(2,1)S(1)} collective-permute-done((bf16[4,56,1152]{2,1,0:T(8,128)(2,1)S(1)}, bf16[4,56,1152]{2,1,0:T(8,128)(2,1)S(1)}, u32[]{:S(2)}, u32[]{:S(2)}) %collective-permute-start.7) | collective-permute-done | bytes 516128 | tf_op jit(solution)/shard_map/ppermute | solution.py:29
  36.5 0.1 pad_maximum_fusion.3
  36.8 3.4 %collective-permute-done.11 = bf16[2,56,1152]{2,1,0:T(8,128)(2,1)S(1)} collective-permute-done((bf16[2,56,1152]{2,1,0:T(8,128)(2,1)S(1)}, bf16[2,56,1152]{2,1,0:T(8,128)(2,1)S(1)}, u32[]{:S(2)}, u32[]{:S(2)}) %collective-permute-start.11) | collective-permute-done | bytes 258080 | tf_op jit(solution)/shard_map/ppermute | solution.py:29
  40.4 1.8 %collective-permute-done.12 = bf16[4,56,1152]{2,1,0:T(8,128)(2,1)S(1)} collective-permute-done((bf16[4,56,1152]{2,1,0:T(8,128)(2,1)S(1)}, bf16[4,56,1152]{2,1,0:T(8,128)(2,1)S(1)}, u32[]{:S(2)}, u32[]{:S(2)}) %collective-permute-start.12) | collective-permute-done | bytes 516128 | tf_op jit(solution)/shard_map/ppermute | solution.py:25
  42.3 0.1 constant_dynamic-update-slice_fusion
  42.5 0.7 convolution_bitcast_fusion.1
  43.2 0.2 fusion.3
  43.4 0.5 fusion.1
  44.0 0.6 multiply_reduce_fusion.1
  44.7 0.5 fusion.13
  45.2 0.5 multiply_reduce_fusion
  45.7 0.4 fusion.76
  46.2 0.2 multiply_convert_fusion
  46.4 0.2 collective-permute-start.13
  46.6 0.4 collective-permute-start.14
  47.1 1.8 %collective-permute-done.14 = bf16[128,1152]{1,0:T(8,128)(2,1)S(1)} collective-permute-done((bf16[128,1152]{1,0:T(8,128)(2,1)S(1)}, bf16[128,1152]{1,0:T(8,128)(2,1)S(1)}, u32[]{:S(2)}, u32[]{:S(2)}) %collective-permute-start.14) | collective-permute-done | bytes 294944 | tf_op jit(solution)/shard_map/ppermute | solution.py:25
  49.0 0.4 fusion.32
  49.5 1.6 %collective-permute-start.15 = (bf16[2,1,56,1152]{3,2,1,0:T(8,128)(2,1)S(1)}, bf16[2,1,56,1152]{3,2,1,0:T(8,128)(2,1)S(1)}, u32[]{:S(2)}, u32[]{:S(2)}) collective-permute-start(bf16[2,1,56,1152]{3,2,1,0:T(8,128)(2,1)S(1)} %fusion.26), channel_id=1, source_target_pairs={{0,16},{1,17},{2,18},{3,19},{4,20},{5,21},{6,22},{7,23},{8,9},{9,8... | collective-permute-start | bytes 774152 | tf_op jit(solution)/shard_map/ppermute | solution.py:29
  51.1 0.7 fusion.27
  51.9 0.9 collective-permute-start.18
  52.7 0.4 fusion.31
  53.2 1.3 %collective-permute-start.22 = (bf16[2,1,56,1152]{3,2,1,0:T(8,128)(2,1)S(1)}, bf16[2,1,56,1152]{3,2,1,0:T(8,128)(2,1)S(1)}, u32[]{:S(2)}, u32[]{:S(2)}) collective-permute-start(bf16[2,1,56,1152]{3,2,1,0:T(8,128)(2,1)S(1)} %fusion.23), channel_id=1, source_target_pairs={{0,16},{1,17},{2,18},{3,19},{4,20},{5,21},{6,22},{7,23},{8,9},{9,8... | collective-permute-start | bytes 774152 | tf_op jit(solution)/shard_map/ppermute | solution.py:29
  54.5 1.4 %collective-permute-done.15 = bf16[2,1,56,1152]{3,2,1,0:T(8,128)(2,1)S(1)} collective-permute-done((bf16[2,1,56,1152]{3,2,1,0:T(8,128)(2,1)S(1)}, bf16[2,1,56,1152]{3,2,1,0:T(8,128)(2,1)S(1)}, u32[]{:S(2)}, u32[]{:S(2)}) %collective-permute-start.15) | collective-permute-done | bytes 258080 | tf_op jit(solution)/shard_map/ppermute | solution.py:29
  56.0 1.6 %collective-permute-start.16 = (bf16[1,56,1152]{2,1,0:T(8,128)(2,1)S(1)}, bf16[1,56,1152]{2,1,0:T(8,128)(2,1)S(1)}, u32[]{:S(2)}, u32[]{:S(2)}) collective-permute-start(bf16[1,56,1152]{2,1,0:T(8,128)(2,1)S(1)} %fusion.52), channel_id=1, source_target_pairs={{0,1},{1,0},{2,3},{3,2},{4,5},{5,4},{6,7},{7,6},{8,24},{9,25},{10,... | collective-permute-start | bytes 387080 | tf_op jit(solution)/shard_map/ppermute | solution.py:29
  57.6 8.0 %collective-permute-done.22 = bf16[2,1,56,1152]{3,2,1,0:T(8,128)(2,1)S(1)} collective-permute-done((bf16[2,1,56,1152]{3,2,1,0:T(8,128)(2,1)S(1)}, bf16[2,1,56,1152]{3,2,1,0:T(8,128)(2,1)S(1)}, u32[]{:S(2)}, u32[]{:S(2)}) %collective-permute-start.22) | collective-permute-done | bytes 258080 | tf_op jit(solution)/shard_map/ppermute | solution.py:29
  65.7 1.6 %collective-permute-start.23 = (bf16[1,56,1152]{2,1,0:T(8,128)(2,1)S(1)}, bf16[1,56,1152]{2,1,0:T(8,128)(2,1)S(1)}, u32[]{:S(2)}, u32[]{:S(2)}) collective-permute-start(bf16[1,56,1152]{2,1,0:T(8,128)(2,1)S(1)} %fusion.53), channel_id=1, source_target_pairs={{0,1},{1,0},{2,3},{3,2},{4,5},{5,4},{6,7},{7,6},{8,24},{9,25},{10,... | collective-permute-start | bytes 387080 | tf_op jit(solution)/shard_map/ppermute | solution.py:29
  67.2 0.1 fusion.15
  67.4 0.6 collective-permute-start.19
  68.0 3.1 %collective-permute-start.17 = (bf16[56,1152]{1,0:T(8,128)(2,1)S(1)}, bf16[56,1152]{1,0:T(8,128)(2,1)S(1)}, u32[]{:S(2)}, u32[]{:S(2)}) collective-permute-start(bf16[56,1152]{1,0:T(8,128)(2,1)S(1)} %fusion.51), channel_id=1, source_target_pairs={{0,6},{1,7},{2,4},{3,5},{4,2},{5,3},{6,0},{7,1},{8,14},{9,15},{10,... | collective-permute-start | bytes 387080 | tf_op jit(solution)/shard_map/ppermute | solution.py:25
  71.1 2.7 %collective-permute-done.19 = bf16[2,56,1152]{2,1,0:T(8,128)(2,1)S(1)} collective-permute-done((bf16[2,56,1152]{2,1,0:T(8,128)(2,1)S(1)}, bf16[2,56,1152]{2,1,0:T(8,128)(2,1)S(1)}, u32[]{:S(2)}, u32[]{:S(2)}) %collective-permute-start.19) | collective-permute-done | bytes 258080 | tf_op jit(solution)/shard_map/ppermute | solution.py:29
  73.9 0.4 collective-permute-start.20
  74.2 2.9 %collective-permute-start.21 = (bf16[56,1152]{1,0:T(8,128)(2,1)S(1)}, bf16[56,1152]{1,0:T(8,128)(2,1)S(1)}, u32[]{:S(2)}, u32[]{:S(2)}) collective-permute-start(bf16[56,1152]{1,0:T(8,128)(2,1)S(1)} %get-tuple-element.26), channel_id=1, source_target_pairs={{0,4},{1,5},{2,6},{3,7},{4,0},{5,1},{6,2},{7,3},{8,12},{9,13},{10,... | collective-permute-start | bytes 387080 | tf_op jit(solution)/shard_map/ppermute | solution.py:25
  77.2 2.0 %collective-permute-done.20 = bf16[56,1152]{1,0:T(8,128)(2,1)S(1)} collective-permute-done((bf16[56,1152]{1,0:T(8,128)(2,1)S(1)}, bf16[56,1152]{1,0:T(8,128)(2,1)S(1)}, u32[]{:S(2)}, u32[]{:S(2)}) %collective-permute-start.20) | collective-permute-done | bytes 129056 | tf_op jit(solution)/shard_map/ppermute | solution.py:25
  79.2 2.5 %collective-permute-done.21 = bf16[56,1152]{1,0:T(8,128)(2,1)S(1)} collective-permute-done((bf16[56,1152]{1,0:T(8,128)(2,1)S(1)}, bf16[56,1152]{1,0:T(8,128)(2,1)S(1)}, u32[]{:S(2)}, u32[]{:S(2)}) %collective-permute-start.21) | collective-permute-done | bytes 129056 | tf_op jit(solution)/shard_map/ppermute | solution.py:25
  81.9 0.1 fusion.50
  82.1 1.1 %collective-permute-done.24 = f32[8,1152]{1,0:T(8,128)S(1)} collective-permute-done((f32[8,1152]{1,0:T(8,128)S(1)}, f32[8,1152]{1,0:T(8,128)S(1)}, u32[]{:S(2)}, u32[]{:S(2)}) %collective-permute-start.24) | collective-permute-done | bytes 36896 | tf_op jit(solution)/shard_map/ppermute | solution.py:25
  83.1 1.1 %collective-permute-start.25 = (f32[16,1152]{1,0:T(8,128)S(1)}, f32[16,1152]{1,0:T(8,128)S(1)}, u32[]{:S(2)}, u32[]{:S(2)}) collective-permute-start(f32[16,1152]{1,0:T(8,128)S(1)} %maximum_select_fusion.1), channel_id=1, source_target_pairs={{0,16},{1,17},{2,18},{3,19},{4,20},{5,21},{6,22},{7,23},{8,24},{9,... | collective-permute-start | bytes 221192 | tf_op jit(solution)/shard_map/ppermute | solution.py:25
  84.3 0.7 slice.221
  85.0 2.6 %collective-permute-done.25 = f32[16,1152]{1,0:T(8,128)S(1)} collective-permute-done((f32[16,1152]{1,0:T(8,128)S(1)}, f32[16,1152]{1,0:T(8,128)S(1)}, u32[]{:S(2)}, u32[]{:S(2)}) %collective-permute-start.25) | collective-permute-done | bytes 73760 | tf_op jit(solution)/shard_map/ppermute | solution.py:25
  87.6 0.2 fusion.47
  87.8 0.8 fusion.49
  (91 shorter events, 2.9 us)
Async XLA Ops:
  2.3 12.8 %collective-permute-start.1 = (bf16[1,56,1152]{2,1,0:T(8,128)(2,1)S(1)}, bf16[1,56,1152]{2,1,0:T(8,128)(2,1)S(1)}, u32[]{:S(2)}, u32[]{:S(2)}) collective-permute-start(bf16[1,56,1152]{2,1,0:T(8,128)(2,1)S(1)} %maximum_bitcast_fusion), channel_id=1, source_target_pairs={{0,1},{1,0},{2,3},{3,2},{4,5},{5,4},{6,7},{7,6},{8,24},{9,25},{10,... | collective-permute-start | bytes 387080 | tf_op jit(solution)/shard_map/ppermute | solution.py:29
  5.3 22.1 %collective-permute-start.9 = (bf16[1,56,1152]{2,1,0:T(8,128)(2,1)S(1)}, bf16[1,56,1152]{2,1,0:T(8,128)(2,1)S(1)}, u32[]{:S(2)}, u32[]{:S(2)}) collective-permute-start(bf16[1,56,1152]{2,1,0:T(8,128)(2,1)S(1)} %maximum_bitcast_fusion), channel_id=1, source_target_pairs={{0,6},{1,7},{2,4},{3,5},{4,2},{5,3},{6,0},{7,1},{8,14},{9,15},{10,... | collective-permute-start | bytes 387080 | tf_op jit(solution)/shard_map/ppermute | solution.py:25
  8.9 7.8 %collective-permute-start.4 = (bf16[1,56,1152]{2,1,0:T(8,128)(2,1)S(1)}, bf16[1,56,1152]{2,1,0:T(8,128)(2,1)S(1)}, u32[]{:S(2)}, u32[]{:S(2)}) collective-permute-start(bf16[1,56,1152]{2,1,0:T(8,128)(2,1)S(1)} %maximum_bitcast_fusion), channel_id=1, source_target_pairs={{0,2},{1,3},{2,0},{3,1},{4,6},{5,7},{6,4},{7,5},{8,10},{9,11},{10,... | collective-permute-start | bytes 387080 | tf_op jit(solution)/shard_map/ppermute | solution.py:25
  8.9 10.6 %collective-permute-start.5 = (bf16[1,56,1152]{2,1,0:T(8,128)(2,1)S(1)}, bf16[1,56,1152]{2,1,0:T(8,128)(2,1)S(1)}, u32[]{:S(2)}, u32[]{:S(2)}) collective-permute-start(bf16[1,56,1152]{2,1,0:T(8,128)(2,1)S(1)} %maximum_bitcast_fusion), channel_id=1, source_target_pairs={{0,4},{1,5},{2,6},{3,7},{4,0},{5,1},{6,2},{7,3},{8,12},{9,13},{10,... | collective-permute-start | bytes 387080 | tf_op jit(solution)/shard_map/ppermute | solution.py:25
  14.7 11.9 %collective-permute-start = (bf16[768,256]{1,0:T(8,128)(2,1)S(1)}, bf16[768,256]{1,0:T(8,128)(2,1)S(1)}, u32[]{:S(2)}, u32[]{:S(2)}) collective-permute-start(bf16[768,256]{1,0:T(8,128)(2,1)S(1)} %pad_maximum_fusion.10), channel_id=1, source_target_pairs={{0,8},{1,9},{2,10},{3,11},{4,12},{5,13},{6,14},{7,15},{8,0},{9,1},... | collective-permute-start | bytes 1179656 | tf_op jit(solution)/shard_map/ppermute | solution.py:25
  15.1 6.5 %collective-permute-start.2 = (bf16[2,56,1152]{2,1,0:T(8,128)(2,1)S(1)}, bf16[2,56,1152]{2,1,0:T(8,128)(2,1)S(1)}, u32[]{:S(2)}, u32[]{:S(2)}) collective-permute-start(bf16[2,56,1152]{2,1,0:T(8,128)(2,1)S(1)} %pad_maximum_fusion.15), channel_id=1, source_target_pairs={{0,16},{1,17},{2,18},{3,19},{4,20},{5,21},{6,22},{7,23},{8,9},{9,8... | collective-permute-start | bytes 774152 | tf_op jit(solution)/shard_map/ppermute | solution.py:29
  19.6 6.4 %collective-permute-start.6 = (bf16[2,56,1152]{2,1,0:T(8,128)(2,1)S(1)}, bf16[2,56,1152]{2,1,0:T(8,128)(2,1)S(1)}, u32[]{:S(2)}, u32[]{:S(2)}) collective-permute-start(bf16[2,56,1152]{2,1,0:T(8,128)(2,1)S(1)} %pad_maximum_fusion.16), channel_id=1, source_target_pairs={{0,1},{1,0},{2,3},{3,2},{4,5},{5,4},{6,7},{7,6},{8,24},{9,25},{10,... | collective-permute-start | bytes 774152 | tf_op jit(solution)/shard_map/ppermute | solution.py:29
  21.7 5.0 %collective-permute-start.3 = (bf16[4,56,1152]{2,1,0:T(8,128)(2,1)S(1)}, bf16[4,56,1152]{2,1,0:T(8,128)(2,1)S(1)}, u32[]{:S(2)}, u32[]{:S(2)}) collective-permute-start(bf16[4,56,1152]{2,1,0:T(8,128)(2,1)S(1)} %pad_maximum_fusion.7), channel_id=1, source_target_pairs={{0,8},{1,9},{2,10},{3,11},{4,12},{5,13},{6,14},{7,15},{8,0},{9,1},... | collective-permute-start | bytes 1548296 | tf_op jit(solution)/shard_map/ppermute | solution.py:25
  26.0 10.5 %collective-permute-start.7 = (bf16[4,56,1152]{2,1,0:T(8,128)(2,1)S(1)}, bf16[4,56,1152]{2,1,0:T(8,128)(2,1)S(1)}, u32[]{:S(2)}, u32[]{:S(2)}) collective-permute-start(bf16[4,56,1152]{2,1,0:T(8,128)(2,1)S(1)} %pad_maximum_fusion.8), channel_id=1, source_target_pairs={{0,16},{1,17},{2,18},{3,19},{4,20},{5,21},{6,22},{7,23},{8,9},{9,8... | collective-permute-start | bytes 1548296 | tf_op jit(solution)/shard_map/ppermute | solution.py:29
  26.6 0.8 copy-start.1
  27.4 6.4 %collective-permute-start.10 = (bf16[1,56,1152]{2,1,0:T(8,128)(2,1)S(1)}, bf16[1,56,1152]{2,1,0:T(8,128)(2,1)S(1)}, u32[]{:S(2)}, u32[]{:S(2)}) collective-permute-start(bf16[1,56,1152]{2,1,0:T(8,128)(2,1)S(1)} %collective-permute-done.9), channel_id=1, source_target_pairs={{0,1},{1,0},{2,3},{3,2},{4,5},{5,4},{6,7},{7,6},{8,24},{9,25},{10,... | collective-permute-start | bytes 387080 | tf_op jit(solution)/shard_map/ppermute | solution.py:29
  33.8 6.4 %collective-permute-start.11 = (bf16[2,56,1152]{2,1,0:T(8,128)(2,1)S(1)}, bf16[2,56,1152]{2,1,0:T(8,128)(2,1)S(1)}, u32[]{:S(2)}, u32[]{:S(2)}) collective-permute-start(bf16[2,56,1152]{2,1,0:T(8,128)(2,1)S(1)} %pad_maximum_fusion.17), channel_id=1, source_target_pairs={{0,16},{1,17},{2,18},{3,19},{4,20},{5,21},{6,22},{7,23},{8,9},{9,8... | collective-permute-start | bytes 774152 | tf_op jit(solution)/shard_map/ppermute | solution.py:29
  36.6 5.7 %collective-permute-start.8 = (bf16[8,56,1152]{2,1,0:T(8,128)(2,1)S(1)}, bf16[8,56,1152]{2,1,0:T(8,128)(2,1)S(1)}, u32[]{:S(2)}, u32[]{:S(2)}) collective-permute-start(bf16[8,56,1152]{2,1,0:T(8,128)(2,1)S(1)} %pad_maximum_fusion.3), channel_id=1, source_target_pairs={{0,8},{1,9},{2,10},{3,11},{4,12},{5,13},{6,14},{7,15},{8,0},{9,1},... | collective-permute-start | bytes 3096584 | tf_op jit(solution)/shard_map/ppermute | solution.py:25
  40.3 2.0 %collective-permute-start.12 = (bf16[4,56,1152]{2,1,0:T(8,128)(2,1)S(1)}, bf16[4,56,1152]{2,1,0:T(8,128)(2,1)S(1)}, u32[]{:S(2)}, u32[]{:S(2)}) collective-permute-start(bf16[4,56,1152]{2,1,0:T(8,128)(2,1)S(1)} %pad_maximum_fusion.9), channel_id=1, source_target_pairs={{0,8},{1,9},{2,10},{3,11},{4,12},{5,13},{6,14},{7,15},{8,0},{9,1},... | collective-permute-start | bytes 1548296 | tf_op jit(solution)/shard_map/ppermute | solution.py:25
  44.0 0.7 copy-start.2
  46.4 2.6 %collective-permute-start.13 = (bf16[256,1152]{1,0:T(8,128)(2,1)S(1)}, bf16[256,1152]{1,0:T(8,128)(2,1)S(1)}, u32[]{:S(2)}, u32[]{:S(2)}) collective-permute-start(bf16[256,1152]{1,0:T(8,128)(2,1)S(1)} %multiply_convert_fusion), channel_id=1, source_target_pairs={{0,8},{1,9},{2,10},{3,11},{4,12},{5,13},{6,14},{7,15},{8,0},{9,1},... | collective-permute-start | bytes 1769480 | tf_op jit(solution)/shard_map/ppermute | solution.py:25
  46.6 2.3 %collective-permute-start.14 = (bf16[128,1152]{1,0:T(8,128)(2,1)S(1)}, bf16[128,1152]{1,0:T(8,128)(2,1)S(1)}, u32[]{:S(2)}, u32[]{:S(2)}) collective-permute-start(bf16[128,1152]{1,0:T(8,128)(2,1)S(1)} %pad_maximum_fusion.14), channel_id=1, source_target_pairs={{0,8},{1,9},{2,10},{3,11},{4,12},{5,13},{6,14},{7,15},{8,0},{9,1},... | collective-permute-start | bytes 884744 | tf_op jit(solution)/shard_map/ppermute | solution.py:25
  49.5 1.6 %slice-start = ((bf16[768,256]{1,0:T(8,128)(2,1)}), bf16[384,256]{1,0:T(8,128)(2,1)S(1)}, s32[]{:S(2)}) async-start(bf16[768,256]{1,0:T(8,128)(2,1)} %copy-done.1), calls=%async_computation | async-start | bytes 393216 | tf_op jit(solution)/shard_map/slice | solution.py:136
  49.5 6.4 %collective-permute-start.15 = (bf16[2,1,56,1152]{3,2,1,0:T(8,128)(2,1)S(1)}, bf16[2,1,56,1152]{3,2,1,0:T(8,128)(2,1)S(1)}, u32[]{:S(2)}, u32[]{:S(2)}) collective-permute-start(bf16[2,1,56,1152]{3,2,1,0:T(8,128)(2,1)S(1)} %fusion.26), channel_id=1, source_target_pairs={{0,16},{1,17},{2,18},{3,19},{4,20},{5,21},{6,22},{7,23},{8,9},{9,8... | collective-permute-start | bytes 774152 | tf_op jit(solution)/shard_map/ppermute | solution.py:29
  51.9 15.4 %collective-permute-start.18 = (bf16[2,2,56,1152]{3,2,1,0:T(8,128)(2,1)S(1)}, bf16[2,2,56,1152]{3,2,1,0:T(8,128)(2,1)S(1)}, u32[]{:S(2)}, u32[]{:S(2)}) collective-permute-start(bf16[2,2,56,1152]{3,2,1,0:T(8,128)(2,1)S(1)} %fusion.16), channel_id=1, source_target_pairs={{0,16},{1,17},{2,18},{3,19},{4,20},{5,21},{6,22},{7,23},{8,9},{9,8... | collective-permute-start | bytes 1548296 | tf_op jit(solution)/shard_map/ppermute | solution.py:29
  53.2 12.4 %collective-permute-start.22 = (bf16[2,1,56,1152]{3,2,1,0:T(8,128)(2,1)S(1)}, bf16[2,1,56,1152]{3,2,1,0:T(8,128)(2,1)S(1)}, u32[]{:S(2)}, u32[]{:S(2)}) collective-permute-start(bf16[2,1,56,1152]{3,2,1,0:T(8,128)(2,1)S(1)} %fusion.23), channel_id=1, source_target_pairs={{0,16},{1,17},{2,18},{3,19},{4,20},{5,21},{6,22},{7,23},{8,9},{9,8... | collective-permute-start | bytes 774152 | tf_op jit(solution)/shard_map/ppermute | solution.py:29
  56.0 12.0 %collective-permute-start.16 = (bf16[1,56,1152]{2,1,0:T(8,128)(2,1)S(1)}, bf16[1,56,1152]{2,1,0:T(8,128)(2,1)S(1)}, u32[]{:S(2)}, u32[]{:S(2)}) collective-permute-start(bf16[1,56,1152]{2,1,0:T(8,128)(2,1)S(1)} %fusion.52), channel_id=1, source_target_pairs={{0,1},{1,0},{2,3},{3,2},{4,5},{5,4},{6,7},{7,6},{8,24},{9,25},{10,... | collective-permute-start | bytes 387080 | tf_op jit(solution)/shard_map/ppermute | solution.py:29
  65.7 11.5 %collective-permute-start.23 = (bf16[1,56,1152]{2,1,0:T(8,128)(2,1)S(1)}, bf16[1,56,1152]{2,1,0:T(8,128)(2,1)S(1)}, u32[]{:S(2)}, u32[]{:S(2)}) collective-permute-start(bf16[1,56,1152]{2,1,0:T(8,128)(2,1)S(1)} %fusion.53), channel_id=1, source_target_pairs={{0,1},{1,0},{2,3},{3,2},{4,5},{5,4},{6,7},{7,6},{8,24},{9,25},{10,... | collective-permute-start | bytes 387080 | tf_op jit(solution)/shard_map/ppermute | solution.py:29
  67.4 6.4 %collective-permute-start.19 = (bf16[2,56,1152]{2,1,0:T(8,128)(2,1)S(1)}, bf16[2,56,1152]{2,1,0:T(8,128)(2,1)S(1)}, u32[]{:S(2)}, u32[]{:S(2)}) collective-permute-start(bf16[2,56,1152]{2,1,0:T(8,128)(2,1)S(1)} %fusion.33), channel_id=1, source_target_pairs={{0,1},{1,0},{2,3},{3,2},{4,5},{5,4},{6,7},{7,6},{8,24},{9,25},{10,... | collective-permute-start | bytes 774152 | tf_op jit(solution)/shard_map/ppermute | solution.py:29
  68.0 13.9 %copy-start = (bf16[32,1152]{1,0:T(8,128)(2,1)S(1)}, bf16[32,1152]{1,0:T(8,128)(2,1)}, u32[]{:S(2)}) copy-start(bf16[32,1152]{1,0:T(8,128)(2,1)} %param.12) | copy-start | bytes 221188
  68.0 9.2 %collective-permute-start.17 = (bf16[56,1152]{1,0:T(8,128)(2,1)S(1)}, bf16[56,1152]{1,0:T(8,128)(2,1)S(1)}, u32[]{:S(2)}, u32[]{:S(2)}) collective-permute-start(bf16[56,1152]{1,0:T(8,128)(2,1)S(1)} %fusion.51), channel_id=1, source_target_pairs={{0,6},{1,7},{2,4},{3,5},{4,2},{5,3},{6,0},{7,1},{8,14},{9,15},{10,... | collective-permute-start | bytes 387080 | tf_op jit(solution)/shard_map/ppermute | solution.py:25
  73.9 5.4 %collective-permute-start.20 = (bf16[56,1152]{1,0:T(8,128)(2,1)S(1)}, bf16[56,1152]{1,0:T(8,128)(2,1)S(1)}, u32[]{:S(2)}, u32[]{:S(2)}) collective-permute-start(bf16[56,1152]{1,0:T(8,128)(2,1)S(1)} %get-tuple-element.25), channel_id=1, source_target_pairs={{0,2},{1,3},{2,0},{3,1},{4,6},{5,7},{6,4},{7,5},{8,10},{9,11},{10,... | collective-permute-start | bytes 387080 | tf_op jit(solution)/shard_map/ppermute | solution.py:25
  74.2 7.5 %collective-permute-start.21 = (bf16[56,1152]{1,0:T(8,128)(2,1)S(1)}, bf16[56,1152]{1,0:T(8,128)(2,1)S(1)}, u32[]{:S(2)}, u32[]{:S(2)}) collective-permute-start(bf16[56,1152]{1,0:T(8,128)(2,1)S(1)} %get-tuple-element.26), channel_id=1, source_target_pairs={{0,4},{1,5},{2,6},{3,7},{4,0},{5,1},{6,2},{7,3},{8,12},{9,13},{10,... | collective-permute-start | bytes 387080 | tf_op jit(solution)/shard_map/ppermute | solution.py:25
  81.8 1.3 %collective-permute-start.24 = (f32[8,1152]{1,0:T(8,128)S(1)}, f32[8,1152]{1,0:T(8,128)S(1)}, u32[]{:S(2)}, u32[]{:S(2)}) collective-permute-start(f32[8,1152]{1,0:T(8,128)S(1)} %slice.222), channel_id=1, source_target_pairs={{0,8},{1,9},{2,10},{3,11},{4,12},{5,13},{6,14},{7,15},{8,0},{9,1},... | collective-permute-start | bytes 110600 | tf_op jit(solution)/shard_map/ppermute | solution.py:25
  83.1 4.4 %collective-permute-start.25 = (f32[16,1152]{1,0:T(8,128)S(1)}, f32[16,1152]{1,0:T(8,128)S(1)}, u32[]{:S(2)}, u32[]{:S(2)}) collective-permute-start(f32[16,1152]{1,0:T(8,128)S(1)} %maximum_select_fusion.1), channel_id=1, source_target_pairs={{0,16},{1,17},{2,18},{3,19},{4,20},{5,21},{6,22},{7,23},{8,24},{9,... | collective-permute-start | bytes 221192 | tf_op jit(solution)/shard_map/ppermute | solution.py:25

commit v3 on v2

--- a/solution.py
+++ b/solution.py
@@ -61,16 +61,15 @@
         )[None]
         by_z = [own] + [None] * (depth - 1)
         for kz in range(1, depth):
-            by_z[kz] = swap(own, 2 * kz)
+            by_z[kz] = swap(by_z[kz - 1], 2) if kz % 2 and kz > 1 else swap(own, 2 * kz)
         gathered = []
-        last = None
-        for chunk in chunks:
+        firsts, seconds = [], []
+        for i, chunk in enumerate(chunks):
             block = jnp.concatenate([by_z[kz] for kz in chunk], axis=0)
-            if last is not None and chunk is chunks[-1]:
-                block, _ = lax.optimization_barrier((block, gathered[0]))
-            pair = jnp.concatenate([block, first(block)], axis=0)
-            quad = jnp.concatenate([pair, second(pair)], axis=0)
-            last = quad
+            firsts.append(first(block))
+            pair = jnp.concatenate([block, firsts[i]], axis=0)
+            seconds.append(second(pair))
+            quad = jnp.concatenate([pair, seconds[i]], axis=0)
             gathered.append(jnp.concatenate([quad, swap(quad, core_mask)], axis=0))
 
         turned = pooled.T.reshape(devices, rows, images)
@@ -129,6 +128,7 @@
         text_at = [4 * quarter * sum(len(c) for c in chunks[:i]) for i in range(len(chunks))]
         row_at = [4 * rows * sum(len(c) for c in chunks[:i]) for i in range(len(chunks))]
         total = None
+        keeps, keepf, pieces = {}, {}, {}
         for i in (2, 1, 0):
             chunk = chunks[i]
             count = len(chunk)
@@ -144,13 +144,18 @@
                 ],
                 axis=2,
             )
-            part = part[:2] + second(part[2:].astype(jnp.bfloat16)).astype(jnp.float32)
-            part = part[0] + first(part[1].astype(jnp.bfloat16)).astype(jnp.float32)
+            away = part[2:].astype(jnp.bfloat16)
+            keeps[i] = second(away)
+            part = part[:2] + keeps[i].astype(jnp.float32)
+            keepf[i] = first(part[1].astype(jnp.bfloat16))
+            part = part[0] + keepf[i].astype(jnp.float32)
             for k, kz in enumerate(chunk):
-                piece = part[k]
-                if kz:
-                    piece = swap(piece.astype(jnp.bfloat16), 2 * kz).astype(jnp.float32)
-                total = piece if total is None else total + piece
+                pieces[kz] = part[k]
+        for kz in range(3, depth, 2):
+            pieces[kz - 1] += swap(pieces[kz].astype(jnp.bfloat16), 2).astype(jnp.float32)
+        total = pieces[0]
+        for kz in [1] + list(range(2, depth, 2)):
+            total += swap(pieces[kz].astype(jnp.bfloat16), 2 * kz).astype(jnp.float32)
         grad_weight = total[:rows]
 
         def joined(array, mask, position):

time: 88.8 us -> 85.2 us (0.959)
  starting transfers between devices: 30.1 us -> 25.2 us
  waiting for transfers between devices: 40.9 us -> 42.7 us
    ppermute x12, starting transfers between devices: 17.2 us -> 13.6 us  [swap_by_core(): return lax.ppermute(array, axes, pairs)]
    ppermute x14, waiting for transfers between devices: 14.6 us -> 17.7 us  [swap(): return lax.ppermute(array, axes, [(i, i ^ mask) for i in range(devices)])]
    ppermute x14, starting transfers between devices: 12.9 us -> 11.6 us  [swap(): return lax.ppermute(array, axes, [(i, i ^ mask) for i in range(devices)])]
    ppermute x12, waiting for transfers between devices: 26.2 us -> 25 us  [swap_by_core(): return lax.ppermute(array, axes, pairs)]
  transfers between devices with their start and end apart: 26 -> 26, of which waited for: 15 -> 12; matrix products, arithmetic and copies ran while one was open for 10% -> 10% of each run, Pallas kernels for 0% -> 0%
where the time goes in v3:
time: 85.2 us; the launch traced here: 84.9 us
  waiting for transfers between devices  42.7 us (50%)
  starting transfers between devices  25.2 us (30%)
  local copies, waits for them, and re-layouts  5.78 us (7%)
  other arithmetic  5.14 us (6%)
  matrix products  4.85 us (6%)
  between operations  1.21 us (1%)
    ppermute x12, waiting for transfers between devices, swap_by_core(): return lax.ppermute(array, axes, pairs)  25 us
    ppermute x14, waiting for transfers between devices, swap(): return lax.ppermute(array, axes, [(i, i ^ mask) for i in range(devices)])  17.7 us
    ppermute x12, starting transfers between devices, swap_by_core(): return lax.ppermute(array, axes, pairs)  13.6 us
    ppermute x14, starting transfers between devices, swap(): return lax.ppermute(array, axes, [(i, i ^ mask) for i in range(devices)])  11.6 us
    dot_general x3, matrix products, shards(): lax.dot_general(c.reshape(-1, images), g[:, :rows].reshape(-1, embed), ((...  1.85 us
  transfers between devices with their start and end apart: 26, of which 12 were waited for; matrix products, arithmetic and copies ran while one was open for 10% of the time, Pallas kernels for 0%

profile of v3, /device:TPU:0, one launch (start us, length us, event | category | flops | bytes accessed | tf_op | source)
XLA Modules:
  0.0 84.9 jit_solution(10800175056783408)
XLA Ops:
  0.6 0.7 constant_dynamic-slice_fusion
  1.4 0.9 %maximum_bitcast_fusion.1 = bf16[1,56,1152]{2,1,0:T(8,128)(2,1)S(1)} fusion(bf16[8,1152]{1,0:T(8,128)(2,1)S(1)} %constant_dynamic-slice_fusion, bf16[48,1152]{1,0:T(8,128)(2,1)} %param.10), kind=kLoop, calls=%fused_computation.111 | loop fusion | flops 258048 | bytes 258048 | tf_op jit(solution)/shard_map/broadcast_in_dim | solution.py:59
  2.3 4.1 %collective-permute-start.5 = (bf16[1,56,1152]{2,1,0:T(8,128)(2,1)S(1)}, bf16[1,56,1152]{2,1,0:T(8,128)(2,1)S(1)}, u32[]{:S(2)}, u32[]{:S(2)}) collective-permute-start(bf16[1,56,1152]{2,1,0:T(8,128)(2,1)S(1)} %maximum_bitcast_fusion.1), channel_id=1, source_target_pairs={{0,4},{1,5},{2,6},{3,7},{4,0},{5,1},{6,2},{7,3},{8,12},{9,13},{10,... | collective-permute-start | bytes 387080 | tf_op jit(solution)/shard_map/ppermute | solution.py:25
  6.4 1.6 %collective-permute-start.4 = (bf16[1,56,1152]{2,1,0:T(8,128)(2,1)S(1)}, bf16[1,56,1152]{2,1,0:T(8,128)(2,1)S(1)}, u32[]{:S(2)}, u32[]{:S(2)}) collective-permute-start(bf16[1,56,1152]{2,1,0:T(8,128)(2,1)S(1)} %maximum_bitcast_fusion.1), channel_id=1, source_target_pairs={{0,2},{1,3},{2,0},{3,1},{4,6},{5,7},{6,4},{7,5},{8,10},{9,11},{10,... | collective-permute-start | bytes 387080 | tf_op jit(solution)/shard_map/ppermute | solution.py:25
  8.0 1.5 %collective-permute-start.1 = (bf16[1,56,1152]{2,1,0:T(8,128)(2,1)S(1)}, bf16[1,56,1152]{2,1,0:T(8,128)(2,1)S(1)}, u32[]{:S(2)}, u32[]{:S(2)}) collective-permute-start(bf16[1,56,1152]{2,1,0:T(8,128)(2,1)S(1)} %maximum_bitcast_fusion.1), channel_id=1, source_target_pairs={{0,1},{1,0},{2,3},{3,2},{4,5},{5,4},{6,7},{7,6},{8,24},{9,25},{10,... | collective-permute-start | bytes 387080 | tf_op jit(solution)/shard_map/ppermute | solution.py:29
  9.5 0.7 broadcast_xor_fusion
  10.7 1.4 %copy.13 = bf16[256,1536]{0,1:T(8,128)(2,1)S(1)} copy(bf16[256,1536]{1,0:T(8,128)(2,1)} %param.9) | data formatting | bytes 1572864 | tf_op args[0]
  12.2 0.6 gather_fusion
  12.8 0.6 gather_fusion.1
  13.4 0.6 gather_fusion.2
  14.0 0.1 broadcast_select_fusion.1
  14.1 0.1 broadcast_select_fusion.2
  14.3 0.1 broadcast_select_fusion
  14.8 0.1 add.156
  14.9 0.6 collective-permute-start.6
  15.5 1.6 %collective-permute-start.2 = (bf16[2,56,1152]{2,1,0:T(8,128)(2,1)S(1)}, bf16[2,56,1152]{2,1,0:T(8,128)(2,1)S(1)}, u32[]{:S(2)}, u32[]{:S(2)}) collective-permute-start(bf16[2,56,1152]{2,1,0:T(8,128)(2,1)S(1)} %pad_maximum_fusion.15), channel_id=1, source_target_pairs={{0,16},{1,17},{2,18},{3,19},{4,20},{5,21},{6,22},{7,23},{8,9},{9,8... | collective-permute-start | bytes 774152 | tf_op jit(solution)/shard_map/ppermute | solution.py:29
  17.1 0.5 collective-permute-start.9
  17.7 4.8 %collective-permute-done.9 = bf16[1,56,1152]{2,1,0:T(8,128)(2,1)S(1)} collective-permute-done((bf16[1,56,1152]{2,1,0:T(8,128)(2,1)S(1)}, bf16[1,56,1152]{2,1,0:T(8,128)(2,1)S(1)}, u32[]{:S(2)}, u32[]{:S(2)}) %collective-permute-start.9) | collective-permute-done | bytes 129056 | tf_op jit(solution)/shard_map/ppermute | solution.py:25
  22.5 1.5 %collective-permute-start.10 = (bf16[1,56,1152]{2,1,0:T(8,128)(2,1)S(1)}, bf16[1,56,1152]{2,1,0:T(8,128)(2,1)S(1)}, u32[]{:S(2)}, u32[]{:S(2)}) collective-permute-start(bf16[1,56,1152]{2,1,0:T(8,128)(2,1)S(1)} %collective-permute-done.9), channel_id=1, source_target_pairs={{0,1},{1,0},{2,3},{3,2},{4,5},{5,4},{6,7},{7,6},{8,24},{9,25},{10,... | collective-permute-start | bytes 387080 | tf_op jit(solution)/shard_map/ppermute | solution.py:29
  24.1 1.5 %collective-permute-start.7 = (bf16[4,56,1152]{2,1,0:T(8,128)(2,1)S(1)}, bf16[4,56,1152]{2,1,0:T(8,128)(2,1)S(1)}, u32[]{:S(2)}, u32[]{:S(2)}) collective-permute-start(bf16[4,56,1152]{2,1,0:T(8,128)(2,1)S(1)} %pad_maximum_fusion.8), channel_id=1, source_target_pairs={{0,16},{1,17},{2,18},{3,19},{4,20},{5,21},{6,22},{7,23},{8,9},{9,8... | collective-permute-start | bytes 1548296 | tf_op jit(solution)/shard_map/ppermute | solution.py:29
  25.6 3.2 %collective-permute-done.10 = bf16[1,56,1152]{2,1,0:T(8,128)(2,1)S(1)} collective-permute-done((bf16[1,56,1152]{2,1,0:T(8,128)(2,1)S(1)}, bf16[1,56,1152]{2,1,0:T(8,128)(2,1)S(1)}, u32[]{:S(2)}, u32[]{:S(2)}) %collective-permute-start.10) | collective-permute-done | bytes 129056 | tf_op jit(solution)/shard_map/ppermute | solution.py:29
  28.8 0.4 collective-permute-start.11
  29.4 6.6 %collective-permute-done.11 = bf16[2,56,1152]{2,1,0:T(8,128)(2,1)S(1)} collective-permute-done((bf16[2,56,1152]{2,1,0:T(8,128)(2,1)S(1)}, bf16[2,56,1152]{2,1,0:T(8,128)(2,1)S(1)}, u32[]{:S(2)}, u32[]{:S(2)}) %collective-permute-start.11) | collective-permute-done | bytes 258080 | tf_op jit(solution)/shard_map/ppermute | solution.py:29
  36.2 0.1 pad_maximum_fusion.3
  36.4 0.6 collective-permute-start.8
  37.0 0.1 pad_maximum_fusion.2
  37.1 0.9 %collective-permute-done.12 = bf16[4,56,1152]{2,1,0:T(8,128)(2,1)S(1)} collective-permute-done((bf16[4,56,1152]{2,1,0:T(8,128)(2,1)S(1)}, bf16[4,56,1152]{2,1,0:T(8,128)(2,1)S(1)}, u32[]{:S(2)}, u32[]{:S(2)}) %collective-permute-start.12) | collective-permute-done | bytes 516128 | tf_op jit(solution)/shard_map/ppermute | solution.py:25
  38.1 1.4 %collective-permute-done.8 = bf16[8,56,1152]{2,1,0:T(8,128)(2,1)S(1)} collective-permute-done((bf16[8,56,1152]{2,1,0:T(8,128)(2,1)S(1)}, bf16[8,56,1152]{2,1,0:T(8,128)(2,1)S(1)}, u32[]{:S(2)}, u32[]{:S(2)}) %collective-permute-start.8) | collective-permute-done | bytes 1032224 | tf_op jit(solution)/shard_map/ppermute | solution.py:25
  39.5 0.1 constant_dynamic-update-slice_fusion
  39.7 0.7 convolution_bitcast_fusion.1
  40.4 0.2 fusion.3
  40.6 0.5 fusion.1
  41.2 0.6 multiply_reduce_fusion.1
  41.8 0.5 fusion.13
  42.4 0.5 multiply_reduce_fusion
  42.9 0.4 fusion.79
  43.4 0.2 multiply_convert_fusion
  43.6 0.2 collective-permute-start.13
  43.8 0.4 collective-permute-start.14
  44.3 1.8 %collective-permute-done.14 = bf16[128,1152]{1,0:T(8,128)(2,1)S(1)} collective-permute-done((bf16[128,1152]{1,0:T(8,128)(2,1)S(1)}, bf16[128,1152]{1,0:T(8,128)(2,1)S(1)}, u32[]{:S(2)}, u32[]{:S(2)}) %collective-permute-start.14) | collective-permute-done | bytes 294944 | tf_op jit(solution)/shard_map/ppermute | solution.py:25
  46.2 0.4 fusion.30
  46.7 1.5 %collective-permute-start.20 = (bf16[2,1,56,1152]{3,2,1,0:T(8,128)(2,1)S(1)}, bf16[2,1,56,1152]{3,2,1,0:T(8,128)(2,1)S(1)}, u32[]{:S(2)}, u32[]{:S(2)}) collective-permute-start(bf16[2,1,56,1152]{3,2,1,0:T(8,128)(2,1)S(1)} %fusion.23), channel_id=1, source_target_pairs={{0,16},{1,17},{2,18},{3,19},{4,20},{5,21},{6,22},{7,23},{8,9},{9,8... | collective-permute-start | bytes 774152 | tf_op jit(solution)/shard_map/ppermute | solution.py:29
  48.2 0.7 fusion.26
  48.9 0.9 %collective-permute-start.17 = (bf16[2,2,56,1152]{3,2,1,0:T(8,128)(2,1)S(1)}, bf16[2,2,56,1152]{3,2,1,0:T(8,128)(2,1)S(1)}, u32[]{:S(2)}, u32[]{:S(2)}) collective-permute-start(bf16[2,2,56,1152]{3,2,1,0:T(8,128)(2,1)S(1)} %fusion.16), channel_id=1, source_target_pairs={{0,16},{1,17},{2,18},{3,19},{4,20},{5,21},{6,22},{7,23},{8,9},{9,8... | collective-permute-start | bytes 1548296 | tf_op jit(solution)/shard_map/ppermute | solution.py:29
  49.8 0.4 fusion.31
  50.3 1.3 %collective-permute-start.15 = (bf16[2,1,56,1152]{3,2,1,0:T(8,128)(2,1)S(1)}, bf16[2,1,56,1152]{3,2,1,0:T(8,128)(2,1)S(1)}, u32[]{:S(2)}, u32[]{:S(2)}) collective-permute-start(bf16[2,1,56,1152]{3,2,1,0:T(8,128)(2,1)S(1)} %fusion.25), channel_id=1, source_target_pairs={{0,16},{1,17},{2,18},{3,19},{4,20},{5,21},{6,22},{7,23},{8,9},{9,8... | collective-permute-start | bytes 774152 | tf_op jit(solution)/shard_map/ppermute | solution.py:29
  51.6 1.5 %collective-permute-done.20 = bf16[2,1,56,1152]{3,2,1,0:T(8,128)(2,1)S(1)} collective-permute-done((bf16[2,1,56,1152]{3,2,1,0:T(8,128)(2,1)S(1)}, bf16[2,1,56,1152]{3,2,1,0:T(8,128)(2,1)S(1)}, u32[]{:S(2)}, u32[]{:S(2)}) %collective-permute-start.20) | collective-permute-done | bytes 258080 | tf_op jit(solution)/shard_map/ppermute | solution.py:29
  53.2 0.8 collective-permute-start.21
  54.0 8.7 %collective-permute-done.15 = bf16[2,1,56,1152]{3,2,1,0:T(8,128)(2,1)S(1)} collective-permute-done((bf16[2,1,56,1152]{3,2,1,0:T(8,128)(2,1)S(1)}, bf16[2,1,56,1152]{3,2,1,0:T(8,128)(2,1)S(1)}, u32[]{:S(2)}, u32[]{:S(2)}) %collective-permute-start.15) | collective-permute-done | bytes 258080 | tf_op jit(solution)/shard_map/ppermute | solution.py:29
  62.9 0.8 collective-permute-start.16
  63.7 0.1 fusion.15
  63.8 1.3 %collective-permute-start.18 = (bf16[2,56,1152]{2,1,0:T(8,128)(2,1)S(1)}, bf16[2,56,1152]{2,1,0:T(8,128)(2,1)S(1)}, u32[]{:S(2)}, u32[]{:S(2)}) collective-permute-start(bf16[2,56,1152]{2,1,0:T(8,128)(2,1)S(1)} %fusion.32), channel_id=1, source_target_pairs={{0,1},{1,0},{2,3},{3,2},{4,5},{5,4},{6,7},{7,6},{8,24},{9,25},{10,... | collective-permute-start | bytes 774152 | tf_op jit(solution)/shard_map/ppermute | solution.py:29
  65.2 0.5 collective-permute-start.22
  65.7 4.9 %collective-permute-done.18 = bf16[2,56,1152]{2,1,0:T(8,128)(2,1)S(1)} collective-permute-done((bf16[2,56,1152]{2,1,0:T(8,128)(2,1)S(1)}, bf16[2,56,1152]{2,1,0:T(8,128)(2,1)S(1)}, u32[]{:S(2)}, u32[]{:S(2)}) %collective-permute-start.18) | collective-permute-done | bytes 258080 | tf_op jit(solution)/shard_map/ppermute | solution.py:29
  70.8 0.4 collective-permute-start.23
  71.2 1.5 %collective-permute-start.19 = (bf16[56,1152]{1,0:T(8,128)(2,1)S(1)}, bf16[56,1152]{1,0:T(8,128)(2,1)S(1)}, u32[]{:S(2)}, u32[]{:S(2)}) collective-permute-start(bf16[56,1152]{1,0:T(8,128)(2,1)S(1)} %fusion.54), channel_id=1, source_target_pairs={{0,2},{1,3},{2,0},{3,1},{4,6},{5,7},{6,4},{7,5},{8,10},{9,11},{10,... | collective-permute-start | bytes 387080 | tf_op jit(solution)/shard_map/ppermute | solution.py:25
  72.7 5.5 %collective-permute-done.23 = bf16[56,1152]{1,0:T(8,128)(2,1)S(1)} collective-permute-done((bf16[56,1152]{1,0:T(8,128)(2,1)S(1)}, bf16[56,1152]{1,0:T(8,128)(2,1)S(1)}, u32[]{:S(2)}, u32[]{:S(2)}) %collective-permute-start.23) | collective-permute-done | bytes 129056 | tf_op jit(solution)/shard_map/ppermute | solution.py:25
  78.3 0.1 fusion.52
  78.5 1.1 %collective-permute-done.24 = f32[8,1152]{1,0:T(8,128)S(1)} collective-permute-done((f32[8,1152]{1,0:T(8,128)S(1)}, f32[8,1152]{1,0:T(8,128)S(1)}, u32[]{:S(2)}, u32[]{:S(2)}) %collective-permute-start.24) | collective-permute-done | bytes 36896 | tf_op jit(solution)/shard_map/ppermute | solution.py:25
  79.5 1.5 %collective-permute-start.25 = (f32[16,1152]{1,0:T(8,128)S(1)}, f32[16,1152]{1,0:T(8,128)S(1)}, u32[]{:S(2)}, u32[]{:S(2)}) collective-permute-start(f32[16,1152]{1,0:T(8,128)S(1)} %maximum_select_fusion.1), channel_id=1, source_target_pairs={{0,16},{1,17},{2,18},{3,19},{4,20},{5,21},{6,22},{7,23},{8,24},{9,... | collective-permute-start | bytes 221192 | tf_op jit(solution)/shard_map/ppermute | solution.py:25
  81.0 0.7 slice.219
  81.7 2.2 %collective-permute-done.25 = f32[16,1152]{1,0:T(8,128)S(1)} collective-permute-done((f32[16,1152]{1,0:T(8,128)S(1)}, f32[16,1152]{1,0:T(8,128)S(1)}, u32[]{:S(2)}, u32[]{:S(2)}) %collective-permute-start.25) | collective-permute-done | bytes 73760 | tf_op jit(solution)/shard_map/ppermute | solution.py:25
  84.0 0.2 fusion.49
  84.2 0.8 fusion.51
  (92 shorter events, 2.7 us)
Async XLA Ops:
  2.3 12.6 %collective-permute-start.5 = (bf16[1,56,1152]{2,1,0:T(8,128)(2,1)S(1)}, bf16[1,56,1152]{2,1,0:T(8,128)(2,1)S(1)}, u32[]{:S(2)}, u32[]{:S(2)}) collective-permute-start(bf16[1,56,1152]{2,1,0:T(8,128)(2,1)S(1)} %maximum_bitcast_fusion.1), channel_id=1, source_target_pairs={{0,4},{1,5},{2,6},{3,7},{4,0},{5,1},{6,2},{7,3},{8,12},{9,13},{10,... | collective-permute-start | bytes 387080 | tf_op jit(solution)/shard_map/ppermute | solution.py:25
  6.4 8.5 %collective-permute-start.4 = (bf16[1,56,1152]{2,1,0:T(8,128)(2,1)S(1)}, bf16[1,56,1152]{2,1,0:T(8,128)(2,1)S(1)}, u32[]{:S(2)}, u32[]{:S(2)}) collective-permute-start(bf16[1,56,1152]{2,1,0:T(8,128)(2,1)S(1)} %maximum_bitcast_fusion.1), channel_id=1, source_target_pairs={{0,2},{1,3},{2,0},{3,1},{4,6},{5,7},{6,4},{7,5},{8,10},{9,11},{10,... | collective-permute-start | bytes 387080 | tf_op jit(solution)/shard_map/ppermute | solution.py:25
  8.0 7.6 %collective-permute-start.1 = (bf16[1,56,1152]{2,1,0:T(8,128)(2,1)S(1)}, bf16[1,56,1152]{2,1,0:T(8,128)(2,1)S(1)}, u32[]{:S(2)}, u32[]{:S(2)}) collective-permute-start(bf16[1,56,1152]{2,1,0:T(8,128)(2,1)S(1)} %maximum_bitcast_fusion.1), channel_id=1, source_target_pairs={{0,1},{1,0},{2,3},{3,2},{4,5},{5,4},{6,7},{7,6},{8,24},{9,25},{10,... | collective-permute-start | bytes 387080 | tf_op jit(solution)/shard_map/ppermute | solution.py:29
  14.5 14.9 %collective-permute-start = (bf16[768,256]{1,0:T(8,128)(2,1)S(1)}, bf16[768,256]{1,0:T(8,128)(2,1)S(1)}, u32[]{:S(2)}, u32[]{:S(2)}) collective-permute-start(bf16[768,256]{1,0:T(8,128)(2,1)S(1)} %pad_maximum_fusion.10), channel_id=1, source_target_pairs={{0,8},{1,9},{2,10},{3,11},{4,12},{5,13},{6,14},{7,15},{8,0},{9,1},... | collective-permute-start | bytes 1179656 | tf_op jit(solution)/shard_map/ppermute | solution.py:25
  14.9 9.1 %collective-permute-start.6 = (bf16[2,56,1152]{2,1,0:T(8,128)(2,1)S(1)}, bf16[2,56,1152]{2,1,0:T(8,128)(2,1)S(1)}, u32[]{:S(2)}, u32[]{:S(2)}) collective-permute-start(bf16[2,56,1152]{2,1,0:T(8,128)(2,1)S(1)} %pad_maximum_fusion.16), channel_id=1, source_target_pairs={{0,1},{1,0},{2,3},{3,2},{4,5},{5,4},{6,7},{7,6},{8,24},{9,25},{10,... | collective-permute-start | bytes 774152 | tf_op jit(solution)/shard_map/ppermute | solution.py:29
  15.5 13.6 %collective-permute-start.2 = (bf16[2,56,1152]{2,1,0:T(8,128)(2,1)S(1)}, bf16[2,56,1152]{2,1,0:T(8,128)(2,1)S(1)}, u32[]{:S(2)}, u32[]{:S(2)}) collective-permute-start(bf16[2,56,1152]{2,1,0:T(8,128)(2,1)S(1)} %pad_maximum_fusion.15), channel_id=1, source_target_pairs={{0,16},{1,17},{2,18},{3,19},{4,20},{5,21},{6,22},{7,23},{8,9},{9,8... | collective-permute-start | bytes 774152 | tf_op jit(solution)/shard_map/ppermute | solution.py:29
  17.1 5.4 %collective-permute-start.9 = (bf16[1,56,1152]{2,1,0:T(8,128)(2,1)S(1)}, bf16[1,56,1152]{2,1,0:T(8,128)(2,1)S(1)}, u32[]{:S(2)}, u32[]{:S(2)}) collective-permute-start(bf16[1,56,1152]{2,1,0:T(8,128)(2,1)S(1)} %collective-permute-done.5), channel_id=1, source_target_pairs={{0,2},{1,3},{2,0},{3,1},{4,6},{5,7},{6,4},{7,5},{8,10},{9,11},{10,... | collective-permute-start | bytes 387080 | tf_op jit(solution)/shard_map/ppermute | solution.py:25
  22.5 6.3 %collective-permute-start.10 = (bf16[1,56,1152]{2,1,0:T(8,128)(2,1)S(1)}, bf16[1,56,1152]{2,1,0:T(8,128)(2,1)S(1)}, u32[]{:S(2)}, u32[]{:S(2)}) collective-permute-start(bf16[1,56,1152]{2,1,0:T(8,128)(2,1)S(1)} %collective-permute-done.9), channel_id=1, source_target_pairs={{0,1},{1,0},{2,3},{3,2},{4,5},{5,4},{6,7},{7,6},{8,24},{9,25},{10,... | collective-permute-start | bytes 387080 | tf_op jit(solution)/shard_map/ppermute | solution.py:29
  24.1 12.1 %collective-permute-start.7 = (bf16[4,56,1152]{2,1,0:T(8,128)(2,1)S(1)}, bf16[4,56,1152]{2,1,0:T(8,128)(2,1)S(1)}, u32[]{:S(2)}, u32[]{:S(2)}) collective-permute-start(bf16[4,56,1152]{2,1,0:T(8,128)(2,1)S(1)} %pad_maximum_fusion.8), channel_id=1, source_target_pairs={{0,16},{1,17},{2,18},{3,19},{4,20},{5,21},{6,22},{7,23},{8,9},{9,8... | collective-permute-start | bytes 1548296 | tf_op jit(solution)/shard_map/ppermute | solution.py:29
  28.8 7.2 %collective-permute-start.11 = (bf16[2,56,1152]{2,1,0:T(8,128)(2,1)S(1)}, bf16[2,56,1152]{2,1,0:T(8,128)(2,1)S(1)}, u32[]{:S(2)}, u32[]{:S(2)}) collective-permute-start(bf16[2,56,1152]{2,1,0:T(8,128)(2,1)S(1)} %pad_maximum_fusion.17), channel_id=1, source_target_pairs={{0,16},{1,17},{2,18},{3,19},{4,20},{5,21},{6,22},{7,23},{8,9},{9,8... | collective-permute-start | bytes 774152 | tf_op jit(solution)/shard_map/ppermute | solution.py:29
  29.2 7.7 %collective-permute-start.3 = (bf16[4,56,1152]{2,1,0:T(8,128)(2,1)S(1)}, bf16[4,56,1152]{2,1,0:T(8,128)(2,1)S(1)}, u32[]{:S(2)}, u32[]{:S(2)}) collective-permute-start(bf16[4,56,1152]{2,1,0:T(8,128)(2,1)S(1)} %pad_maximum_fusion.7), channel_id=1, source_target_pairs={{0,8},{1,9},{2,10},{3,11},{4,12},{5,13},{6,14},{7,15},{8,0},{9,1},... | collective-permute-start | bytes 1548296 | tf_op jit(solution)/shard_map/ppermute | solution.py:25
  29.4 7.0 %copy-start.1 = (bf16[768,256]{1,0:T(8,128)(2,1)}, bf16[768,256]{1,0:T(8,128)(2,1)S(1)}, u32[]{:S(2)}) copy-start(bf16[768,256]{1,0:T(8,128)(2,1)S(1)} %collective-permute-done) | copy-start | bytes 1179652
  36.1 2.0 %collective-permute-start.12 = (bf16[4,56,1152]{2,1,0:T(8,128)(2,1)S(1)}, bf16[4,56,1152]{2,1,0:T(8,128)(2,1)S(1)}, u32[]{:S(2)}, u32[]{:S(2)}) collective-permute-start(bf16[4,56,1152]{2,1,0:T(8,128)(2,1)S(1)} %pad_maximum_fusion.9), channel_id=1, source_target_pairs={{0,8},{1,9},{2,10},{3,11},{4,12},{5,13},{6,14},{7,15},{8,0},{9,1},... | collective-permute-start | bytes 1548296 | tf_op jit(solution)/shard_map/ppermute | solution.py:25
  36.4 3.2 %collective-permute-start.8 = (bf16[8,56,1152]{2,1,0:T(8,128)(2,1)S(1)}, bf16[8,56,1152]{2,1,0:T(8,128)(2,1)S(1)}, u32[]{:S(2)}, u32[]{:S(2)}) collective-permute-start(bf16[8,56,1152]{2,1,0:T(8,128)(2,1)S(1)} %pad_maximum_fusion.3), channel_id=1, source_target_pairs={{0,8},{1,9},{2,10},{3,11},{4,12},{5,13},{6,14},{7,15},{8,0},{9,1},... | collective-permute-start | bytes 3096584 | tf_op jit(solution)/shard_map/ppermute | solution.py:25
  41.2 0.7 copy-start.2
  43.6 2.6 %collective-permute-start.13 = (bf16[256,1152]{1,0:T(8,128)(2,1)S(1)}, bf16[256,1152]{1,0:T(8,128)(2,1)S(1)}, u32[]{:S(2)}, u32[]{:S(2)}) collective-permute-start(bf16[256,1152]{1,0:T(8,128)(2,1)S(1)} %multiply_convert_fusion), channel_id=1, source_target_pairs={{0,8},{1,9},{2,10},{3,11},{4,12},{5,13},{6,14},{7,15},{8,0},{9,1},... | collective-permute-start | bytes 1769480 | tf_op jit(solution)/shard_map/ppermute | solution.py:25
  43.8 2.3 %collective-permute-start.14 = (bf16[128,1152]{1,0:T(8,128)(2,1)S(1)}, bf16[128,1152]{1,0:T(8,128)(2,1)S(1)}, u32[]{:S(2)}, u32[]{:S(2)}) collective-permute-start(bf16[128,1152]{1,0:T(8,128)(2,1)S(1)} %pad_maximum_fusion.14), channel_id=1, source_target_pairs={{0,8},{1,9},{2,10},{3,11},{4,12},{5,13},{6,14},{7,15},{8,0},{9,1},... | collective-permute-start | bytes 884744 | tf_op jit(solution)/shard_map/ppermute | solution.py:25
  46.7 1.5 %slice-start = ((bf16[768,256]{1,0:T(8,128)(2,1)}), bf16[384,256]{1,0:T(8,128)(2,1)S(1)}, s32[]{:S(2)}) async-start(bf16[768,256]{1,0:T(8,128)(2,1)} %copy-done.1), calls=%async_computation | async-start | bytes 393216 | tf_op jit(solution)/shard_map/slice | solution.py:136
  46.7 6.4 %collective-permute-start.20 = (bf16[2,1,56,1152]{3,2,1,0:T(8,128)(2,1)S(1)}, bf16[2,1,56,1152]{3,2,1,0:T(8,128)(2,1)S(1)}, u32[]{:S(2)}, u32[]{:S(2)}) collective-permute-start(bf16[2,1,56,1152]{3,2,1,0:T(8,128)(2,1)S(1)} %fusion.23), channel_id=1, source_target_pairs={{0,16},{1,17},{2,18},{3,19},{4,20},{5,21},{6,22},{7,23},{8,9},{9,8... | collective-permute-start | bytes 774152 | tf_op jit(solution)/shard_map/ppermute | solution.py:29
  48.9 14.8 %collective-permute-start.17 = (bf16[2,2,56,1152]{3,2,1,0:T(8,128)(2,1)S(1)}, bf16[2,2,56,1152]{3,2,1,0:T(8,128)(2,1)S(1)}, u32[]{:S(2)}, u32[]{:S(2)}) collective-permute-start(bf16[2,2,56,1152]{3,2,1,0:T(8,128)(2,1)S(1)} %fusion.16), channel_id=1, source_target_pairs={{0,16},{1,17},{2,18},{3,19},{4,20},{5,21},{6,22},{7,23},{8,9},{9,8... | collective-permute-start | bytes 1548296 | tf_op jit(solution)/shard_map/ppermute | solution.py:29
  50.3 12.5 %collective-permute-start.15 = (bf16[2,1,56,1152]{3,2,1,0:T(8,128)(2,1)S(1)}, bf16[2,1,56,1152]{3,2,1,0:T(8,128)(2,1)S(1)}, u32[]{:S(2)}, u32[]{:S(2)}) collective-permute-start(bf16[2,1,56,1152]{3,2,1,0:T(8,128)(2,1)S(1)} %fusion.25), channel_id=1, source_target_pairs={{0,16},{1,17},{2,18},{3,19},{4,20},{5,21},{6,22},{7,23},{8,9},{9,8... | collective-permute-start | bytes 774152 | tf_op jit(solution)/shard_map/ppermute | solution.py:29
  53.2 12.0 %collective-permute-start.21 = (bf16[1,56,1152]{2,1,0:T(8,128)(2,1)S(1)}, bf16[1,56,1152]{2,1,0:T(8,128)(2,1)S(1)}, u32[]{:S(2)}, u32[]{:S(2)}) collective-permute-start(bf16[1,56,1152]{2,1,0:T(8,128)(2,1)S(1)} %fusion.56), channel_id=1, source_target_pairs={{0,1},{1,0},{2,3},{3,2},{4,5},{5,4},{6,7},{7,6},{8,24},{9,25},{10,... | collective-permute-start | bytes 387080 | tf_op jit(solution)/shard_map/ppermute | solution.py:29
  62.9 9.8 %collective-permute-start.16 = (bf16[1,56,1152]{2,1,0:T(8,128)(2,1)S(1)}, bf16[1,56,1152]{2,1,0:T(8,128)(2,1)S(1)}, u32[]{:S(2)}, u32[]{:S(2)}) collective-permute-start(bf16[1,56,1152]{2,1,0:T(8,128)(2,1)S(1)} %fusion.53), channel_id=1, source_target_pairs={{0,1},{1,0},{2,3},{3,2},{4,5},{5,4},{6,7},{7,6},{8,24},{9,25},{10,... | collective-permute-start | bytes 387080 | tf_op jit(solution)/shard_map/ppermute | solution.py:29
  63.8 6.8 %collective-permute-start.18 = (bf16[2,56,1152]{2,1,0:T(8,128)(2,1)S(1)}, bf16[2,56,1152]{2,1,0:T(8,128)(2,1)S(1)}, u32[]{:S(2)}, u32[]{:S(2)}) collective-permute-start(bf16[2,56,1152]{2,1,0:T(8,128)(2,1)S(1)} %fusion.32), channel_id=1, source_target_pairs={{0,1},{1,0},{2,3},{3,2},{4,5},{5,4},{6,7},{7,6},{8,24},{9,25},{10,... | collective-permute-start | bytes 774152 | tf_op jit(solution)/shard_map/ppermute | solution.py:29
  65.2 5.5 %collective-permute-start.22 = (bf16[56,1152]{1,0:T(8,128)(2,1)S(1)}, bf16[56,1152]{1,0:T(8,128)(2,1)S(1)}, u32[]{:S(2)}, u32[]{:S(2)}) collective-permute-start(bf16[56,1152]{1,0:T(8,128)(2,1)S(1)} %fusion.55), channel_id=1, source_target_pairs={{0,2},{1,3},{2,0},{3,1},{4,6},{5,7},{6,4},{7,5},{8,10},{9,11},{10,... | collective-permute-start | bytes 387080 | tf_op jit(solution)/shard_map/ppermute | solution.py:25
  70.7 7.6 %copy-start = (bf16[32,1152]{1,0:T(8,128)(2,1)S(1)}, bf16[32,1152]{1,0:T(8,128)(2,1)}, u32[]{:S(2)}) copy-start(bf16[32,1152]{1,0:T(8,128)(2,1)} %param.12) | copy-start | bytes 221188
  70.8 7.4 %collective-permute-start.23 = (bf16[56,1152]{1,0:T(8,128)(2,1)S(1)}, bf16[56,1152]{1,0:T(8,128)(2,1)S(1)}, u32[]{:S(2)}, u32[]{:S(2)}) collective-permute-start(bf16[56,1152]{1,0:T(8,128)(2,1)S(1)} %fusion.36), channel_id=1, source_target_pairs={{0,4},{1,5},{2,6},{3,7},{4,0},{5,1},{6,2},{7,3},{8,12},{9,13},{10,... | collective-permute-start | bytes 387080 | tf_op jit(solution)/shard_map/ppermute | solution.py:25
  71.2 7.0 %collective-permute-start.19 = (bf16[56,1152]{1,0:T(8,128)(2,1)S(1)}, bf16[56,1152]{1,0:T(8,128)(2,1)S(1)}, u32[]{:S(2)}, u32[]{:S(2)}) collective-permute-start(bf16[56,1152]{1,0:T(8,128)(2,1)S(1)} %fusion.54), channel_id=1, source_target_pairs={{0,2},{1,3},{2,0},{3,1},{4,6},{5,7},{6,4},{7,5},{8,10},{9,11},{10,... | collective-permute-start | bytes 387080 | tf_op jit(solution)/shard_map/ppermute | solution.py:25
  78.3 1.3 %collective-permute-start.24 = (f32[8,1152]{1,0:T(8,128)S(1)}, f32[8,1152]{1,0:T(8,128)S(1)}, u32[]{:S(2)}, u32[]{:S(2)}) collective-permute-start(f32[8,1152]{1,0:T(8,128)S(1)} %slice.220), channel_id=1, source_target_pairs={{0,8},{1,9},{2,10},{3,11},{4,12},{5,13},{6,14},{7,15},{8,0},{9,1},... | collective-permute-start | bytes 110600 | tf_op jit(solution)/shard_map/ppermute | solution.py:25
  79.5 4.4 %collective-permute-start.25 = (f32[16,1152]{1,0:T(8,128)S(1)}, f32[16,1152]{1,0:T(8,128)S(1)}, u32[]{:S(2)}, u32[]{:S(2)}) collective-permute-start(f32[16,1152]{1,0:T(8,128)S(1)} %maximum_select_fusion.1), channel_id=1, source_target_pairs={{0,16},{1,17},{2,18},{3,19},{4,20},{5,21},{6,22},{7,23},{8,24},{9,... | collective-permute-start | bytes 221192 | tf_op jit(solution)/shard_map/ppermute | solution.py:25

commit v4 on v3

v4 whole, which is shorter than its diff:
```python
import jax
import jax.numpy as jnp
from jax import lax
from jax.sharding import PartitionSpec as P

epsilon = 1e-06
logit_scale = 10.0
logit_bias = -5.0
axes = ("grp", "blk")
F32, BF16 = jnp.float32, jnp.bfloat16


def after(array, earlier):
    return lax.optimization_barrier((array, earlier))[0]


def unit_rows(raw_rows):
    inverse = lax.rsqrt(jnp.sum(raw_rows * raw_rows, axis=1, keepdims=True) + epsilon)
    return (raw_rows * inverse, inverse)


def make_shards(grp_size, blk_size):
    devices = grp_size * blk_size
    core_mask, y_mask, x_mask = blk_size, 2 * blk_size, 1
    depth = blk_size // 2
    assert grp_size == 4 and blk_size & (blk_size - 1) == 0 and depth >= 4

    def swap(array, mask):
        return lax.ppermute(array, axes, [(i, i ^ mask) for i in range(devices)])

    def swap_by_core(array, masks):
        pairs = [(i, i ^ masks[1 if i & core_mask else 0]) for i in range(devices)]
        return lax.ppermute(array, axes, pairs)

    def first(array):
        return swap_by_core(array, (x_mask, y_mask))

    def second(array):
        return swap_by_core(array, (y_mask, x_mask))

    def shards(pooled, img_weight, img_label, text_raw):
        images, width = pooled.shape
        rows, embed = img_weight.shape
        texts = text_raw.shape[0]
        quarter = texts // grp_size
        grp, blk = lax.axis_index("grp"), lax.axis_index("blk")
        core, side = grp % 2, grp // 2
        place = grp * blk_size + blk

        own = jnp.concatenate(
            [img_weight, lax.dynamic_slice_in_dim(text_raw, grp * quarter, quarter, 0)], axis=0
        )[None]
        by_z = [own]
        for kz in range(1, depth):
            by_z.append(swap(by_z[kz - 1], 2) if kz % 2 and kz > 1 else swap(own, 2 * kz))
        quads, firsts = [], []
        for kz, block in enumerate(by_z):
            if kz == 1:
                block = after(block, firsts[0])
            if kz == 2:
                block = after(block, by_z[1])
            firsts.append(first(block))
            pair = jnp.concatenate([by_z[kz], firsts[kz]], axis=0)
            quads.append(jnp.concatenate([pair, second(pair)], axis=0))
        gathered = [
            jnp.concatenate(quads, axis=0),
            jnp.concatenate([swap(quad, core_mask) for quad in quads], axis=0),
        ]

        def block_sources(kc):
            f = jnp.where((core ^ kc) == 0, x_mask, y_mask)
            s = x_mask + y_mask - f
            number = jnp.arange(4 * depth, dtype=jnp.int32)
            j, kz = number % 4, number // 4
            return place ^ (kc * core_mask) ^ (2 * kz) ^ ((j % 2) * f) ^ ((j // 2) * s)

        sources = jnp.concatenate([block_sources(0), block_sources(1)])

        turned = pooled.T.reshape(devices, rows, images)
        columns = jnp.take(turned, sources, axis=0).reshape(2, -1, images)
        mine, other = columns[0], columns[1]
        theirs = swap(other, core_mask)

        text_all = jnp.concatenate([g[:, rows:].reshape(-1, embed) for g in gathered], axis=0)
        text_all = unit_rows(text_all.astype(F32))[0].astype(BF16)
        text_first = (sources % blk_size) * texts + (sources // blk_size) * quarter
        text_ids = (text_first[:, None] + jnp.arange(quarter, dtype=jnp.int32)[None, :]).reshape(-1)

        def partly(column, found):
            return lax.dot_general(
                column,
                found[:, :rows].reshape(-1, embed),
                (((0,), (0,)), ((), ())),
                preferred_element_type=F32,
            )

        projected = partly(mine, gathered[0]) + partly(other, gathered[1])
        embed_float, inverse = unit_rows(projected)
        embedded = embed_float.astype(BF16)
        embedded_theirs = swap(embedded, core_mask)

        logits = (
            logit_scale
            * lax.dot_general(embedded, text_all, (((1,), (1,)), ((), ())), preferred_element_type=F32)
            + logit_bias
        )
        polarity = jnp.where(img_label[:, None] == text_ids[None, :], 1.0, -1.0).astype(F32)
        pair_slope = (
            -polarity * jax.nn.sigmoid(-polarity * logits) * (logit_scale / texts)
        ).astype(BF16)
        half = pair_slope.shape[1] // 2
        slope_theirs = swap(pair_slope[:, half:], core_mask)
        grad_embed = jnp.dot(pair_slope, text_all, preferred_element_type=F32)
        grad_proj = (
            inverse
            * (grad_embed - embed_float * jnp.sum(grad_embed * embed_float, axis=1, keepdims=True))
        ).astype(BF16)
        proj_theirs = swap(grad_proj, core_mask)

        across = (((0,), (0,)), ((), ()))
        grad_unit = lax.dot_general(
            pair_slope[:, :half], embedded, across, preferred_element_type=F32
        ) + lax.dot_general(slope_theirs, embedded_theirs, across, preferred_element_type=F32)
        grad_unit = grad_unit.reshape(depth, 4, quarter, embed)
        mine = mine.reshape(depth, 4 * rows, images)
        theirs = theirs.reshape(depth, 4 * rows, images)

        def send(array):
            return array.astype(BF16)

        halves, pieces = {}, {}
        for kz in range(depth - 1, -1, -1):
            part = jnp.dot(mine[kz], grad_proj, preferred_element_type=F32)
            part += jnp.dot(theirs[kz], proj_theirs, preferred_element_type=F32)
            part = jnp.concatenate([part.reshape(4, rows, embed), grad_unit[kz]], axis=1)
            away = send(part[2:])
            if kz + 2 in halves:
                away = after(away, halves[kz + 2])
            halves[kz] = second(away)
            part = part[:2] + halves[kz].astype(F32)
            pieces[kz] = part[0] + first(send(part[1])).astype(F32)
        for kz in range(3, depth, 2):
            pieces[kz - 1] += swap(send(pieces[kz]), 2).astype(F32)
        total = pieces[0]
        for kz in [1] + list(range(2, depth, 2)):
            total += swap(send(pieces[kz]), 2 * kz).astype(F32)
        grad_weight, grad_unit = total[:rows], total[rows:]

        def joined(array, mask, position):
            other = swap(array, mask)
            return jnp.where(
                position == 0,
                jnp.concatenate([array, other], axis=0),
                jnp.concatenate([other, array], axis=0),
            )

        grad_unit = joined(joined(grad_unit, core_mask, core), y_mask, side)
        text_float, text_inverse = unit_rows(text_raw.astype(F32))
        grad_text = text_inverse * (
            grad_unit - text_float * jnp.sum(grad_unit * text_float, axis=1, keepdims=True)
        )
        return (grad_weight, grad_text)

    return shards


def solution(mesh):
    return jax.shard_map(
        make_shards(mesh.shape["grp"], mesh.shape["blk"]),
        mesh=mesh,
        in_specs=(
            P(("grp", "blk"), None),
            P(("grp", "blk"), None),
            P(("grp", "blk")),
            P("blk", None),
        ),
        out_specs=(P(("grp", "blk"), None), P("blk", None)),
        check_vma=False,
    )
```

time: 85.2 us -> 76.4 us (0.90)
  waiting for transfers between devices: 42.7 us -> 34 us
  starting transfers between devices: 25.2 us -> 27.2 us
  local copies, waits for them, and re-layouts: 5.78 us -> 4.33 us
  other arithmetic: 5.14 us -> 4.03 us
    ppermute x12 -> x16, waiting for transfers between devices: 25 us -> 20.6 us  [swap_by_core(): return lax.ppermute(array, axes, pairs)]
    ppermute x14 -> x16, waiting for transfers between devices: 17.7 us -> 13.4 us  [swap(): return lax.ppermute(array, axes, [(i, i ^ mask) for i in range(devices)])]
    ppermute x12 -> x16, starting transfers between devices: 13.6 us -> 16.6 us  [swap_by_core(): return lax.ppermute(array, axes, pairs)]
    gather x3 -> x1, local copies, waits for them, and re-layouts: 1.69 us -> 0.6 us  [shards(): columns = jnp.take(turned, sources, axis=0).reshape(2, -1, images)]
    ppermute x14 -> x16, starting transfers between devices: 11.6 us -> 10.6 us  [swap(): return lax.ppermute(array, axes, [(i, i ^ mask) for i in range(devices)])]
    dot_general x8 -> x13, matrix products: 4.32 us -> 4.96 us  [the longest x2 1.51 us: partly(): lax.dot_general(column, found[:, :rows].reshape(-1, embed), (((0,), (0,))...]
    unnamed x14 -> x20, local copies, waits for them, and re-layouts: 1.63 us -> 1.91 us
  transfers between devices with their start and end apart: 26 -> 32, of which waited for: 12 -> 16; matrix products, arithmetic and copies ran while one was open for 10% -> 14% of each run, Pallas kernels for 0% -> 0%
where the time goes in v4:
time: 76.4 us; the launch traced here: 76.1 us
  waiting for transfers between devices  34 us (45%)
  starting transfers between devices  27.2 us (36%)
  matrix products  5.47 us (7%)
  local copies, waits for them, and re-layouts  4.33 us (6%)
  other arithmetic  4.03 us (5%)
  between operations  1.17 us (2%)
    ppermute x16, waiting for transfers between devices, swap_by_core(): return lax.ppermute(array, axes, pairs)  20.6 us
    ppermute x16, starting transfers between devices, swap_by_core(): return lax.ppermute(array, axes, pairs)  16.6 us
    ppermute x16, waiting for transfers between devices, swap(): return lax.ppermute(array, axes, [(i, i ^ mask) for i in range(devices)])  13.4 us
    ppermute x16, starting transfers between devices, swap(): return lax.ppermute(array, axes, [(i, i ^ mask) for i in range(devices)])  10.6 us
    unnamed x20, local copies, waits for them, and re-layouts  1.91 us
  transfers between devices with their start and end apart: 32, of which 16 were waited for; matrix products, arithmetic and copies ran while one was open for 14% of the time, Pallas kernels for 0%

profile of v4, /device:TPU:0, one launch (start us, length us, event | category | flops | bytes accessed | tf_op | source)
XLA Modules:
  0.0 76.1 jit_solution(9986526096703259693)
XLA Ops:
  0.6 0.7 constant_dynamic-slice_fusion
  1.4 0.9 %maximum_bitcast_fusion = bf16[1,56,1152]{2,1,0:T(8,128)(2,1)S(1)} fusion(bf16[8,1152]{1,0:T(8,128)(2,1)S(1)} %constant_dynamic-slice_fusion, bf16[48,1152]{1,0:T(8,128)(2,1)} %param.5), kind=kLoop, calls=%fused_computation.100 | loop fusion | flops 258048 | bytes 258048 | tf_op jit(solution)/shard_map/broadcast_in_dim | solution.py:50
  2.3 3.0 %collective-permute-start = (bf16[1,56,1152]{2,1,0:T(8,128)(2,1)S(1)}, bf16[1,56,1152]{2,1,0:T(8,128)(2,1)S(1)}, u32[]{:S(2)}, u32[]{:S(2)}) collective-permute-start(bf16[1,56,1152]{2,1,0:T(8,128)(2,1)S(1)} %maximum_bitcast_fusion), channel_id=1, source_target_pairs={{0,1},{1,0},{2,3},{3,2},{4,5},{5,4},{6,7},{7,6},{8,24},{9,25},{10,... | collective-permute-start | bytes 387080 | tf_op jit(solution)/shard_map/ppermute | solution.py:33
  5.3 1.6 %collective-permute-start.2 = (bf16[1,56,1152]{2,1,0:T(8,128)(2,1)S(1)}, bf16[1,56,1152]{2,1,0:T(8,128)(2,1)S(1)}, u32[]{:S(2)}, u32[]{:S(2)}) collective-permute-start(bf16[1,56,1152]{2,1,0:T(8,128)(2,1)S(1)} %maximum_bitcast_fusion), channel_id=1, source_target_pairs={{0,2},{1,3},{2,0},{3,1},{4,6},{5,7},{6,4},{7,5},{8,10},{9,11},{10,... | collective-permute-start | bytes 387080 | tf_op jit(solution)/shard_map/ppermute | solution.py:29
  6.9 2.6 %collective-permute-start.5 = (bf16[1,56,1152]{2,1,0:T(8,128)(2,1)S(1)}, bf16[1,56,1152]{2,1,0:T(8,128)(2,1)S(1)}, u32[]{:S(2)}, u32[]{:S(2)}) collective-permute-start(bf16[1,56,1152]{2,1,0:T(8,128)(2,1)S(1)} %maximum_bitcast_fusion), channel_id=1, source_target_pairs={{0,4},{1,5},{2,6},{3,7},{4,0},{5,1},{6,2},{7,3},{8,12},{9,13},{10,... | collective-permute-start | bytes 387080 | tf_op jit(solution)/shard_map/ppermute | solution.py:29
  9.6 1.4 %copy.6 = bf16[256,1536]{0,1:T(8,128)(2,1)S(1)} copy(bf16[256,1536]{1,0:T(8,128)(2,1)} %param.4) | data formatting | bytes 1572864 | tf_op args[0]
  11.0 0.6 gather_fusion
  12.3 1.6 %collective-permute-start.1 = (bf16[2,56,1152]{2,1,0:T(8,128)(2,1)S(1)}, bf16[2,56,1152]{2,1,0:T(8,128)(2,1)S(1)}, u32[]{:S(2)}, u32[]{:S(2)}) collective-permute-start(bf16[2,56,1152]{2,1,0:T(8,128)(2,1)S(1)} %pad_maximum_fusion.9), channel_id=1, source_target_pairs={{0,16},{1,17},{2,18},{3,19},{4,20},{5,21},{6,22},{7,23},{8,9},{9,8... | collective-permute-start | bytes 774152 | tf_op jit(solution)/shard_map/ppermute | solution.py:33
  13.9 0.5 collective-permute-start.3
  14.4 0.8 %collective-permute-done.5 = bf16[1,56,1152]{2,1,0:T(8,128)(2,1)S(1)} collective-permute-done((bf16[1,56,1152]{2,1,0:T(8,128)(2,1)S(1)}, bf16[1,56,1152]{2,1,0:T(8,128)(2,1)S(1)}, u32[]{:S(2)}, u32[]{:S(2)}) %collective-permute-start.5) | collective-permute-done | bytes 129056 | tf_op jit(solution)/shard_map/ppermute | solution.py:29
  15.2 1.5 %collective-permute-start.6 = (bf16[1,56,1152]{2,1,0:T(8,128)(2,1)S(1)}, bf16[1,56,1152]{2,1,0:T(8,128)(2,1)S(1)}, u32[]{:S(2)}, u32[]{:S(2)}) collective-permute-start(bf16[1,56,1152]{2,1,0:T(8,128)(2,1)S(1)} %collective-permute-done.5), channel_id=1, source_target_pairs={{0,1},{1,0},{2,3},{3,2},{4,5},{5,4},{6,7},{7,6},{8,24},{9,25},{10,... | collective-permute-start | bytes 387080 | tf_op jit(solution)/shard_map/ppermute | solution.py:33
  16.7 0.4 collective-permute-start.8
  17.2 2.4 %collective-permute-done.3 = bf16[1,56,1152]{2,1,0:T(8,128)(2,1)S(1)} collective-permute-done((bf16[1,56,1152]{2,1,0:T(8,128)(2,1)S(1)}, bf16[1,56,1152]{2,1,0:T(8,128)(2,1)S(1)}, u32[]{:S(2)}, u32[]{:S(2)}) %collective-permute-start.3) | collective-permute-done | bytes 129056 | tf_op jit(solution)/shard_map/ppermute | solution.py:33
  19.7 1.2 %collective-permute-start.4 = (bf16[2,56,1152]{2,1,0:T(8,128)(2,1)S(1)}, bf16[2,56,1152]{2,1,0:T(8,128)(2,1)S(1)}, u32[]{:S(2)}, u32[]{:S(2)}) collective-permute-start(bf16[2,56,1152]{2,1,0:T(8,128)(2,1)S(1)} %pad_maximum_fusion.10), channel_id=1, source_target_pairs={{0,16},{1,17},{2,18},{3,19},{4,20},{5,21},{6,22},{7,23},{8,9},{9,8... | collective-permute-start | bytes 774152 | tf_op jit(solution)/shard_map/ppermute | solution.py:33
  20.8 0.8 %collective-permute-done.8 = bf16[1,56,1152]{2,1,0:T(8,128)(2,1)S(1)} collective-permute-done((bf16[1,56,1152]{2,1,0:T(8,128)(2,1)S(1)}, bf16[1,56,1152]{2,1,0:T(8,128)(2,1)S(1)}, u32[]{:S(2)}, u32[]{:S(2)}) %collective-permute-start.8) | collective-permute-done | bytes 129056 | tf_op jit(solution)/shard_map/ppermute | solution.py:29
  21.7 0.5 collective-permute-start.9
  22.2 0.8 %collective-permute-start.7 = (bf16[2,56,1152]{2,1,0:T(8,128)(2,1)S(1)}, bf16[2,56,1152]{2,1,0:T(8,128)(2,1)S(1)}, u32[]{:S(2)}, u32[]{:S(2)}) collective-permute-start(bf16[2,56,1152]{2,1,0:T(8,128)(2,1)S(1)} %pad_maximum_fusion.11), channel_id=1, source_target_pairs={{0,16},{1,17},{2,18},{3,19},{4,20},{5,21},{6,22},{7,23},{8,9},{9,8... | collective-permute-start | bytes 774152 | tf_op jit(solution)/shard_map/ppermute | solution.py:33
  23.1 5.0 %collective-permute-done.9 = bf16[1,56,1152]{2,1,0:T(8,128)(2,1)S(1)} collective-permute-done((bf16[1,56,1152]{2,1,0:T(8,128)(2,1)S(1)}, bf16[1,56,1152]{2,1,0:T(8,128)(2,1)S(1)}, u32[]{:S(2)}, u32[]{:S(2)}) %collective-permute-start.9) | collective-permute-done | bytes 129056 | tf_op jit(solution)/shard_map/ppermute | solution.py:33
  28.1 0.6 collective-permute-start.10
  29.0 0.6 collective-permute-start.12
  29.9 4.6 %collective-permute-done.10 = bf16[2,56,1152]{2,1,0:T(8,128)(2,1)S(1)} collective-permute-done((bf16[2,56,1152]{2,1,0:T(8,128)(2,1)S(1)}, bf16[2,56,1152]{2,1,0:T(8,128)(2,1)S(1)}, u32[]{:S(2)}, u32[]{:S(2)}) %collective-permute-start.10) | collective-permute-done | bytes 258080 | tf_op jit(solution)/shard_map/ppermute | solution.py:33
  34.9 1.7 %collective-permute-done.14 = bf16[4,56,1152]{2,1,0:T(8,128)(2,1)S(1)} collective-permute-done((bf16[4,56,1152]{2,1,0:T(8,128)(2,1)S(1)}, bf16[4,56,1152]{2,1,0:T(8,128)(2,1)S(1)}, u32[]{:S(2)}, u32[]{:S(2)}) %collective-permute-start.14) | collective-permute-done | bytes 516128 | tf_op jit(solution)/shard_map/ppermute | solution.py:29
  36.7 0.7 convolution_bitcast_fusion
  37.4 0.8 %multiply_reduce_fusion.1 = (f32[256]{0:T(256)S(1)}, f32[256,1152]{1,0:T(8,128)S(1)}) fusion(f32[256,1152]{1,0:T(8,128)S(1)} %convolution_bitcast_fusion, bf16[32,48,256]{2,1,0:T(8,128)(2,1)S(1)} %broadcast_select_fusion, bf16[16,56,1152]{2,1,0:T(8,128)(2,1)S(1)} %constant_dynamic-update-slice_fusion), kind=kOutput, calls=%fused_computation.17 | convolution fusion | flops 453869312 | bytes 4916224 | tf_op jit(solution)/shard_map/dot_general | solution.py:90
  38.6 0.2 collective-permute-start.18
  38.9 0.5 fusion.13
  39.4 0.5 multiply_reduce_fusion
  39.9 0.2 multiply_convert_fusion
  40.2 0.3 collective-permute-start.16
  40.5 0.3 fusion.64
  40.8 0.3 collective-permute-start.17
  41.1 0.3 fusion.65
  41.4 0.3 fusion.63
  41.7 0.3 fusion.62
  42.0 0.3 fusion.50
  42.3 0.3 convolution_add_fusion.4
  42.7 0.3 convolution_add_fusion
  43.0 0.6 collective-permute-start.22
  43.6 0.3 convolution_add_fusion.2
  44.0 1.6 %collective-permute-start.19 = (bf16[2,56,1152]{2,1,0:T(8,128)(2,1)S(1)}, bf16[2,56,1152]{2,1,0:T(8,128)(2,1)S(1)}, u32[]{:S(2)}, u32[]{:S(2)}) collective-permute-start(bf16[2,56,1152]{2,1,0:T(8,128)(2,1)S(1)} %fusion.19), channel_id=1, source_target_pairs={{0,16},{1,17},{2,18},{3,19},{4,20},{5,21},{6,22},{7,23},{8,9},{9,8... | collective-permute-start | bytes 774152 | tf_op jit(solution)/shard_map/ppermute | solution.py:33
  45.5 0.3 convolution_add_fusion.1
  45.8 0.3 convolution_add_fusion.3
  46.2 3.2 %collective-permute-done.22 = bf16[2,56,1152]{2,1,0:T(8,128)(2,1)S(1)} collective-permute-done((bf16[2,56,1152]{2,1,0:T(8,128)(2,1)S(1)}, bf16[2,56,1152]{2,1,0:T(8,128)(2,1)S(1)}, u32[]{:S(2)}, u32[]{:S(2)}) %collective-permute-start.22) | collective-permute-done | bytes 258080 | tf_op jit(solution)/shard_map/ppermute | solution.py:33
  49.4 0.5 collective-permute-start.23
  50.0 0.9 %collective-permute-start.27 = (bf16[56,1152]{1,0:T(8,128)(2,1)S(1)}, bf16[56,1152]{1,0:T(8,128)(2,1)S(1)}, u32[]{:S(2)}, u32[]{:S(2)}) collective-permute-start(bf16[56,1152]{1,0:T(8,128)(2,1)S(1)} %fusion.45), channel_id=1, source_target_pairs={{0,1},{1,0},{2,3},{3,2},{4,5},{5,4},{6,7},{7,6},{8,24},{9,25},{10,... | collective-permute-start | bytes 387080 | tf_op jit(solution)/shard_map/ppermute | solution.py:33
  50.9 1.6 %collective-permute-done.19 = bf16[2,56,1152]{2,1,0:T(8,128)(2,1)S(1)} collective-permute-done((bf16[2,56,1152]{2,1,0:T(8,128)(2,1)S(1)}, bf16[2,56,1152]{2,1,0:T(8,128)(2,1)S(1)}, u32[]{:S(2)}, u32[]{:S(2)}) %collective-permute-start.19) | collective-permute-done | bytes 258080 | tf_op jit(solution)/shard_map/ppermute | solution.py:33
  52.6 0.3 collective-permute-start.26
  52.9 0.9 %collective-permute-start.20 = (bf16[2,56,1152]{2,1,0:T(8,128)(2,1)S(1)}, bf16[2,56,1152]{2,1,0:T(8,128)(2,1)S(1)}, u32[]{:S(2)}, u32[]{:S(2)}) collective-permute-start(bf16[2,56,1152]{2,1,0:T(8,128)(2,1)S(1)} %fusion.25), channel_id=1, source_target_pairs={{0,16},{1,17},{2,18},{3,19},{4,20},{5,21},{6,22},{7,23},{8,9},{9,8... | collective-permute-start | bytes 774152 | tf_op jit(solution)/shard_map/ppermute | solution.py:33
  53.8 2.7 %collective-permute-done.27 = bf16[56,1152]{1,0:T(8,128)(2,1)S(1)} collective-permute-done((bf16[56,1152]{1,0:T(8,128)(2,1)S(1)}, bf16[56,1152]{1,0:T(8,128)(2,1)S(1)}, u32[]{:S(2)}, u32[]{:S(2)}) %collective-permute-start.27) | collective-permute-done | bytes 129056 | tf_op jit(solution)/shard_map/ppermute | solution.py:33
  56.5 0.4 collective-permute-start.28
  56.9 0.8 %collective-permute-done.23 = bf16[2,56,1152]{2,1,0:T(8,128)(2,1)S(1)} collective-permute-done((bf16[2,56,1152]{2,1,0:T(8,128)(2,1)S(1)}, bf16[2,56,1152]{2,1,0:T(8,128)(2,1)S(1)}, u32[]{:S(2)}, u32[]{:S(2)}) %collective-permute-start.23) | collective-permute-done | bytes 258080 | tf_op jit(solution)/shard_map/ppermute | solution.py:33
  57.8 1.2 %collective-permute-start.24 = (bf16[56,1152]{1,0:T(8,128)(2,1)S(1)}, bf16[56,1152]{1,0:T(8,128)(2,1)S(1)}, u32[]{:S(2)}, u32[]{:S(2)}) collective-permute-start(bf16[56,1152]{1,0:T(8,128)(2,1)S(1)} %fusion.43), channel_id=1, source_target_pairs={{0,1},{1,0},{2,3},{3,2},{4,5},{5,4},{6,7},{7,6},{8,24},{9,25},{10,... | collective-permute-start | bytes 387080 | tf_op jit(solution)/shard_map/ppermute | solution.py:33
  59.0 0.2 collective-permute-done.26
  59.2 2.3 %collective-permute-done.28 = bf16[56,1152]{1,0:T(8,128)(2,1)S(1)} collective-permute-done((bf16[56,1152]{1,0:T(8,128)(2,1)S(1)}, bf16[56,1152]{1,0:T(8,128)(2,1)S(1)}, u32[]{:S(2)}, u32[]{:S(2)}) %collective-permute-start.28) | collective-permute-done | bytes 129056 | tf_op jit(solution)/shard_map/ppermute | solution.py:29
  61.6 0.7 collective-permute-start.29
  62.3 0.9 %collective-permute-start.21 = (bf16[56,1152]{1,0:T(8,128)(2,1)S(1)}, bf16[56,1152]{1,0:T(8,128)(2,1)S(1)}, u32[]{:S(2)}, u32[]{:S(2)}) collective-permute-start(bf16[56,1152]{1,0:T(8,128)(2,1)S(1)} %fusion.42), channel_id=1, source_target_pairs={{0,1},{1,0},{2,3},{3,2},{4,5},{5,4},{6,7},{7,6},{8,24},{9,25},{10,... | collective-permute-start | bytes 387080 | tf_op jit(solution)/shard_map/ppermute | solution.py:33
  63.3 2.1 %collective-permute-start.25 = (bf16[56,1152]{1,0:T(8,128)(2,1)S(1)}, bf16[56,1152]{1,0:T(8,128)(2,1)S(1)}, u32[]{:S(2)}, u32[]{:S(2)}) collective-permute-start(bf16[56,1152]{1,0:T(8,128)(2,1)S(1)} %fusion.32), channel_id=1, source_target_pairs={{0,2},{1,3},{2,0},{3,1},{4,6},{5,7},{6,4},{7,5},{8,10},{9,11},{10,... | collective-permute-start | bytes 387080 | tf_op jit(solution)/shard_map/ppermute | solution.py:29
  65.4 3.5 %collective-permute-done.29 = bf16[56,1152]{1,0:T(8,128)(2,1)S(1)} collective-permute-done((bf16[56,1152]{1,0:T(8,128)(2,1)S(1)}, bf16[56,1152]{1,0:T(8,128)(2,1)S(1)}, u32[]{:S(2)}, u32[]{:S(2)}) %collective-permute-start.29) | collective-permute-done | bytes 129056 | tf_op jit(solution)/shard_map/ppermute | solution.py:29
  68.9 0.5 collective-permute-done.25
  69.7 1.1 %collective-permute-done.30 = f32[8,1152]{1,0:T(8,128)S(1)} collective-permute-done((f32[8,1152]{1,0:T(8,128)S(1)}, f32[8,1152]{1,0:T(8,128)S(1)}, u32[]{:S(2)}, u32[]{:S(2)}) %collective-permute-start.30) | collective-permute-done | bytes 36896 | tf_op jit(solution)/shard_map/ppermute | solution.py:29
  70.8 1.0 %collective-permute-start.31 = (f32[16,1152]{1,0:T(8,128)S(1)}, f32[16,1152]{1,0:T(8,128)S(1)}, u32[]{:S(2)}, u32[]{:S(2)}) collective-permute-start(f32[16,1152]{1,0:T(8,128)S(1)} %maximum_select_fusion.1), channel_id=1, source_target_pairs={{0,16},{1,17},{2,18},{3,19},{4,20},{5,21},{6,22},{7,23},{8,24},{9,... | collective-permute-start | bytes 221192 | tf_op jit(solution)/shard_map/ppermute | solution.py:29
  71.8 0.7 slice.215
  72.5 2.7 %collective-permute-done.31 = f32[16,1152]{1,0:T(8,128)S(1)} collective-permute-done((f32[16,1152]{1,0:T(8,128)S(1)}, f32[16,1152]{1,0:T(8,128)S(1)}, u32[]{:S(2)}, u32[]{:S(2)}) %collective-permute-start.31) | collective-permute-done | bytes 73760 | tf_op jit(solution)/shard_map/ppermute | solution.py:29
  75.4 0.8 fusion.40
  (92 shorter events, 3.5 us)
Async XLA Ops:
  2.3 10.0 %collective-permute-start = (bf16[1,56,1152]{2,1,0:T(8,128)(2,1)S(1)}, bf16[1,56,1152]{2,1,0:T(8,128)(2,1)S(1)}, u32[]{:S(2)}, u32[]{:S(2)}) collective-permute-start(bf16[1,56,1152]{2,1,0:T(8,128)(2,1)S(1)} %maximum_bitcast_fusion), channel_id=1, source_target_pairs={{0,1},{1,0},{2,3},{3,2},{4,5},{5,4},{6,7},{7,6},{8,24},{9,25},{10,... | collective-permute-start | bytes 387080 | tf_op jit(solution)/shard_map/ppermute | solution.py:33
  5.3 8.6 %collective-permute-start.2 = (bf16[1,56,1152]{2,1,0:T(8,128)(2,1)S(1)}, bf16[1,56,1152]{2,1,0:T(8,128)(2,1)S(1)}, u32[]{:S(2)}, u32[]{:S(2)}) collective-permute-start(bf16[1,56,1152]{2,1,0:T(8,128)(2,1)S(1)} %maximum_bitcast_fusion), channel_id=1, source_target_pairs={{0,2},{1,3},{2,0},{3,1},{4,6},{5,7},{6,4},{7,5},{8,10},{9,11},{10,... | collective-permute-start | bytes 387080 | tf_op jit(solution)/shard_map/ppermute | solution.py:29
  6.9 8.4 %collective-permute-start.5 = (bf16[1,56,1152]{2,1,0:T(8,128)(2,1)S(1)}, bf16[1,56,1152]{2,1,0:T(8,128)(2,1)S(1)}, u32[]{:S(2)}, u32[]{:S(2)}) collective-permute-start(bf16[1,56,1152]{2,1,0:T(8,128)(2,1)S(1)} %maximum_bitcast_fusion), channel_id=1, source_target_pairs={{0,4},{1,5},{2,6},{3,7},{4,0},{5,1},{6,2},{7,3},{8,12},{9,13},{10,... | collective-permute-start | bytes 387080 | tf_op jit(solution)/shard_map/ppermute | solution.py:29
  11.0 1.2 %copy-start.1 = (bf16[48,1152]{1,0:T(8,128)(2,1)S(1)}, bf16[48,1152]{1,0:T(8,128)(2,1)}, u32[]{:S(2)}) copy-start(bf16[48,1152]{1,0:T(8,128)(2,1)} %param.5) | copy-start | bytes 331780
  11.9 30.8 %collective-permute-start.15 = (bf16[768,256]{1,0:T(8,128)(2,1)S(1)}, bf16[768,256]{1,0:T(8,128)(2,1)S(1)}, u32[]{:S(2)}, u32[]{:S(2)}) collective-permute-start(bf16[768,256]{1,0:T(8,128)(2,1)S(1)} %bitcast.108), channel_id=1, source_target_pairs={{0,8},{1,9},{2,10},{3,11},{4,12},{5,13},{6,14},{7,15},{8,0},{9,1},... | collective-permute-start | bytes 1179656 | tf_op jit(solution)/shard_map/ppermute | solution.py:29
  12.3 16.3 %collective-permute-start.1 = (bf16[2,56,1152]{2,1,0:T(8,128)(2,1)S(1)}, bf16[2,56,1152]{2,1,0:T(8,128)(2,1)S(1)}, u32[]{:S(2)}, u32[]{:S(2)}) collective-permute-start(bf16[2,56,1152]{2,1,0:T(8,128)(2,1)S(1)} %pad_maximum_fusion.9), channel_id=1, source_target_pairs={{0,16},{1,17},{2,18},{3,19},{4,20},{5,21},{6,22},{7,23},{8,9},{9,8... | collective-permute-start | bytes 774152 | tf_op jit(solution)/shard_map/ppermute | solution.py:33
  13.9 5.7 %collective-permute-start.3 = (bf16[1,56,1152]{2,1,0:T(8,128)(2,1)S(1)}, bf16[1,56,1152]{2,1,0:T(8,128)(2,1)S(1)}, u32[]{:S(2)}, u32[]{:S(2)}) collective-permute-start(bf16[1,56,1152]{2,1,0:T(8,128)(2,1)S(1)} %collective-permute-done.2), channel_id=1, source_target_pairs={{0,1},{1,0},{2,3},{3,2},{4,5},{5,4},{6,7},{7,6},{8,24},{9,25},{10,... | collective-permute-start | bytes 387080 | tf_op jit(solution)/shard_map/ppermute | solution.py:33
  15.2 7.0 %collective-permute-start.6 = (bf16[1,56,1152]{2,1,0:T(8,128)(2,1)S(1)}, bf16[1,56,1152]{2,1,0:T(8,128)(2,1)S(1)}, u32[]{:S(2)}, u32[]{:S(2)}) collective-permute-start(bf16[1,56,1152]{2,1,0:T(8,128)(2,1)S(1)} %collective-permute-done.5), channel_id=1, source_target_pairs={{0,1},{1,0},{2,3},{3,2},{4,5},{5,4},{6,7},{7,6},{8,24},{9,25},{10,... | collective-permute-start | bytes 387080 | tf_op jit(solution)/shard_map/ppermute | solution.py:33
  16.7 4.9 %collective-permute-start.8 = (bf16[1,56,1152]{2,1,0:T(8,128)(2,1)S(1)}, bf16[1,56,1152]{2,1,0:T(8,128)(2,1)S(1)}, u32[]{:S(2)}, u32[]{:S(2)}) collective-permute-start(bf16[1,56,1152]{2,1,0:T(8,128)(2,1)S(1)} %collective-permute-done.5), channel_id=1, source_target_pairs={{0,2},{1,3},{2,0},{3,1},{4,6},{5,7},{6,4},{7,5},{8,10},{9,11},{10,... | collective-permute-start | bytes 387080 | tf_op jit(solution)/shard_map/ppermute | solution.py:29
  19.7 9.2 %collective-permute-start.4 = (bf16[2,56,1152]{2,1,0:T(8,128)(2,1)S(1)}, bf16[2,56,1152]{2,1,0:T(8,128)(2,1)S(1)}, u32[]{:S(2)}, u32[]{:S(2)}) collective-permute-start(bf16[2,56,1152]{2,1,0:T(8,128)(2,1)S(1)} %pad_maximum_fusion.10), channel_id=1, source_target_pairs={{0,16},{1,17},{2,18},{3,19},{4,20},{5,21},{6,22},{7,23},{8,9},{9,8... | collective-permute-start | bytes 774152 | tf_op jit(solution)/shard_map/ppermute | solution.py:33
  21.7 6.4 %collective-permute-start.9 = (bf16[1,56,1152]{2,1,0:T(8,128)(2,1)S(1)}, bf16[1,56,1152]{2,1,0:T(8,128)(2,1)S(1)}, u32[]{:S(2)}, u32[]{:S(2)}) collective-permute-start(bf16[1,56,1152]{2,1,0:T(8,128)(2,1)S(1)} %collective-permute-done.8), channel_id=1, source_target_pairs={{0,1},{1,0},{2,3},{3,2},{4,5},{5,4},{6,7},{7,6},{8,24},{9,25},{10,... | collective-permute-start | bytes 387080 | tf_op jit(solution)/shard_map/ppermute | solution.py:33
  22.2 7.3 %collective-permute-start.7 = (bf16[2,56,1152]{2,1,0:T(8,128)(2,1)S(1)}, bf16[2,56,1152]{2,1,0:T(8,128)(2,1)S(1)}, u32[]{:S(2)}, u32[]{:S(2)}) collective-permute-start(bf16[2,56,1152]{2,1,0:T(8,128)(2,1)S(1)} %pad_maximum_fusion.11), channel_id=1, source_target_pairs={{0,16},{1,17},{2,18},{3,19},{4,20},{5,21},{6,22},{7,23},{8,9},{9,8... | collective-permute-start | bytes 774152 | tf_op jit(solution)/shard_map/ppermute | solution.py:33
  28.1 6.4 %collective-permute-start.10 = (bf16[2,56,1152]{2,1,0:T(8,128)(2,1)S(1)}, bf16[2,56,1152]{2,1,0:T(8,128)(2,1)S(1)}, u32[]{:S(2)}, u32[]{:S(2)}) collective-permute-start(bf16[2,56,1152]{2,1,0:T(8,128)(2,1)S(1)} %pad_maximum_fusion.12), channel_id=1, source_target_pairs={{0,16},{1,17},{2,18},{3,19},{4,20},{5,21},{6,22},{7,23},{8,9},{9,8... | collective-permute-start | bytes 774152 | tf_op jit(solution)/shard_map/ppermute | solution.py:33
  28.7 6.0 %collective-permute-start.11 = (bf16[4,56,1152]{2,1,0:T(8,128)(2,1)S(1)}, bf16[4,56,1152]{2,1,0:T(8,128)(2,1)S(1)}, u32[]{:S(2)}, u32[]{:S(2)}) collective-permute-start(bf16[4,56,1152]{2,1,0:T(8,128)(2,1)S(1)} %pad_maximum_fusion.5), channel_id=1, source_target_pairs={{0,8},{1,9},{2,10},{3,11},{4,12},{5,13},{6,14},{7,15},{8,0},{9,1},... | collective-permute-start | bytes 1548296 | tf_op jit(solution)/shard_map/ppermute | solution.py:29
  29.0 5.8 %collective-permute-start.12 = (bf16[4,56,1152]{2,1,0:T(8,128)(2,1)S(1)}, bf16[4,56,1152]{2,1,0:T(8,128)(2,1)S(1)}, u32[]{:S(2)}, u32[]{:S(2)}) collective-permute-start(bf16[4,56,1152]{2,1,0:T(8,128)(2,1)S(1)} %pad_maximum_fusion.6), channel_id=1, source_target_pairs={{0,8},{1,9},{2,10},{3,11},{4,12},{5,13},{6,14},{7,15},{8,0},{9,1},... | collective-permute-start | bytes 1548296 | tf_op jit(solution)/shard_map/ppermute | solution.py:29
  29.6 5.2 %collective-permute-start.13 = (bf16[4,56,1152]{2,1,0:T(8,128)(2,1)S(1)}, bf16[4,56,1152]{2,1,0:T(8,128)(2,1)S(1)}, u32[]{:S(2)}, u32[]{:S(2)}) collective-permute-start(bf16[4,56,1152]{2,1,0:T(8,128)(2,1)S(1)} %pad_maximum_fusion.7), channel_id=1, source_target_pairs={{0,8},{1,9},{2,10},{3,11},{4,12},{5,13},{6,14},{7,15},{8,0},{9,1},... | collective-permute-start | bytes 1548296 | tf_op jit(solution)/shard_map/ppermute | solution.py:29
  34.6 2.0 %collective-permute-start.14 = (bf16[4,56,1152]{2,1,0:T(8,128)(2,1)S(1)}, bf16[4,56,1152]{2,1,0:T(8,128)(2,1)S(1)}, u32[]{:S(2)}, u32[]{:S(2)}) collective-permute-start(bf16[4,56,1152]{2,1,0:T(8,128)(2,1)S(1)} %pad_maximum_fusion.8), channel_id=1, source_target_pairs={{0,8},{1,9},{2,10},{3,11},{4,12},{5,13},{6,14},{7,15},{8,0},{9,1},... | collective-permute-start | bytes 1548296 | tf_op jit(solution)/shard_map/ppermute | solution.py:29
  38.2 0.7 copy-start.2
  38.6 3.8 %collective-permute-start.18 = (bf16[256,1152]{1,0:T(8,128)(2,1)S(1)}, bf16[256,1152]{1,0:T(8,128)(2,1)S(1)}, u32[]{:S(2)}, u32[]{:S(2)}) collective-permute-start(bf16[256,1152]{1,0:T(8,128)(2,1)S(1)} %multiply_convert_fusion.1), channel_id=1, source_target_pairs={{0,8},{1,9},{2,10},{3,11},{4,12},{5,13},{6,14},{7,15},{8,0},{9,1},... | collective-permute-start | bytes 1769480 | tf_op jit(solution)/shard_map/ppermute | solution.py:29
  40.2 2.5 %collective-permute-start.16 = (bf16[256,1152]{1,0:T(8,128)(2,1)S(1)}, bf16[256,1152]{1,0:T(8,128)(2,1)S(1)}, u32[]{:S(2)}, u32[]{:S(2)}) collective-permute-start(bf16[256,1152]{1,0:T(8,128)(2,1)S(1)} %multiply_convert_fusion), channel_id=1, source_target_pairs={{0,8},{1,9},{2,10},{3,11},{4,12},{5,13},{6,14},{7,15},{8,0},{9,1},... | collective-permute-start | bytes 1769480 | tf_op jit(solution)/shard_map/ppermute | solution.py:29
  40.8 1.5 %collective-permute-start.17 = (bf16[256,128]{1,0:T(8,128)(2,1)S(1)}, bf16[256,128]{1,0:T(8,128)(2,1)S(1)}, u32[]{:S(2)}, u32[]{:S(2)}) collective-permute-start(bf16[256,128]{1,0:T(8,128)(2,1)S(1)} %slice.188), channel_id=1, source_target_pairs={{0,8},{1,9},{2,10},{3,11},{4,12},{5,13},{6,14},{7,15},{8,0},{9,1},... | collective-permute-start | bytes 196616 | tf_op jit(solution)/shard_map/ppermute | solution.py:29
  43.0 6.4 %collective-permute-start.22 = (bf16[2,56,1152]{2,1,0:T(8,128)(2,1)S(1)}, bf16[2,56,1152]{2,1,0:T(8,128)(2,1)S(1)}, u32[]{:S(2)}, u32[]{:S(2)}) collective-permute-start(bf16[2,56,1152]{2,1,0:T(8,128)(2,1)S(1)} %fusion.15), channel_id=1, source_target_pairs={{0,16},{1,17},{2,18},{3,19},{4,20},{5,21},{6,22},{7,23},{8,9},{9,8... | collective-permute-start | bytes 774152 | tf_op jit(solution)/shard_map/ppermute | solution.py:33
  44.0 8.5 %collective-permute-start.19 = (bf16[2,56,1152]{2,1,0:T(8,128)(2,1)S(1)}, bf16[2,56,1152]{2,1,0:T(8,128)(2,1)S(1)}, u32[]{:S(2)}, u32[]{:S(2)}) collective-permute-start(bf16[2,56,1152]{2,1,0:T(8,128)(2,1)S(1)} %fusion.19), channel_id=1, source_target_pairs={{0,16},{1,17},{2,18},{3,19},{4,20},{5,21},{6,22},{7,23},{8,9},{9,8... | collective-permute-start | bytes 774152 | tf_op jit(solution)/shard_map/ppermute | solution.py:33
  49.4 8.3 %collective-permute-start.23 = (bf16[2,56,1152]{2,1,0:T(8,128)(2,1)S(1)}, bf16[2,56,1152]{2,1,0:T(8,128)(2,1)S(1)}, u32[]{:S(2)}, u32[]{:S(2)}) collective-permute-start(bf16[2,56,1152]{2,1,0:T(8,128)(2,1)S(1)} %fusion.24), channel_id=1, source_target_pairs={{0,16},{1,17},{2,18},{3,19},{4,20},{5,21},{6,22},{7,23},{8,9},{9,8... | collective-permute-start | bytes 774152 | tf_op jit(solution)/shard_map/ppermute | solution.py:33
  50.0 6.5 %collective-permute-start.27 = (bf16[56,1152]{1,0:T(8,128)(2,1)S(1)}, bf16[56,1152]{1,0:T(8,128)(2,1)S(1)}, u32[]{:S(2)}, u32[]{:S(2)}) collective-permute-start(bf16[56,1152]{1,0:T(8,128)(2,1)S(1)} %fusion.45), channel_id=1, source_target_pairs={{0,1},{1,0},{2,3},{3,2},{4,5},{5,4},{6,7},{7,6},{8,24},{9,25},{10,... | collective-permute-start | bytes 387080 | tf_op jit(solution)/shard_map/ppermute | solution.py:33
  52.6 6.7 %collective-permute-start.26 = (bf16[56,1152]{1,0:T(8,128)(2,1)S(1)}, bf16[56,1152]{1,0:T(8,128)(2,1)S(1)}, u32[]{:S(2)}, u32[]{:S(2)}) collective-permute-start(bf16[56,1152]{1,0:T(8,128)(2,1)S(1)} %fusion.44), channel_id=1, source_target_pairs={{0,1},{1,0},{2,3},{3,2},{4,5},{5,4},{6,7},{7,6},{8,24},{9,25},{10,... | collective-permute-start | bytes 387080 | tf_op jit(solution)/shard_map/ppermute | solution.py:33
  52.9 9.4 %collective-permute-start.20 = (bf16[2,56,1152]{2,1,0:T(8,128)(2,1)S(1)}, bf16[2,56,1152]{2,1,0:T(8,128)(2,1)S(1)}, u32[]{:S(2)}, u32[]{:S(2)}) collective-permute-start(bf16[2,56,1152]{2,1,0:T(8,128)(2,1)S(1)} %fusion.25), channel_id=1, source_target_pairs={{0,16},{1,17},{2,18},{3,19},{4,20},{5,21},{6,22},{7,23},{8,9},{9,8... | collective-permute-start | bytes 774152 | tf_op jit(solution)/shard_map/ppermute | solution.py:33
  56.5 5.0 %collective-permute-start.28 = (bf16[56,1152]{1,0:T(8,128)(2,1)S(1)}, bf16[56,1152]{1,0:T(8,128)(2,1)S(1)}, u32[]{:S(2)}, u32[]{:S(2)}) collective-permute-start(bf16[56,1152]{1,0:T(8,128)(2,1)S(1)} %fusion.27), channel_id=1, source_target_pairs={{0,2},{1,3},{2,0},{3,1},{4,6},{5,7},{6,4},{7,5},{8,10},{9,11},{10,... | collective-permute-start | bytes 387080 | tf_op jit(solution)/shard_map/ppermute | solution.py:29
  57.8 11.7 %copy-start = (bf16[32,1152]{1,0:T(8,128)(2,1)S(1)}, bf16[32,1152]{1,0:T(8,128)(2,1)}, u32[]{:S(2)}) copy-start(bf16[32,1152]{1,0:T(8,128)(2,1)} %param.7) | copy-start | bytes 221188
  57.8 5.4 %collective-permute-start.24 = (bf16[56,1152]{1,0:T(8,128)(2,1)S(1)}, bf16[56,1152]{1,0:T(8,128)(2,1)S(1)}, u32[]{:S(2)}, u32[]{:S(2)}) collective-permute-start(bf16[56,1152]{1,0:T(8,128)(2,1)S(1)} %fusion.43), channel_id=1, source_target_pairs={{0,1},{1,0},{2,3},{3,2},{4,5},{5,4},{6,7},{7,6},{8,24},{9,25},{10,... | collective-permute-start | bytes 387080 | tf_op jit(solution)/shard_map/ppermute | solution.py:33
  61.6 7.3 %collective-permute-start.29 = (bf16[56,1152]{1,0:T(8,128)(2,1)S(1)}, bf16[56,1152]{1,0:T(8,128)(2,1)S(1)}, u32[]{:S(2)}, u32[]{:S(2)}) collective-permute-start(bf16[56,1152]{1,0:T(8,128)(2,1)S(1)} %fusion.30), channel_id=1, source_target_pairs={{0,4},{1,5},{2,6},{3,7},{4,0},{5,1},{6,2},{7,3},{8,12},{9,13},{10,... | collective-permute-start | bytes 387080 | tf_op jit(solution)/shard_map/ppermute | solution.py:29
  62.3 6.5 %collective-permute-start.21 = (bf16[56,1152]{1,0:T(8,128)(2,1)S(1)}, bf16[56,1152]{1,0:T(8,128)(2,1)S(1)}, u32[]{:S(2)}, u32[]{:S(2)}) collective-permute-start(bf16[56,1152]{1,0:T(8,128)(2,1)S(1)} %fusion.42), channel_id=1, source_target_pairs={{0,1},{1,0},{2,3},{3,2},{4,5},{5,4},{6,7},{7,6},{8,24},{9,25},{10,... | collective-permute-start | bytes 387080 | tf_op jit(solution)/shard_map/ppermute | solution.py:33
  63.3 6.1 %collective-permute-start.25 = (bf16[56,1152]{1,0:T(8,128)(2,1)S(1)}, bf16[56,1152]{1,0:T(8,128)(2,1)S(1)}, u32[]{:S(2)}, u32[]{:S(2)}) collective-permute-start(bf16[56,1152]{1,0:T(8,128)(2,1)S(1)} %fusion.32), channel_id=1, source_target_pairs={{0,2},{1,3},{2,0},{3,1},{4,6},{5,7},{6,4},{7,5},{8,10},{9,11},{10,... | collective-permute-start | bytes 387080 | tf_op jit(solution)/shard_map/ppermute | solution.py:29
  69.5 1.3 %collective-permute-start.30 = (f32[8,1152]{1,0:T(8,128)S(1)}, f32[8,1152]{1,0:T(8,128)S(1)}, u32[]{:S(2)}, u32[]{:S(2)}) collective-permute-start(f32[8,1152]{1,0:T(8,128)S(1)} %slice.216), channel_id=1, source_target_pairs={{0,8},{1,9},{2,10},{3,11},{4,12},{5,13},{6,14},{7,15},{8,0},{9,1},... | collective-permute-start | bytes 110600 | tf_op jit(solution)/shard_map/ppermute | solution.py:29
  70.8 4.4 %collective-permute-start.31 = (f32[16,1152]{1,0:T(8,128)S(1)}, f32[16,1152]{1,0:T(8,128)S(1)}, u32[]{:S(2)}, u32[]{:S(2)}) collective-permute-start(f32[16,1152]{1,0:T(8,128)S(1)} %maximum_select_fusion.1), channel_id=1, source_target_pairs={{0,16},{1,17},{2,18},{3,19},{4,20},{5,21},{6,22},{7,23},{8,24},{9,... | collective-permute-start | bytes 221192 | tf_op jit(solution)/shard_map/ppermute | solution.py:29

commit v5 on v4

--- a/solution.py
+++ b/solution.py
@@ -44,7 +44,7 @@
         texts = text_raw.shape[0]
         quarter = texts // grp_size
         grp, blk = lax.axis_index("grp"), lax.axis_index("blk")
-        core, side = grp % 2, grp // 2
+        core = grp % 2
         place = grp * blk_size + blk
 
         own = jnp.concatenate(
@@ -146,15 +146,14 @@
             total += swap(send(pieces[kz]), 2 * kz).astype(F32)
         grad_weight, grad_unit = total[:rows], total[rows:]
 
-        def joined(array, mask, position):
-            other = swap(array, mask)
-            return jnp.where(
-                position == 0,
-                jnp.concatenate([array, other], axis=0),
-                jnp.concatenate([other, array], axis=0),
-            )
-
-        grad_unit = joined(joined(grad_unit, core_mask, core), y_mask, side)
+        quarters = [grad_unit] + [swap(grad_unit, g * core_mask) for g in range(1, grp_size)]
+        ordered = []
+        for g in range(grp_size):
+            found = quarters[0]
+            for k in range(1, grp_size):
+                found = jnp.where(grp == (g ^ k), quarters[k], found)
+            ordered.append(found)
+        grad_unit = jnp.concatenate(ordered, axis=0)
         text_float, text_inverse = unit_rows(text_raw.astype(F32))
         grad_text = text_inverse * (
             grad_unit - text_float * jnp.sum(grad_unit * text_float, axis=1, keepdims=True)

time: 76.4 us -> 75.2 us (0.984)
  waiting for transfers between devices: 34 us -> 31.9 us
  starting transfers between devices: 27.2 us -> 28 us
    ppermute x16 -> x17, waiting for transfers between devices: 13.4 us -> 11.3 us  [swap(): return lax.ppermute(array, axes, [(i, i ^ mask) for i in range(devices)])]
    ppermute x16 -> x17, starting transfers between devices: 10.6 us -> 11.4 us  [swap(): return lax.ppermute(array, axes, [(i, i ^ mask) for i in range(devices)])]
  transfers between devices with their start and end apart: 32 -> 33, of which waited for: 16 -> 16; matrix products, arithmetic and copies ran while one was open for 14% -> 14% of each run, Pallas kernels for 0% -> 0%
where the time goes in v5:
time: 75.2 us; the launch traced here: 74.9 us
  waiting for transfers between devices  31.9 us (42%)
  starting transfers between devices  28 us (37%)
  matrix products  5.47 us (7%)
  local copies, waits for them, and re-layouts  4.33 us (6%)
  other arithmetic  4.04 us (5%)
  between operations  1.16 us (2%)
    ppermute x16, waiting for transfers between devices, swap_by_core(): return lax.ppermute(array, axes, pairs)  20.6 us
    ppermute x16, starting transfers between devices, swap_by_core(): return lax.ppermute(array, axes, pairs)  16.6 us
    ppermute x17, starting transfers between devices, swap(): return lax.ppermute(array, axes, [(i, i ^ mask) for i in range(devices)])  11.4 us
    ppermute x17, waiting for transfers between devices, swap(): return lax.ppermute(array, axes, [(i, i ^ mask) for i in range(devices)])  11.3 us
    unnamed x20, local copies, waits for them, and re-layouts  1.91 us
    dot_general x2, matrix products, partly(): lax.dot_general(column, found[:, :rows].reshape(-1, embed), (((0,), (0,))...  1.51 us
  transfers between devices with their start and end apart: 33, of which 16 were waited for; matrix products, arithmetic and copies ran while one was open for 14% of the time, Pallas kernels for 0%

profile of v5, /device:TPU:0, one launch (start us, length us, event | category | flops | bytes accessed | tf_op | source)
XLA Modules:
  0.0 74.9 jit_solution(409452734772060207)
XLA Ops:
  0.6 0.7 constant_dynamic-slice_fusion
  1.4 0.9 %maximum_bitcast_fusion = bf16[1,56,1152]{2,1,0:T(8,128)(2,1)S(1)} fusion(bf16[8,1152]{1,0:T(8,128)(2,1)S(1)} %constant_dynamic-slice_fusion, bf16[48,1152]{1,0:T(8,128)(2,1)} %param.5), kind=kLoop, calls=%fused_computation.100 | loop fusion | flops 258048 | bytes 258048 | tf_op jit(solution)/shard_map/broadcast_in_dim | solution.py:50
  2.3 3.0 %collective-permute-start = (bf16[1,56,1152]{2,1,0:T(8,128)(2,1)S(1)}, bf16[1,56,1152]{2,1,0:T(8,128)(2,1)S(1)}, u32[]{:S(2)}, u32[]{:S(2)}) collective-permute-start(bf16[1,56,1152]{2,1,0:T(8,128)(2,1)S(1)} %maximum_bitcast_fusion), channel_id=1, source_target_pairs={{0,1},{1,0},{2,3},{3,2},{4,5},{5,4},{6,7},{7,6},{8,24},{9,25},{10,... | collective-permute-start | bytes 387080 | tf_op jit(solution)/shard_map/ppermute | solution.py:33
  5.3 1.6 %collective-permute-start.2 = (bf16[1,56,1152]{2,1,0:T(8,128)(2,1)S(1)}, bf16[1,56,1152]{2,1,0:T(8,128)(2,1)S(1)}, u32[]{:S(2)}, u32[]{:S(2)}) collective-permute-start(bf16[1,56,1152]{2,1,0:T(8,128)(2,1)S(1)} %maximum_bitcast_fusion), channel_id=1, source_target_pairs={{0,2},{1,3},{2,0},{3,1},{4,6},{5,7},{6,4},{7,5},{8,10},{9,11},{10,... | collective-permute-start | bytes 387080 | tf_op jit(solution)/shard_map/ppermute | solution.py:29
  6.9 2.6 %collective-permute-start.5 = (bf16[1,56,1152]{2,1,0:T(8,128)(2,1)S(1)}, bf16[1,56,1152]{2,1,0:T(8,128)(2,1)S(1)}, u32[]{:S(2)}, u32[]{:S(2)}) collective-permute-start(bf16[1,56,1152]{2,1,0:T(8,128)(2,1)S(1)} %maximum_bitcast_fusion), channel_id=1, source_target_pairs={{0,4},{1,5},{2,6},{3,7},{4,0},{5,1},{6,2},{7,3},{8,12},{9,13},{10,... | collective-permute-start | bytes 387080 | tf_op jit(solution)/shard_map/ppermute | solution.py:29
  9.6 1.4 %copy.6 = bf16[256,1536]{0,1:T(8,128)(2,1)S(1)} copy(bf16[256,1536]{1,0:T(8,128)(2,1)} %param.4) | data formatting | bytes 1572864 | tf_op args[0]
  11.0 0.6 gather_fusion
  12.3 1.6 %collective-permute-start.1 = (bf16[2,56,1152]{2,1,0:T(8,128)(2,1)S(1)}, bf16[2,56,1152]{2,1,0:T(8,128)(2,1)S(1)}, u32[]{:S(2)}, u32[]{:S(2)}) collective-permute-start(bf16[2,56,1152]{2,1,0:T(8,128)(2,1)S(1)} %pad_maximum_fusion.9), channel_id=1, source_target_pairs={{0,16},{1,17},{2,18},{3,19},{4,20},{5,21},{6,22},{7,23},{8,9},{9,8... | collective-permute-start | bytes 774152 | tf_op jit(solution)/shard_map/ppermute | solution.py:33
  13.9 0.5 collective-permute-start.3
  14.4 0.8 %collective-permute-done.5 = bf16[1,56,1152]{2,1,0:T(8,128)(2,1)S(1)} collective-permute-done((bf16[1,56,1152]{2,1,0:T(8,128)(2,1)S(1)}, bf16[1,56,1152]{2,1,0:T(8,128)(2,1)S(1)}, u32[]{:S(2)}, u32[]{:S(2)}) %collective-permute-start.5) | collective-permute-done | bytes 129056 | tf_op jit(solution)/shard_map/ppermute | solution.py:29
  15.2 1.5 %collective-permute-start.6 = (bf16[1,56,1152]{2,1,0:T(8,128)(2,1)S(1)}, bf16[1,56,1152]{2,1,0:T(8,128)(2,1)S(1)}, u32[]{:S(2)}, u32[]{:S(2)}) collective-permute-start(bf16[1,56,1152]{2,1,0:T(8,128)(2,1)S(1)} %collective-permute-done.5), channel_id=1, source_target_pairs={{0,1},{1,0},{2,3},{3,2},{4,5},{5,4},{6,7},{7,6},{8,24},{9,25},{10,... | collective-permute-start | bytes 387080 | tf_op jit(solution)/shard_map/ppermute | solution.py:33
  16.7 0.4 collective-permute-start.8
  17.2 2.4 %collective-permute-done.3 = bf16[1,56,1152]{2,1,0:T(8,128)(2,1)S(1)} collective-permute-done((bf16[1,56,1152]{2,1,0:T(8,128)(2,1)S(1)}, bf16[1,56,1152]{2,1,0:T(8,128)(2,1)S(1)}, u32[]{:S(2)}, u32[]{:S(2)}) %collective-permute-start.3) | collective-permute-done | bytes 129056 | tf_op jit(solution)/shard_map/ppermute | solution.py:33
  19.7 1.2 %collective-permute-start.4 = (bf16[2,56,1152]{2,1,0:T(8,128)(2,1)S(1)}, bf16[2,56,1152]{2,1,0:T(8,128)(2,1)S(1)}, u32[]{:S(2)}, u32[]{:S(2)}) collective-permute-start(bf16[2,56,1152]{2,1,0:T(8,128)(2,1)S(1)} %pad_maximum_fusion.10), channel_id=1, source_target_pairs={{0,16},{1,17},{2,18},{3,19},{4,20},{5,21},{6,22},{7,23},{8,9},{9,8... | collective-permute-start | bytes 774152 | tf_op jit(solution)/shard_map/ppermute | solution.py:33
  20.8 0.8 %collective-permute-done.8 = bf16[1,56,1152]{2,1,0:T(8,128)(2,1)S(1)} collective-permute-done((bf16[1,56,1152]{2,1,0:T(8,128)(2,1)S(1)}, bf16[1,56,1152]{2,1,0:T(8,128)(2,1)S(1)}, u32[]{:S(2)}, u32[]{:S(2)}) %collective-permute-start.8) | collective-permute-done | bytes 129056 | tf_op jit(solution)/shard_map/ppermute | solution.py:29
  21.7 0.5 collective-permute-start.9
  22.2 0.8 %collective-permute-start.7 = (bf16[2,56,1152]{2,1,0:T(8,128)(2,1)S(1)}, bf16[2,56,1152]{2,1,0:T(8,128)(2,1)S(1)}, u32[]{:S(2)}, u32[]{:S(2)}) collective-permute-start(bf16[2,56,1152]{2,1,0:T(8,128)(2,1)S(1)} %pad_maximum_fusion.11), channel_id=1, source_target_pairs={{0,16},{1,17},{2,18},{3,19},{4,20},{5,21},{6,22},{7,23},{8,9},{9,8... | collective-permute-start | bytes 774152 | tf_op jit(solution)/shard_map/ppermute | solution.py:33
  23.1 5.0 %collective-permute-done.9 = bf16[1,56,1152]{2,1,0:T(8,128)(2,1)S(1)} collective-permute-done((bf16[1,56,1152]{2,1,0:T(8,128)(2,1)S(1)}, bf16[1,56,1152]{2,1,0:T(8,128)(2,1)S(1)}, u32[]{:S(2)}, u32[]{:S(2)}) %collective-permute-start.9) | collective-permute-done | bytes 129056 | tf_op jit(solution)/shard_map/ppermute | solution.py:33
  28.1 0.6 collective-permute-start.10
  29.0 0.6 collective-permute-start.12
  29.9 4.6 %collective-permute-done.10 = bf16[2,56,1152]{2,1,0:T(8,128)(2,1)S(1)} collective-permute-done((bf16[2,56,1152]{2,1,0:T(8,128)(2,1)S(1)}, bf16[2,56,1152]{2,1,0:T(8,128)(2,1)S(1)}, u32[]{:S(2)}, u32[]{:S(2)}) %collective-permute-start.10) | collective-permute-done | bytes 258080 | tf_op jit(solution)/shard_map/ppermute | solution.py:33
  34.9 1.7 %collective-permute-done.14 = bf16[4,56,1152]{2,1,0:T(8,128)(2,1)S(1)} collective-permute-done((bf16[4,56,1152]{2,1,0:T(8,128)(2,1)S(1)}, bf16[4,56,1152]{2,1,0:T(8,128)(2,1)S(1)}, u32[]{:S(2)}, u32[]{:S(2)}) %collective-permute-start.14) | collective-permute-done | bytes 516128 | tf_op jit(solution)/shard_map/ppermute | solution.py:29
  36.7 0.7 convolution_bitcast_fusion
  37.4 0.8 %multiply_reduce_fusion.1 = (f32[256]{0:T(256)S(1)}, f32[256,1152]{1,0:T(8,128)S(1)}) fusion(f32[256,1152]{1,0:T(8,128)S(1)} %convolution_bitcast_fusion, bf16[32,48,256]{2,1,0:T(8,128)(2,1)S(1)} %broadcast_select_fusion, bf16[16,56,1152]{2,1,0:T(8,128)(2,1)S(1)} %constant_dynamic-update-slice_fusion), kind=kOutput, calls=%fused_computation.17 | convolution fusion | flops 453869312 | bytes 4916224 | tf_op jit(solution)/shard_map/dot_general | solution.py:90
  38.9 0.5 fusion.13
  39.4 0.5 multiply_reduce_fusion
  39.9 0.2 multiply_convert_fusion
  40.2 0.3 collective-permute-start.16
  40.5 0.3 fusion.64
  40.8 0.3 collective-permute-start.17
  41.1 0.3 fusion.65
  41.4 0.3 fusion.63
  41.7 0.3 fusion.62
  42.0 0.3 fusion.50
  42.3 0.3 convolution_add_fusion.4
  42.7 0.3 convolution_add_fusion
  43.0 0.6 collective-permute-start.22
  43.6 0.3 convolution_add_fusion.2
  44.0 1.6 %collective-permute-start.19 = (bf16[2,56,1152]{2,1,0:T(8,128)(2,1)S(1)}, bf16[2,56,1152]{2,1,0:T(8,128)(2,1)S(1)}, u32[]{:S(2)}, u32[]{:S(2)}) collective-permute-start(bf16[2,56,1152]{2,1,0:T(8,128)(2,1)S(1)} %fusion.19), channel_id=1, source_target_pairs={{0,16},{1,17},{2,18},{3,19},{4,20},{5,21},{6,22},{7,23},{8,9},{9,8... | collective-permute-start | bytes 774152 | tf_op jit(solution)/shard_map/ppermute | solution.py:33
  45.5 0.3 convolution_add_fusion.1
  45.8 0.3 convolution_add_fusion.3
  46.2 3.2 %collective-permute-done.22 = bf16[2,56,1152]{2,1,0:T(8,128)(2,1)S(1)} collective-permute-done((bf16[2,56,1152]{2,1,0:T(8,128)(2,1)S(1)}, bf16[2,56,1152]{2,1,0:T(8,128)(2,1)S(1)}, u32[]{:S(2)}, u32[]{:S(2)}) %collective-permute-start.22) | collective-permute-done | bytes 258080 | tf_op jit(solution)/shard_map/ppermute | solution.py:33
  49.4 0.5 collective-permute-start.23
  50.0 0.9 %collective-permute-start.27 = (bf16[56,1152]{1,0:T(8,128)(2,1)S(1)}, bf16[56,1152]{1,0:T(8,128)(2,1)S(1)}, u32[]{:S(2)}, u32[]{:S(2)}) collective-permute-start(bf16[56,1152]{1,0:T(8,128)(2,1)S(1)} %fusion.45), channel_id=1, source_target_pairs={{0,1},{1,0},{2,3},{3,2},{4,5},{5,4},{6,7},{7,6},{8,24},{9,25},{10,... | collective-permute-start | bytes 387080 | tf_op jit(solution)/shard_map/ppermute | solution.py:33
  50.9 1.6 %collective-permute-done.19 = bf16[2,56,1152]{2,1,0:T(8,128)(2,1)S(1)} collective-permute-done((bf16[2,56,1152]{2,1,0:T(8,128)(2,1)S(1)}, bf16[2,56,1152]{2,1,0:T(8,128)(2,1)S(1)}, u32[]{:S(2)}, u32[]{:S(2)}) %collective-permute-start.19) | collective-permute-done | bytes 258080 | tf_op jit(solution)/shard_map/ppermute | solution.py:33
  52.6 0.3 collective-permute-start.26
  52.9 0.9 %collective-permute-start.20 = (bf16[2,56,1152]{2,1,0:T(8,128)(2,1)S(1)}, bf16[2,56,1152]{2,1,0:T(8,128)(2,1)S(1)}, u32[]{:S(2)}, u32[]{:S(2)}) collective-permute-start(bf16[2,56,1152]{2,1,0:T(8,128)(2,1)S(1)} %fusion.25), channel_id=1, source_target_pairs={{0,16},{1,17},{2,18},{3,19},{4,20},{5,21},{6,22},{7,23},{8,9},{9,8... | collective-permute-start | bytes 774152 | tf_op jit(solution)/shard_map/ppermute | solution.py:33
  53.8 2.7 %collective-permute-done.27 = bf16[56,1152]{1,0:T(8,128)(2,1)S(1)} collective-permute-done((bf16[56,1152]{1,0:T(8,128)(2,1)S(1)}, bf16[56,1152]{1,0:T(8,128)(2,1)S(1)}, u32[]{:S(2)}, u32[]{:S(2)}) %collective-permute-start.27) | collective-permute-done | bytes 129056 | tf_op jit(solution)/shard_map/ppermute | solution.py:33
  56.5 0.4 collective-permute-start.28
  56.9 0.8 %collective-permute-done.23 = bf16[2,56,1152]{2,1,0:T(8,128)(2,1)S(1)} collective-permute-done((bf16[2,56,1152]{2,1,0:T(8,128)(2,1)S(1)}, bf16[2,56,1152]{2,1,0:T(8,128)(2,1)S(1)}, u32[]{:S(2)}, u32[]{:S(2)}) %collective-permute-start.23) | collective-permute-done | bytes 258080 | tf_op jit(solution)/shard_map/ppermute | solution.py:33
  57.8 1.2 %collective-permute-start.24 = (bf16[56,1152]{1,0:T(8,128)(2,1)S(1)}, bf16[56,1152]{1,0:T(8,128)(2,1)S(1)}, u32[]{:S(2)}, u32[]{:S(2)}) collective-permute-start(bf16[56,1152]{1,0:T(8,128)(2,1)S(1)} %fusion.43), channel_id=1, source_target_pairs={{0,1},{1,0},{2,3},{3,2},{4,5},{5,4},{6,7},{7,6},{8,24},{9,25},{10,... | collective-permute-start | bytes 387080 | tf_op jit(solution)/shard_map/ppermute | solution.py:33
  59.0 0.2 collective-permute-done.26
  59.2 2.3 %collective-permute-done.28 = bf16[56,1152]{1,0:T(8,128)(2,1)S(1)} collective-permute-done((bf16[56,1152]{1,0:T(8,128)(2,1)S(1)}, bf16[56,1152]{1,0:T(8,128)(2,1)S(1)}, u32[]{:S(2)}, u32[]{:S(2)}) %collective-permute-start.28) | collective-permute-done | bytes 129056 | tf_op jit(solution)/shard_map/ppermute | solution.py:29
  61.6 0.7 collective-permute-start.29
  62.3 0.9 %collective-permute-start.21 = (bf16[56,1152]{1,0:T(8,128)(2,1)S(1)}, bf16[56,1152]{1,0:T(8,128)(2,1)S(1)}, u32[]{:S(2)}, u32[]{:S(2)}) collective-permute-start(bf16[56,1152]{1,0:T(8,128)(2,1)S(1)} %fusion.42), channel_id=1, source_target_pairs={{0,1},{1,0},{2,3},{3,2},{4,5},{5,4},{6,7},{7,6},{8,24},{9,25},{10,... | collective-permute-start | bytes 387080 | tf_op jit(solution)/shard_map/ppermute | solution.py:33
  63.3 2.1 %collective-permute-start.25 = (bf16[56,1152]{1,0:T(8,128)(2,1)S(1)}, bf16[56,1152]{1,0:T(8,128)(2,1)S(1)}, u32[]{:S(2)}, u32[]{:S(2)}) collective-permute-start(bf16[56,1152]{1,0:T(8,128)(2,1)S(1)} %fusion.32), channel_id=1, source_target_pairs={{0,2},{1,3},{2,0},{3,1},{4,6},{5,7},{6,4},{7,5},{8,10},{9,11},{10,... | collective-permute-start | bytes 387080 | tf_op jit(solution)/shard_map/ppermute | solution.py:29
  65.5 3.4 %collective-permute-done.29 = bf16[56,1152]{1,0:T(8,128)(2,1)S(1)} collective-permute-done((bf16[56,1152]{1,0:T(8,128)(2,1)S(1)}, bf16[56,1152]{1,0:T(8,128)(2,1)S(1)}, u32[]{:S(2)}, u32[]{:S(2)}) %collective-permute-start.29) | collective-permute-done | bytes 129056 | tf_op jit(solution)/shard_map/ppermute | solution.py:29
  68.9 0.5 collective-permute-done.25
  69.5 1.0 %collective-permute-start.31 = (f32[8,1152]{1,0:T(8,128)S(1)}, f32[8,1152]{1,0:T(8,128)S(1)}, u32[]{:S(2)}, u32[]{:S(2)}) collective-permute-start(f32[8,1152]{1,0:T(8,128)S(1)} %slice.216), channel_id=1, source_target_pairs={{0,16},{1,17},{2,18},{3,19},{4,20},{5,21},{6,22},{7,23},{8,24},{9,... | collective-permute-start | bytes 110600 | tf_op jit(solution)/shard_map/ppermute | solution.py:29
  70.6 0.8 %collective-permute-start.32 = (f32[8,1152]{1,0:T(8,128)S(1)}, f32[8,1152]{1,0:T(8,128)S(1)}, u32[]{:S(2)}, u32[]{:S(2)}) collective-permute-start(f32[8,1152]{1,0:T(8,128)S(1)} %slice.216), channel_id=1, source_target_pairs={{0,8},{1,9},{2,10},{3,11},{4,12},{5,13},{6,14},{7,15},{8,0},{9,1},... | collective-permute-start | bytes 110600 | tf_op jit(solution)/shard_map/ppermute | solution.py:29
  71.4 0.7 slice.215
  72.1 0.8 %collective-permute-done.30 = f32[8,1152]{1,0:T(8,128)S(1)} collective-permute-done((f32[8,1152]{1,0:T(8,128)S(1)}, f32[8,1152]{1,0:T(8,128)S(1)}, u32[]{:S(2)}, u32[]{:S(2)}) %collective-permute-start.30) | collective-permute-done | bytes 36896 | tf_op jit(solution)/shard_map/ppermute | solution.py:29
  72.9 1.0 %collective-permute-done.31 = f32[8,1152]{1,0:T(8,128)S(1)} collective-permute-done((f32[8,1152]{1,0:T(8,128)S(1)}, f32[8,1152]{1,0:T(8,128)S(1)}, u32[]{:S(2)}, u32[]{:S(2)}) %collective-permute-start.31) | collective-permute-done | bytes 36896 | tf_op jit(solution)/shard_map/ppermute | solution.py:29
  74.1 0.8 %fusion.40 = f32[32,1152]{1,0:T(8,128)} fusion(bf16[32,1152]{1,0:T(8,128)(2,1)S(1)} %copy-done, f32[8,1152]{1,0:T(8,128)S(1)} %get-tuple-element.19, f32[8,1152]{1,0:T(8,128)S(1)} %get-tuple-element.20, f32[8,1152]{1,0:T(8,128)S(1)} %get-tuple-element.21, f32[8,1152]{1,0:T(8,128)S(1)} %get-tuple-element.18, f32[32]{0:T(128)S(1)} %fusion.38, ...), kind=kLoop, calls=%fused_computation.89 | loop fusion | flops 294912 | bytes 368896 | tf_op jit(solution)/shard_map/mul | solution.py:158
  (94 shorter events, 3.7 us)
Async XLA Ops:
  2.3 10.0 %collective-permute-start = (bf16[1,56,1152]{2,1,0:T(8,128)(2,1)S(1)}, bf16[1,56,1152]{2,1,0:T(8,128)(2,1)S(1)}, u32[]{:S(2)}, u32[]{:S(2)}) collective-permute-start(bf16[1,56,1152]{2,1,0:T(8,128)(2,1)S(1)} %maximum_bitcast_fusion), channel_id=1, source_target_pairs={{0,1},{1,0},{2,3},{3,2},{4,5},{5,4},{6,7},{7,6},{8,24},{9,25},{10,... | collective-permute-start | bytes 387080 | tf_op jit(solution)/shard_map/ppermute | solution.py:33
  5.3 8.6 %collective-permute-start.2 = (bf16[1,56,1152]{2,1,0:T(8,128)(2,1)S(1)}, bf16[1,56,1152]{2,1,0:T(8,128)(2,1)S(1)}, u32[]{:S(2)}, u32[]{:S(2)}) collective-permute-start(bf16[1,56,1152]{2,1,0:T(8,128)(2,1)S(1)} %maximum_bitcast_fusion), channel_id=1, source_target_pairs={{0,2},{1,3},{2,0},{3,1},{4,6},{5,7},{6,4},{7,5},{8,10},{9,11},{10,... | collective-permute-start | bytes 387080 | tf_op jit(solution)/shard_map/ppermute | solution.py:29
  6.9 8.4 %collective-permute-start.5 = (bf16[1,56,1152]{2,1,0:T(8,128)(2,1)S(1)}, bf16[1,56,1152]{2,1,0:T(8,128)(2,1)S(1)}, u32[]{:S(2)}, u32[]{:S(2)}) collective-permute-start(bf16[1,56,1152]{2,1,0:T(8,128)(2,1)S(1)} %maximum_bitcast_fusion), channel_id=1, source_target_pairs={{0,4},{1,5},{2,6},{3,7},{4,0},{5,1},{6,2},{7,3},{8,12},{9,13},{10,... | collective-permute-start | bytes 387080 | tf_op jit(solution)/shard_map/ppermute | solution.py:29
  11.0 1.2 %copy-start.1 = (bf16[48,1152]{1,0:T(8,128)(2,1)S(1)}, bf16[48,1152]{1,0:T(8,128)(2,1)}, u32[]{:S(2)}) copy-start(bf16[48,1152]{1,0:T(8,128)(2,1)} %param.5) | copy-start | bytes 331780
  11.9 30.8 %collective-permute-start.15 = (bf16[768,256]{1,0:T(8,128)(2,1)S(1)}, bf16[768,256]{1,0:T(8,128)(2,1)S(1)}, u32[]{:S(2)}, u32[]{:S(2)}) collective-permute-start(bf16[768,256]{1,0:T(8,128)(2,1)S(1)} %bitcast.108), channel_id=1, source_target_pairs={{0,8},{1,9},{2,10},{3,11},{4,12},{5,13},{6,14},{7,15},{8,0},{9,1},... | collective-permute-start | bytes 1179656 | tf_op jit(solution)/shard_map/ppermute | solution.py:29
  12.3 16.3 %collective-permute-start.1 = (bf16[2,56,1152]{2,1,0:T(8,128)(2,1)S(1)}, bf16[2,56,1152]{2,1,0:T(8,128)(2,1)S(1)}, u32[]{:S(2)}, u32[]{:S(2)}) collective-permute-start(bf16[2,56,1152]{2,1,0:T(8,128)(2,1)S(1)} %pad_maximum_fusion.9), channel_id=1, source_target_pairs={{0,16},{1,17},{2,18},{3,19},{4,20},{5,21},{6,22},{7,23},{8,9},{9,8... | collective-permute-start | bytes 774152 | tf_op jit(solution)/shard_map/ppermute | solution.py:33
  13.9 5.7 %collective-permute-start.3 = (bf16[1,56,1152]{2,1,0:T(8,128)(2,1)S(1)}, bf16[1,56,1152]{2,1,0:T(8,128)(2,1)S(1)}, u32[]{:S(2)}, u32[]{:S(2)}) collective-permute-start(bf16[1,56,1152]{2,1,0:T(8,128)(2,1)S(1)} %collective-permute-done.2), channel_id=1, source_target_pairs={{0,1},{1,0},{2,3},{3,2},{4,5},{5,4},{6,7},{7,6},{8,24},{9,25},{10,... | collective-permute-start | bytes 387080 | tf_op jit(solution)/shard_map/ppermute | solution.py:33
  15.2 7.0 %collective-permute-start.6 = (bf16[1,56,1152]{2,1,0:T(8,128)(2,1)S(1)}, bf16[1,56,1152]{2,1,0:T(8,128)(2,1)S(1)}, u32[]{:S(2)}, u32[]{:S(2)}) collective-permute-start(bf16[1,56,1152]{2,1,0:T(8,128)(2,1)S(1)} %collective-permute-done.5), channel_id=1, source_target_pairs={{0,1},{1,0},{2,3},{3,2},{4,5},{5,4},{6,7},{7,6},{8,24},{9,25},{10,... | collective-permute-start | bytes 387080 | tf_op jit(solution)/shard_map/ppermute | solution.py:33
  16.7 4.9 %collective-permute-start.8 = (bf16[1,56,1152]{2,1,0:T(8,128)(2,1)S(1)}, bf16[1,56,1152]{2,1,0:T(8,128)(2,1)S(1)}, u32[]{:S(2)}, u32[]{:S(2)}) collective-permute-start(bf16[1,56,1152]{2,1,0:T(8,128)(2,1)S(1)} %collective-permute-done.5), channel_id=1, source_target_pairs={{0,2},{1,3},{2,0},{3,1},{4,6},{5,7},{6,4},{7,5},{8,10},{9,11},{10,... | collective-permute-start | bytes 387080 | tf_op jit(solution)/shard_map/ppermute | solution.py:29
  19.7 9.2 %collective-permute-start.4 = (bf16[2,56,1152]{2,1,0:T(8,128)(2,1)S(1)}, bf16[2,56,1152]{2,1,0:T(8,128)(2,1)S(1)}, u32[]{:S(2)}, u32[]{:S(2)}) collective-permute-start(bf16[2,56,1152]{2,1,0:T(8,128)(2,1)S(1)} %pad_maximum_fusion.10), channel_id=1, source_target_pairs={{0,16},{1,17},{2,18},{3,19},{4,20},{5,21},{6,22},{7,23},{8,9},{9,8... | collective-permute-start | bytes 774152 | tf_op jit(solution)/shard_map/ppermute | solution.py:33
  21.7 6.4 %collective-permute-start.9 = (bf16[1,56,1152]{2,1,0:T(8,128)(2,1)S(1)}, bf16[1,56,1152]{2,1,0:T(8,128)(2,1)S(1)}, u32[]{:S(2)}, u32[]{:S(2)}) collective-permute-start(bf16[1,56,1152]{2,1,0:T(8,128)(2,1)S(1)} %collective-permute-done.8), channel_id=1, source_target_pairs={{0,1},{1,0},{2,3},{3,2},{4,5},{5,4},{6,7},{7,6},{8,24},{9,25},{10,... | collective-permute-start | bytes 387080 | tf_op jit(solution)/shard_map/ppermute | solution.py:33
  22.2 7.3 %collective-permute-start.7 = (bf16[2,56,1152]{2,1,0:T(8,128)(2,1)S(1)}, bf16[2,56,1152]{2,1,0:T(8,128)(2,1)S(1)}, u32[]{:S(2)}, u32[]{:S(2)}) collective-permute-start(bf16[2,56,1152]{2,1,0:T(8,128)(2,1)S(1)} %pad_maximum_fusion.11), channel_id=1, source_target_pairs={{0,16},{1,17},{2,18},{3,19},{4,20},{5,21},{6,22},{7,23},{8,9},{9,8... | collective-permute-start | bytes 774152 | tf_op jit(solution)/shard_map/ppermute | solution.py:33
  28.1 6.4 %collective-permute-start.10 = (bf16[2,56,1152]{2,1,0:T(8,128)(2,1)S(1)}, bf16[2,56,1152]{2,1,0:T(8,128)(2,1)S(1)}, u32[]{:S(2)}, u32[]{:S(2)}) collective-permute-start(bf16[2,56,1152]{2,1,0:T(8,128)(2,1)S(1)} %pad_maximum_fusion.12), channel_id=1, source_target_pairs={{0,16},{1,17},{2,18},{3,19},{4,20},{5,21},{6,22},{7,23},{8,9},{9,8... | collective-permute-start | bytes 774152 | tf_op jit(solution)/shard_map/ppermute | solution.py:33
  28.7 6.0 %collective-permute-start.11 = (bf16[4,56,1152]{2,1,0:T(8,128)(2,1)S(1)}, bf16[4,56,1152]{2,1,0:T(8,128)(2,1)S(1)}, u32[]{:S(2)}, u32[]{:S(2)}) collective-permute-start(bf16[4,56,1152]{2,1,0:T(8,128)(2,1)S(1)} %pad_maximum_fusion.5), channel_id=1, source_target_pairs={{0,8},{1,9},{2,10},{3,11},{4,12},{5,13},{6,14},{7,15},{8,0},{9,1},... | collective-permute-start | bytes 1548296 | tf_op jit(solution)/shard_map/ppermute | solution.py:29
  29.0 5.8 %collective-permute-start.12 = (bf16[4,56,1152]{2,1,0:T(8,128)(2,1)S(1)}, bf16[4,56,1152]{2,1,0:T(8,128)(2,1)S(1)}, u32[]{:S(2)}, u32[]{:S(2)}) collective-permute-start(bf16[4,56,1152]{2,1,0:T(8,128)(2,1)S(1)} %pad_maximum_fusion.6), channel_id=1, source_target_pairs={{0,8},{1,9},{2,10},{3,11},{4,12},{5,13},{6,14},{7,15},{8,0},{9,1},... | collective-permute-start | bytes 1548296 | tf_op jit(solution)/shard_map/ppermute | solution.py:29
  29.6 5.2 %collective-permute-start.13 = (bf16[4,56,1152]{2,1,0:T(8,128)(2,1)S(1)}, bf16[4,56,1152]{2,1,0:T(8,128)(2,1)S(1)}, u32[]{:S(2)}, u32[]{:S(2)}) collective-permute-start(bf16[4,56,1152]{2,1,0:T(8,128)(2,1)S(1)} %pad_maximum_fusion.7), channel_id=1, source_target_pairs={{0,8},{1,9},{2,10},{3,11},{4,12},{5,13},{6,14},{7,15},{8,0},{9,1},... | collective-permute-start | bytes 1548296 | tf_op jit(solution)/shard_map/ppermute | solution.py:29
  34.6 2.0 %collective-permute-start.14 = (bf16[4,56,1152]{2,1,0:T(8,128)(2,1)S(1)}, bf16[4,56,1152]{2,1,0:T(8,128)(2,1)S(1)}, u32[]{:S(2)}, u32[]{:S(2)}) collective-permute-start(bf16[4,56,1152]{2,1,0:T(8,128)(2,1)S(1)} %pad_maximum_fusion.8), channel_id=1, source_target_pairs={{0,8},{1,9},{2,10},{3,11},{4,12},{5,13},{6,14},{7,15},{8,0},{9,1},... | collective-permute-start | bytes 1548296 | tf_op jit(solution)/shard_map/ppermute | solution.py:29
  38.2 0.7 copy-start.2
  38.6 3.8 %collective-permute-start.18 = (bf16[256,1152]{1,0:T(8,128)(2,1)S(1)}, bf16[256,1152]{1,0:T(8,128)(2,1)S(1)}, u32[]{:S(2)}, u32[]{:S(2)}) collective-permute-start(bf16[256,1152]{1,0:T(8,128)(2,1)S(1)} %multiply_convert_fusion.1), channel_id=1, source_target_pairs={{0,8},{1,9},{2,10},{3,11},{4,12},{5,13},{6,14},{7,15},{8,0},{9,1},... | collective-permute-start | bytes 1769480 | tf_op jit(solution)/shard_map/ppermute | solution.py:29
  40.2 2.5 %collective-permute-start.16 = (bf16[256,1152]{1,0:T(8,128)(2,1)S(1)}, bf16[256,1152]{1,0:T(8,128)(2,1)S(1)}, u32[]{:S(2)}, u32[]{:S(2)}) collective-permute-start(bf16[256,1152]{1,0:T(8,128)(2,1)S(1)} %multiply_convert_fusion), channel_id=1, source_target_pairs={{0,8},{1,9},{2,10},{3,11},{4,12},{5,13},{6,14},{7,15},{8,0},{9,1},... | collective-permute-start | bytes 1769480 | tf_op jit(solution)/shard_map/ppermute | solution.py:29
  40.8 1.5 %collective-permute-start.17 = (bf16[256,128]{1,0:T(8,128)(2,1)S(1)}, bf16[256,128]{1,0:T(8,128)(2,1)S(1)}, u32[]{:S(2)}, u32[]{:S(2)}) collective-permute-start(bf16[256,128]{1,0:T(8,128)(2,1)S(1)} %slice.188), channel_id=1, source_target_pairs={{0,8},{1,9},{2,10},{3,11},{4,12},{5,13},{6,14},{7,15},{8,0},{9,1},... | collective-permute-start | bytes 196616 | tf_op jit(solution)/shard_map/ppermute | solution.py:29
  43.0 6.4 %collective-permute-start.22 = (bf16[2,56,1152]{2,1,0:T(8,128)(2,1)S(1)}, bf16[2,56,1152]{2,1,0:T(8,128)(2,1)S(1)}, u32[]{:S(2)}, u32[]{:S(2)}) collective-permute-start(bf16[2,56,1152]{2,1,0:T(8,128)(2,1)S(1)} %fusion.15), channel_id=1, source_target_pairs={{0,16},{1,17},{2,18},{3,19},{4,20},{5,21},{6,22},{7,23},{8,9},{9,8... | collective-permute-start | bytes 774152 | tf_op jit(solution)/shard_map/ppermute | solution.py:33
  44.0 8.5 %collective-permute-start.19 = (bf16[2,56,1152]{2,1,0:T(8,128)(2,1)S(1)}, bf16[2,56,1152]{2,1,0:T(8,128)(2,1)S(1)}, u32[]{:S(2)}, u32[]{:S(2)}) collective-permute-start(bf16[2,56,1152]{2,1,0:T(8,128)(2,1)S(1)} %fusion.19), channel_id=1, source_target_pairs={{0,16},{1,17},{2,18},{3,19},{4,20},{5,21},{6,22},{7,23},{8,9},{9,8... | collective-permute-start | bytes 774152 | tf_op jit(solution)/shard_map/ppermute | solution.py:33
  49.4 8.3 %collective-permute-start.23 = (bf16[2,56,1152]{2,1,0:T(8,128)(2,1)S(1)}, bf16[2,56,1152]{2,1,0:T(8,128)(2,1)S(1)}, u32[]{:S(2)}, u32[]{:S(2)}) collective-permute-start(bf16[2,56,1152]{2,1,0:T(8,128)(2,1)S(1)} %fusion.24), channel_id=1, source_target_pairs={{0,16},{1,17},{2,18},{3,19},{4,20},{5,21},{6,22},{7,23},{8,9},{9,8... | collective-permute-start | bytes 774152 | tf_op jit(solution)/shard_map/ppermute | solution.py:33
  50.0 6.5 %collective-permute-start.27 = (bf16[56,1152]{1,0:T(8,128)(2,1)S(1)}, bf16[56,1152]{1,0:T(8,128)(2,1)S(1)}, u32[]{:S(2)}, u32[]{:S(2)}) collective-permute-start(bf16[56,1152]{1,0:T(8,128)(2,1)S(1)} %fusion.45), channel_id=1, source_target_pairs={{0,1},{1,0},{2,3},{3,2},{4,5},{5,4},{6,7},{7,6},{8,24},{9,25},{10,... | collective-permute-start | bytes 387080 | tf_op jit(solution)/shard_map/ppermute | solution.py:33
  52.6 6.7 %collective-permute-start.26 = (bf16[56,1152]{1,0:T(8,128)(2,1)S(1)}, bf16[56,1152]{1,0:T(8,128)(2,1)S(1)}, u32[]{:S(2)}, u32[]{:S(2)}) collective-permute-start(bf16[56,1152]{1,0:T(8,128)(2,1)S(1)} %fusion.44), channel_id=1, source_target_pairs={{0,1},{1,0},{2,3},{3,2},{4,5},{5,4},{6,7},{7,6},{8,24},{9,25},{10,... | collective-permute-start | bytes 387080 | tf_op jit(solution)/shard_map/ppermute | solution.py:33
  52.9 9.4 %collective-permute-start.20 = (bf16[2,56,1152]{2,1,0:T(8,128)(2,1)S(1)}, bf16[2,56,1152]{2,1,0:T(8,128)(2,1)S(1)}, u32[]{:S(2)}, u32[]{:S(2)}) collective-permute-start(bf16[2,56,1152]{2,1,0:T(8,128)(2,1)S(1)} %fusion.25), channel_id=1, source_target_pairs={{0,16},{1,17},{2,18},{3,19},{4,20},{5,21},{6,22},{7,23},{8,9},{9,8... | collective-permute-start | bytes 774152 | tf_op jit(solution)/shard_map/ppermute | solution.py:33
  56.5 5.0 %collective-permute-start.28 = (bf16[56,1152]{1,0:T(8,128)(2,1)S(1)}, bf16[56,1152]{1,0:T(8,128)(2,1)S(1)}, u32[]{:S(2)}, u32[]{:S(2)}) collective-permute-start(bf16[56,1152]{1,0:T(8,128)(2,1)S(1)} %fusion.27), channel_id=1, source_target_pairs={{0,2},{1,3},{2,0},{3,1},{4,6},{5,7},{6,4},{7,5},{8,10},{9,11},{10,... | collective-permute-start | bytes 387080 | tf_op jit(solution)/shard_map/ppermute | solution.py:29
  57.8 7.6 %copy-start = (bf16[32,1152]{1,0:T(8,128)(2,1)S(1)}, bf16[32,1152]{1,0:T(8,128)(2,1)}, u32[]{:S(2)}) copy-start(bf16[32,1152]{1,0:T(8,128)(2,1)} %param.7) | copy-start | bytes 221188
  57.8 5.4 %collective-permute-start.24 = (bf16[56,1152]{1,0:T(8,128)(2,1)S(1)}, bf16[56,1152]{1,0:T(8,128)(2,1)S(1)}, u32[]{:S(2)}, u32[]{:S(2)}) collective-permute-start(bf16[56,1152]{1,0:T(8,128)(2,1)S(1)} %fusion.43), channel_id=1, source_target_pairs={{0,1},{1,0},{2,3},{3,2},{4,5},{5,4},{6,7},{7,6},{8,24},{9,25},{10,... | collective-permute-start | bytes 387080 | tf_op jit(solution)/shard_map/ppermute | solution.py:33
  61.6 7.3 %collective-permute-start.29 = (bf16[56,1152]{1,0:T(8,128)(2,1)S(1)}, bf16[56,1152]{1,0:T(8,128)(2,1)S(1)}, u32[]{:S(2)}, u32[]{:S(2)}) collective-permute-start(bf16[56,1152]{1,0:T(8,128)(2,1)S(1)} %fusion.30), channel_id=1, source_target_pairs={{0,4},{1,5},{2,6},{3,7},{4,0},{5,1},{6,2},{7,3},{8,12},{9,13},{10,... | collective-permute-start | bytes 387080 | tf_op jit(solution)/shard_map/ppermute | solution.py:29
  62.3 6.5 %collective-permute-start.21 = (bf16[56,1152]{1,0:T(8,128)(2,1)S(1)}, bf16[56,1152]{1,0:T(8,128)(2,1)S(1)}, u32[]{:S(2)}, u32[]{:S(2)}) collective-permute-start(bf16[56,1152]{1,0:T(8,128)(2,1)S(1)} %fusion.42), channel_id=1, source_target_pairs={{0,1},{1,0},{2,3},{3,2},{4,5},{5,4},{6,7},{7,6},{8,24},{9,25},{10,... | collective-permute-start | bytes 387080 | tf_op jit(solution)/shard_map/ppermute | solution.py:33
  63.3 6.1 %collective-permute-start.25 = (bf16[56,1152]{1,0:T(8,128)(2,1)S(1)}, bf16[56,1152]{1,0:T(8,128)(2,1)S(1)}, u32[]{:S(2)}, u32[]{:S(2)}) collective-permute-start(bf16[56,1152]{1,0:T(8,128)(2,1)S(1)} %fusion.32), channel_id=1, source_target_pairs={{0,2},{1,3},{2,0},{3,1},{4,6},{5,7},{6,4},{7,5},{8,10},{9,11},{10,... | collective-permute-start | bytes 387080 | tf_op jit(solution)/shard_map/ppermute | solution.py:29
  69.5 3.4 %collective-permute-start.30 = (f32[8,1152]{1,0:T(8,128)S(1)}, f32[8,1152]{1,0:T(8,128)S(1)}, u32[]{:S(2)}, u32[]{:S(2)}) collective-permute-start(f32[8,1152]{1,0:T(8,128)S(1)} %slice.216), channel_id=1, source_target_pairs={{0,24},{1,25},{2,26},{3,27},{4,28},{5,29},{6,30},{7,31},{8,16},{9,... | collective-permute-start | bytes 110600 | tf_op jit(solution)/shard_map/ppermute | solution.py:29
  69.5 4.4 %collective-permute-start.31 = (f32[8,1152]{1,0:T(8,128)S(1)}, f32[8,1152]{1,0:T(8,128)S(1)}, u32[]{:S(2)}, u32[]{:S(2)}) collective-permute-start(f32[8,1152]{1,0:T(8,128)S(1)} %slice.216), channel_id=1, source_target_pairs={{0,16},{1,17},{2,18},{3,19},{4,20},{5,21},{6,22},{7,23},{8,24},{9,... | collective-permute-start | bytes 110600 | tf_op jit(solution)/shard_map/ppermute | solution.py:29
  70.6 3.3 %collective-permute-start.32 = (f32[8,1152]{1,0:T(8,128)S(1)}, f32[8,1152]{1,0:T(8,128)S(1)}, u32[]{:S(2)}, u32[]{:S(2)}) collective-permute-start(f32[8,1152]{1,0:T(8,128)S(1)} %slice.216), channel_id=1, source_target_pairs={{0,8},{1,9},{2,10},{3,11},{4,12},{5,13},{6,14},{7,15},{8,0},{9,1},... | collective-permute-start | bytes 110600 | tf_op jit(solution)/shard_map/ppermute | solution.py:29

commit v6 on v5

--- a/solution.py
+++ b/solution.py
@@ -59,7 +59,10 @@
                 block = after(block, firsts[0])
             if kz == 2:
                 block = after(block, by_z[1])
-            firsts.append(first(block))
+            if kz % 2 and kz > 1:
+                firsts.append(swap(firsts[kz - 1], 2))
+            else:
+                firsts.append(first(block))
             pair = jnp.concatenate([by_z[kz], firsts[kz]], axis=0)
             quads.append(jnp.concatenate([pair, second(pair)], axis=0))
         gathered = [
@@ -79,7 +82,7 @@
         turned = pooled.T.reshape(devices, rows, images)
         columns = jnp.take(turned, sources, axis=0).reshape(2, -1, images)
         mine, other = columns[0], columns[1]
-        theirs = swap(other, core_mask)
+        theirs = swap(after(other, firsts[2]), core_mask)
 
         text_all = jnp.concatenate([g[:, rows:].reshape(-1, embed) for g in gathered], axis=0)
         text_all = unit_rows(text_all.astype(F32))[0].astype(BF16)

time: 75.2 us -> 73.1 us (0.972)
  waiting for transfers between devices: 31.9 us -> 26.4 us
  starting transfers between devices: 28 us -> 31.4 us
    ppermute x16 -> x15, waiting for transfers between devices: 20.6 us -> 13.4 us  [swap_by_core(): return lax.ppermute(array, axes, pairs)]
    ppermute x16 -> x15, starting transfers between devices: 16.6 us -> 19.6 us  [swap_by_core(): return lax.ppermute(array, axes, pairs)]
    ppermute x17 -> x18, waiting for transfers between devices: 11.3 us -> 13 us  [swap(): return lax.ppermute(array, axes, [(i, i ^ mask) for i in range(devices)])]
    ppermute x17 -> x18, starting transfers between devices: 11.4 us -> 11.8 us  [swap(): return lax.ppermute(array, axes, [(i, i ^ mask) for i in range(devices)])]
  transfers between devices with their start and end apart: 33 -> 33, of which waited for: 16 -> 17; matrix products, arithmetic and copies ran while one was open for 14% -> 15% of each run, Pallas kernels for 0% -> 0%
where the time goes in v6:
time: 73.1 us; the launch traced here: 72.8 us
  starting transfers between devices  31.4 us (43%)
  waiting for transfers between devices  26.4 us (36%)
  matrix products  5.47 us (7%)
  local copies, waits for them, and re-layouts  4.33 us (6%)
  other arithmetic  4.04 us (6%)
  between operations  1.16 us (2%)
    ppermute x15, starting transfers between devices, swap_by_core(): return lax.ppermute(array, axes, pairs)  19.6 us
    ppermute x15, waiting for transfers between devices, swap_by_core(): return lax.ppermute(array, axes, pairs)  13.4 us
    ppermute x18, waiting for transfers between devices, swap(): return lax.ppermute(array, axes, [(i, i ^ mask) for i in range(devices)])  13 us
    ppermute x18, starting transfers between devices, swap(): return lax.ppermute(array, axes, [(i, i ^ mask) for i in range(devices)])  11.8 us
    unnamed x20, local copies, waits for them, and re-layouts  1.9 us
    dot_general x2, matrix products, partly(): lax.dot_general(column, found[:, :rows].reshape(-1, embed), (((0,), (0,))...  1.51 us
  transfers between devices with their start and end apart: 33, of which 17 were waited for; matrix products, arithmetic and copies ran while one was open for 15% of the time, Pallas kernels for 0%

profile of v6, /device:TPU:0, one launch (start us, length us, event | category | flops | bytes accessed | tf_op | source)
XLA Modules:
  0.0 72.8 jit_solution(13651593055085219095)
XLA Ops:
  0.6 0.7 %constant_dynamic-slice_fusion = bf16[8,1152]{1,0:T(8,128)(2,1)S(1)} fusion(bf16[32,1152]{1,0:T(8,128)(2,1)} %param.7, s32[]{:T(128)S(6)} %select_n.307), kind=kLoop, calls=%fused_computation.158 | loop fusion | bytes 36868 | tf_op jit(solution)/shard_map/dynamic_slice | solution.py:51
  1.4 0.9 %maximum_bitcast_fusion = bf16[1,56,1152]{2,1,0:T(8,128)(2,1)S(1)} fusion(bf16[8,1152]{1,0:T(8,128)(2,1)S(1)} %constant_dynamic-slice_fusion, bf16[48,1152]{1,0:T(8,128)(2,1)} %param.5), kind=kLoop, calls=%fused_computation.100 | loop fusion | flops 258048 | bytes 258048 | tf_op jit(solution)/shard_map/broadcast_in_dim | solution.py:50
  2.3 3.0 %collective-permute-start = (bf16[1,56,1152]{2,1,0:T(8,128)(2,1)S(1)}, bf16[1,56,1152]{2,1,0:T(8,128)(2,1)S(1)}, u32[]{:S(2)}, u32[]{:S(2)}) collective-permute-start(bf16[1,56,1152]{2,1,0:T(8,128)(2,1)S(1)} %maximum_bitcast_fusion), channel_id=1, source_target_pairs={{0,1},{1,0},{2,3},{3,2},{4,5},{5,4},{6,7},{7,6},{8,24},{9,25},{10,... | collective-permute-start | bytes 387080 | tf_op jit(solution)/shard_map/ppermute | solution.py:33
  5.3 1.6 %collective-permute-start.2 = (bf16[1,56,1152]{2,1,0:T(8,128)(2,1)S(1)}, bf16[1,56,1152]{2,1,0:T(8,128)(2,1)S(1)}, u32[]{:S(2)}, u32[]{:S(2)}) collective-permute-start(bf16[1,56,1152]{2,1,0:T(8,128)(2,1)S(1)} %maximum_bitcast_fusion), channel_id=1, source_target_pairs={{0,2},{1,3},{2,0},{3,1},{4,6},{5,7},{6,4},{7,5},{8,10},{9,11},{10,... | collective-permute-start | bytes 387080 | tf_op jit(solution)/shard_map/ppermute | solution.py:29
  6.9 2.6 %collective-permute-start.5 = (bf16[1,56,1152]{2,1,0:T(8,128)(2,1)S(1)}, bf16[1,56,1152]{2,1,0:T(8,128)(2,1)S(1)}, u32[]{:S(2)}, u32[]{:S(2)}) collective-permute-start(bf16[1,56,1152]{2,1,0:T(8,128)(2,1)S(1)} %maximum_bitcast_fusion), channel_id=1, source_target_pairs={{0,4},{1,5},{2,6},{3,7},{4,0},{5,1},{6,2},{7,3},{8,12},{9,13},{10,... | collective-permute-start | bytes 387080 | tf_op jit(solution)/shard_map/ppermute | solution.py:29
  9.8 1.4 %copy.6 = bf16[256,1536]{0,1:T(8,128)(2,1)S(1)} copy(bf16[256,1536]{1,0:T(8,128)(2,1)} %param.4) | data formatting | bytes 1572864 | tf_op args[0]
  11.2 0.6 gather_fusion
  12.2 1.6 %collective-permute-start.1 = (bf16[2,56,1152]{2,1,0:T(8,128)(2,1)S(1)}, bf16[2,56,1152]{2,1,0:T(8,128)(2,1)S(1)}, u32[]{:S(2)}, u32[]{:S(2)}) collective-permute-start(bf16[2,56,1152]{2,1,0:T(8,128)(2,1)S(1)} %pad_maximum_fusion.9), channel_id=1, source_target_pairs={{0,16},{1,17},{2,18},{3,19},{4,20},{5,21},{6,22},{7,23},{8,9},{9,8... | collective-permute-start | bytes 774152 | tf_op jit(solution)/shard_map/ppermute | solution.py:33
  13.8 0.5 collective-permute-start.3
  14.4 0.9 %collective-permute-done.5 = bf16[1,56,1152]{2,1,0:T(8,128)(2,1)S(1)} collective-permute-done((bf16[1,56,1152]{2,1,0:T(8,128)(2,1)S(1)}, bf16[1,56,1152]{2,1,0:T(8,128)(2,1)S(1)}, u32[]{:S(2)}, u32[]{:S(2)}) %collective-permute-start.5) | collective-permute-done | bytes 129056 | tf_op jit(solution)/shard_map/ppermute | solution.py:29
  15.2 1.5 %collective-permute-start.6 = (bf16[1,56,1152]{2,1,0:T(8,128)(2,1)S(1)}, bf16[1,56,1152]{2,1,0:T(8,128)(2,1)S(1)}, u32[]{:S(2)}, u32[]{:S(2)}) collective-permute-start(bf16[1,56,1152]{2,1,0:T(8,128)(2,1)S(1)} %collective-permute-done.5), channel_id=1, source_target_pairs={{0,1},{1,0},{2,3},{3,2},{4,5},{5,4},{6,7},{7,6},{8,24},{9,25},{10,... | collective-permute-start | bytes 387080 | tf_op jit(solution)/shard_map/ppermute | solution.py:33
  16.7 0.4 collective-permute-start.8
  17.2 1.6 %collective-permute-done.3 = bf16[1,56,1152]{2,1,0:T(8,128)(2,1)S(1)} collective-permute-done((bf16[1,56,1152]{2,1,0:T(8,128)(2,1)S(1)}, bf16[1,56,1152]{2,1,0:T(8,128)(2,1)S(1)}, u32[]{:S(2)}, u32[]{:S(2)}) %collective-permute-start.3) | collective-permute-done | bytes 129056 | tf_op jit(solution)/shard_map/ppermute | solution.py:33
  18.8 0.6 collective-permute-start.4
  19.4 0.8 %collective-permute-done.6 = bf16[1,56,1152]{2,1,0:T(8,128)(2,1)S(1)} collective-permute-done((bf16[1,56,1152]{2,1,0:T(8,128)(2,1)S(1)}, bf16[1,56,1152]{2,1,0:T(8,128)(2,1)S(1)}, u32[]{:S(2)}, u32[]{:S(2)}) %collective-permute-start.6) | collective-permute-done | bytes 129056 | tf_op jit(solution)/shard_map/ppermute | solution.py:33
  20.2 0.5 collective-permute-start.9
  20.7 1.7 %collective-permute-start.7 = (bf16[2,56,1152]{2,1,0:T(8,128)(2,1)S(1)}, bf16[2,56,1152]{2,1,0:T(8,128)(2,1)S(1)}, u32[]{:S(2)}, u32[]{:S(2)}) collective-permute-start(bf16[2,56,1152]{2,1,0:T(8,128)(2,1)S(1)} %pad_maximum_fusion.11), channel_id=1, source_target_pairs={{0,16},{1,17},{2,18},{3,19},{4,20},{5,21},{6,22},{7,23},{8,9},{9,8... | collective-permute-start | bytes 774152 | tf_op jit(solution)/shard_map/ppermute | solution.py:33
  22.4 3.0 %collective-permute-done.9 = bf16[1,56,1152]{2,1,0:T(8,128)(2,1)S(1)} collective-permute-done((bf16[1,56,1152]{2,1,0:T(8,128)(2,1)S(1)}, bf16[1,56,1152]{2,1,0:T(8,128)(2,1)S(1)}, u32[]{:S(2)}, u32[]{:S(2)}) %collective-permute-start.9) | collective-permute-done | bytes 129056 | tf_op jit(solution)/shard_map/ppermute | solution.py:29
  25.5 0.5 collective-permute-start.10
  26.0 0.9 %collective-permute-start.11 = (bf16[4,56,1152]{2,1,0:T(8,128)(2,1)S(1)}, bf16[4,56,1152]{2,1,0:T(8,128)(2,1)S(1)}, u32[]{:S(2)}, u32[]{:S(2)}) collective-permute-start(bf16[4,56,1152]{2,1,0:T(8,128)(2,1)S(1)} %pad_maximum_fusion.5), channel_id=1, source_target_pairs={{0,8},{1,9},{2,10},{3,11},{4,12},{5,13},{6,14},{7,15},{8,0},{9,1},... | collective-permute-start | bytes 1548296 | tf_op jit(solution)/shard_map/ppermute | solution.py:29
  27.2 0.8 %collective-permute-done.7 = bf16[2,56,1152]{2,1,0:T(8,128)(2,1)S(1)} collective-permute-done((bf16[2,56,1152]{2,1,0:T(8,128)(2,1)S(1)}, bf16[2,56,1152]{2,1,0:T(8,128)(2,1)S(1)}, u32[]{:S(2)}, u32[]{:S(2)}) %collective-permute-start.7) | collective-permute-done | bytes 258080 | tf_op jit(solution)/shard_map/ppermute | solution.py:33
  28.3 3.6 %collective-permute-done.10 = bf16[2,56,1152]{2,1,0:T(8,128)(2,1)S(1)} collective-permute-done((bf16[2,56,1152]{2,1,0:T(8,128)(2,1)S(1)}, bf16[2,56,1152]{2,1,0:T(8,128)(2,1)S(1)}, u32[]{:S(2)}, u32[]{:S(2)}) %collective-permute-start.10) | collective-permute-done | bytes 258080 | tf_op jit(solution)/shard_map/ppermute | solution.py:33
  32.3 1.7 %collective-permute-done.14 = bf16[4,56,1152]{2,1,0:T(8,128)(2,1)S(1)} collective-permute-done((bf16[4,56,1152]{2,1,0:T(8,128)(2,1)S(1)}, bf16[4,56,1152]{2,1,0:T(8,128)(2,1)S(1)}, u32[]{:S(2)}, u32[]{:S(2)}) %collective-permute-start.14) | collective-permute-done | bytes 516128 | tf_op jit(solution)/shard_map/ppermute | solution.py:29
  34.1 0.7 convolution_bitcast_fusion
  34.8 0.8 %multiply_reduce_fusion.1 = (f32[256]{0:T(256)S(1)}, f32[256,1152]{1,0:T(8,128)S(1)}) fusion(f32[256,1152]{1,0:T(8,128)S(1)} %convolution_bitcast_fusion, bf16[32,48,256]{2,1,0:T(8,128)(2,1)S(1)} %broadcast_select_fusion, bf16[16,56,1152]{2,1,0:T(8,128)(2,1)S(1)} %constant_dynamic-update-slice_fusion), kind=kOutput, calls=%fused_computation.17 | convolution fusion | flops 453869312 | bytes 4916224 | tf_op jit(solution)/shard_map/dot_general | solution.py:93
  36.3 0.5 fusion.13
  36.8 0.5 multiply_reduce_fusion
  37.6 0.3 collective-permute-start.16
  37.9 0.3 fusion.64
  38.2 0.3 collective-permute-start.17
  38.5 0.3 fusion.65
  38.8 0.3 fusion.63
  39.1 0.3 fusion.62
  39.4 0.3 fusion.50
  39.7 0.3 convolution_add_fusion.4
  40.1 0.3 convolution_add_fusion
  40.4 0.5 collective-permute-start.22
  40.9 0.3 convolution_add_fusion.2
  41.2 1.7 %collective-permute-start.19 = (bf16[2,56,1152]{2,1,0:T(8,128)(2,1)S(1)}, bf16[2,56,1152]{2,1,0:T(8,128)(2,1)S(1)}, u32[]{:S(2)}, u32[]{:S(2)}) collective-permute-start(bf16[2,56,1152]{2,1,0:T(8,128)(2,1)S(1)} %fusion.19), channel_id=1, source_target_pairs={{0,16},{1,17},{2,18},{3,19},{4,20},{5,21},{6,22},{7,23},{8,9},{9,8... | collective-permute-start | bytes 774152 | tf_op jit(solution)/shard_map/ppermute | solution.py:33
  42.9 0.3 convolution_add_fusion.1
  43.2 0.3 convolution_add_fusion.3
  43.6 3.2 %collective-permute-done.22 = bf16[2,56,1152]{2,1,0:T(8,128)(2,1)S(1)} collective-permute-done((bf16[2,56,1152]{2,1,0:T(8,128)(2,1)S(1)}, bf16[2,56,1152]{2,1,0:T(8,128)(2,1)S(1)}, u32[]{:S(2)}, u32[]{:S(2)}) %collective-permute-start.22) | collective-permute-done | bytes 258080 | tf_op jit(solution)/shard_map/ppermute | solution.py:33
  46.8 0.4 collective-permute-start.23
  47.3 2.0 %collective-permute-start.27 = (bf16[56,1152]{1,0:T(8,128)(2,1)S(1)}, bf16[56,1152]{1,0:T(8,128)(2,1)S(1)}, u32[]{:S(2)}, u32[]{:S(2)}) collective-permute-start(bf16[56,1152]{1,0:T(8,128)(2,1)S(1)} %fusion.45), channel_id=1, source_target_pairs={{0,1},{1,0},{2,3},{3,2},{4,5},{5,4},{6,7},{7,6},{8,24},{9,25},{10,... | collective-permute-start | bytes 387080 | tf_op jit(solution)/shard_map/ppermute | solution.py:33
  49.3 0.3 collective-permute-done.19
  49.7 2.6 %collective-permute-start.26 = (bf16[56,1152]{1,0:T(8,128)(2,1)S(1)}, bf16[56,1152]{1,0:T(8,128)(2,1)S(1)}, u32[]{:S(2)}, u32[]{:S(2)}) collective-permute-start(bf16[56,1152]{1,0:T(8,128)(2,1)S(1)} %fusion.44), channel_id=1, source_target_pairs={{0,1},{1,0},{2,3},{3,2},{4,5},{5,4},{6,7},{7,6},{8,24},{9,25},{10,... | collective-permute-start | bytes 387080 | tf_op jit(solution)/shard_map/ppermute | solution.py:33
  52.3 0.4 collective-permute-start.20
  52.6 1.1 %collective-permute-done.27 = bf16[56,1152]{1,0:T(8,128)(2,1)S(1)} collective-permute-done((bf16[56,1152]{1,0:T(8,128)(2,1)S(1)}, bf16[56,1152]{1,0:T(8,128)(2,1)S(1)}, u32[]{:S(2)}, u32[]{:S(2)}) %collective-permute-start.27) | collective-permute-done | bytes 129056 | tf_op jit(solution)/shard_map/ppermute | solution.py:33
  53.8 0.5 collective-permute-start.28
  54.3 1.3 %collective-permute-done.23 = bf16[2,56,1152]{2,1,0:T(8,128)(2,1)S(1)} collective-permute-done((bf16[2,56,1152]{2,1,0:T(8,128)(2,1)S(1)}, bf16[2,56,1152]{2,1,0:T(8,128)(2,1)S(1)}, u32[]{:S(2)}, u32[]{:S(2)}) %collective-permute-start.23) | collective-permute-done | bytes 258080 | tf_op jit(solution)/shard_map/ppermute | solution.py:33
  55.8 1.5 %collective-permute-start.24 = (bf16[56,1152]{1,0:T(8,128)(2,1)S(1)}, bf16[56,1152]{1,0:T(8,128)(2,1)S(1)}, u32[]{:S(2)}, u32[]{:S(2)}) collective-permute-start(bf16[56,1152]{1,0:T(8,128)(2,1)S(1)} %fusion.43), channel_id=1, source_target_pairs={{0,1},{1,0},{2,3},{3,2},{4,5},{5,4},{6,7},{7,6},{8,24},{9,25},{10,... | collective-permute-start | bytes 387080 | tf_op jit(solution)/shard_map/ppermute | solution.py:33
  57.3 1.7 %collective-permute-done.28 = bf16[56,1152]{1,0:T(8,128)(2,1)S(1)} collective-permute-done((bf16[56,1152]{1,0:T(8,128)(2,1)S(1)}, bf16[56,1152]{1,0:T(8,128)(2,1)S(1)}, u32[]{:S(2)}, u32[]{:S(2)}) %collective-permute-start.28) | collective-permute-done | bytes 129056 | tf_op jit(solution)/shard_map/ppermute | solution.py:29
  59.0 0.4 collective-permute-start.29
  59.4 0.6 collective-permute-done.20
  60.1 1.2 %collective-permute-start.21 = (bf16[56,1152]{1,0:T(8,128)(2,1)S(1)}, bf16[56,1152]{1,0:T(8,128)(2,1)S(1)}, u32[]{:S(2)}, u32[]{:S(2)}) collective-permute-start(bf16[56,1152]{1,0:T(8,128)(2,1)S(1)} %fusion.42), channel_id=1, source_target_pairs={{0,1},{1,0},{2,3},{3,2},{4,5},{5,4},{6,7},{7,6},{8,24},{9,25},{10,... | collective-permute-start | bytes 387080 | tf_op jit(solution)/shard_map/ppermute | solution.py:33
  61.4 1.9 %collective-permute-start.25 = (bf16[56,1152]{1,0:T(8,128)(2,1)S(1)}, bf16[56,1152]{1,0:T(8,128)(2,1)S(1)}, u32[]{:S(2)}, u32[]{:S(2)}) collective-permute-start(bf16[56,1152]{1,0:T(8,128)(2,1)S(1)} %fusion.32), channel_id=1, source_target_pairs={{0,2},{1,3},{2,0},{3,1},{4,6},{5,7},{6,4},{7,5},{8,10},{9,11},{10,... | collective-permute-start | bytes 387080 | tf_op jit(solution)/shard_map/ppermute | solution.py:29
  63.4 3.2 %collective-permute-done.29 = bf16[56,1152]{1,0:T(8,128)(2,1)S(1)} collective-permute-done((bf16[56,1152]{1,0:T(8,128)(2,1)S(1)}, bf16[56,1152]{1,0:T(8,128)(2,1)S(1)}, u32[]{:S(2)}, u32[]{:S(2)}) %collective-permute-start.29) | collective-permute-done | bytes 129056 | tf_op jit(solution)/shard_map/ppermute | solution.py:29
  66.6 0.9 %collective-permute-done.25 = bf16[56,1152]{1,0:T(8,128)(2,1)S(1)} collective-permute-done((bf16[56,1152]{1,0:T(8,128)(2,1)S(1)}, bf16[56,1152]{1,0:T(8,128)(2,1)S(1)}, u32[]{:S(2)}, u32[]{:S(2)}) %collective-permute-start.25) | collective-permute-done | bytes 129056 | tf_op jit(solution)/shard_map/ppermute | solution.py:29
  67.7 0.6 collective-permute-start.31
  68.3 1.2 %collective-permute-start.32 = (f32[8,1152]{1,0:T(8,128)S(1)}, f32[8,1152]{1,0:T(8,128)S(1)}, u32[]{:S(2)}, u32[]{:S(2)}) collective-permute-start(f32[8,1152]{1,0:T(8,128)S(1)} %slice.216), channel_id=1, source_target_pairs={{0,8},{1,9},{2,10},{3,11},{4,12},{5,13},{6,14},{7,15},{8,0},{9,1},... | collective-permute-start | bytes 110600 | tf_op jit(solution)/shard_map/ppermute | solution.py:29
  69.5 0.7 slice.215
  70.2 0.8 %collective-permute-done.30 = f32[8,1152]{1,0:T(8,128)S(1)} collective-permute-done((f32[8,1152]{1,0:T(8,128)S(1)}, f32[8,1152]{1,0:T(8,128)S(1)}, u32[]{:S(2)}, u32[]{:S(2)}) %collective-permute-start.30) | collective-permute-done | bytes 36896 | tf_op jit(solution)/shard_map/ppermute | solution.py:29
  71.0 0.8 %collective-permute-done.31 = f32[8,1152]{1,0:T(8,128)S(1)} collective-permute-done((f32[8,1152]{1,0:T(8,128)S(1)}, f32[8,1152]{1,0:T(8,128)S(1)}, u32[]{:S(2)}, u32[]{:S(2)}) %collective-permute-start.31) | collective-permute-done | bytes 36896 | tf_op jit(solution)/shard_map/ppermute | solution.py:29
  72.0 0.8 %fusion.40 = f32[32,1152]{1,0:T(8,128)} fusion(bf16[32,1152]{1,0:T(8,128)(2,1)S(1)} %copy-done, f32[8,1152]{1,0:T(8,128)S(1)} %get-tuple-element.21, f32[8,1152]{1,0:T(8,128)S(1)} %get-tuple-element.22, f32[8,1152]{1,0:T(8,128)S(1)} %get-tuple-element.23, f32[8,1152]{1,0:T(8,128)S(1)} %get-tuple-element.20, f32[32]{0:T(128)S(1)} %fusion.38, ...), kind=kLoop, calls=%fused_computation.89 | loop fusion | flops 294912 | bytes 368896 | tf_op jit(solution)/shard_map/mul | solution.py:161
  (94 shorter events, 3.9 us)
Async XLA Ops:
  2.3 9.9 %collective-permute-start = (bf16[1,56,1152]{2,1,0:T(8,128)(2,1)S(1)}, bf16[1,56,1152]{2,1,0:T(8,128)(2,1)S(1)}, u32[]{:S(2)}, u32[]{:S(2)}) collective-permute-start(bf16[1,56,1152]{2,1,0:T(8,128)(2,1)S(1)} %maximum_bitcast_fusion), channel_id=1, source_target_pairs={{0,1},{1,0},{2,3},{3,2},{4,5},{5,4},{6,7},{7,6},{8,24},{9,25},{10,... | collective-permute-start | bytes 387080 | tf_op jit(solution)/shard_map/ppermute | solution.py:33
  5.3 8.6 %collective-permute-start.2 = (bf16[1,56,1152]{2,1,0:T(8,128)(2,1)S(1)}, bf16[1,56,1152]{2,1,0:T(8,128)(2,1)S(1)}, u32[]{:S(2)}, u32[]{:S(2)}) collective-permute-start(bf16[1,56,1152]{2,1,0:T(8,128)(2,1)S(1)} %maximum_bitcast_fusion), channel_id=1, source_target_pairs={{0,2},{1,3},{2,0},{3,1},{4,6},{5,7},{6,4},{7,5},{8,10},{9,11},{10,... | collective-permute-start | bytes 387080 | tf_op jit(solution)/shard_map/ppermute | solution.py:29
  6.9 8.4 %collective-permute-start.5 = (bf16[1,56,1152]{2,1,0:T(8,128)(2,1)S(1)}, bf16[1,56,1152]{2,1,0:T(8,128)(2,1)S(1)}, u32[]{:S(2)}, u32[]{:S(2)}) collective-permute-start(bf16[1,56,1152]{2,1,0:T(8,128)(2,1)S(1)} %maximum_bitcast_fusion), channel_id=1, source_target_pairs={{0,4},{1,5},{2,6},{3,7},{4,0},{5,1},{6,2},{7,3},{8,12},{9,13},{10,... | collective-permute-start | bytes 387080 | tf_op jit(solution)/shard_map/ppermute | solution.py:29
  11.2 1.0 %copy-start.1 = (bf16[48,1152]{1,0:T(8,128)(2,1)S(1)}, bf16[48,1152]{1,0:T(8,128)(2,1)}, u32[]{:S(2)}) copy-start(bf16[48,1152]{1,0:T(8,128)(2,1)} %param.5) | copy-start | bytes 331780
  12.2 13.7 %collective-permute-start.1 = (bf16[2,56,1152]{2,1,0:T(8,128)(2,1)S(1)}, bf16[2,56,1152]{2,1,0:T(8,128)(2,1)S(1)}, u32[]{:S(2)}, u32[]{:S(2)}) collective-permute-start(bf16[2,56,1152]{2,1,0:T(8,128)(2,1)S(1)} %pad_maximum_fusion.9), channel_id=1, source_target_pairs={{0,16},{1,17},{2,18},{3,19},{4,20},{5,21},{6,22},{7,23},{8,9},{9,8... | collective-permute-start | bytes 774152 | tf_op jit(solution)/shard_map/ppermute | solution.py:33
  13.8 4.9 %collective-permute-start.3 = (bf16[1,56,1152]{2,1,0:T(8,128)(2,1)S(1)}, bf16[1,56,1152]{2,1,0:T(8,128)(2,1)S(1)}, u32[]{:S(2)}, u32[]{:S(2)}) collective-permute-start(bf16[1,56,1152]{2,1,0:T(8,128)(2,1)S(1)} %collective-permute-done.2), channel_id=1, source_target_pairs={{0,1},{1,0},{2,3},{3,2},{4,5},{5,4},{6,7},{7,6},{8,24},{9,25},{10,... | collective-permute-start | bytes 387080 | tf_op jit(solution)/shard_map/ppermute | solution.py:33
  15.2 4.9 %collective-permute-start.6 = (bf16[1,56,1152]{2,1,0:T(8,128)(2,1)S(1)}, bf16[1,56,1152]{2,1,0:T(8,128)(2,1)S(1)}, u32[]{:S(2)}, u32[]{:S(2)}) collective-permute-start(bf16[1,56,1152]{2,1,0:T(8,128)(2,1)S(1)} %collective-permute-done.5), channel_id=1, source_target_pairs={{0,1},{1,0},{2,3},{3,2},{4,5},{5,4},{6,7},{7,6},{8,24},{9,25},{10,... | collective-permute-start | bytes 387080 | tf_op jit(solution)/shard_map/ppermute | solution.py:33
  16.7 5.7 %collective-permute-start.8 = (bf16[1,56,1152]{2,1,0:T(8,128)(2,1)S(1)}, bf16[1,56,1152]{2,1,0:T(8,128)(2,1)S(1)}, u32[]{:S(2)}, u32[]{:S(2)}) collective-permute-start(bf16[1,56,1152]{2,1,0:T(8,128)(2,1)S(1)} %collective-permute-done.5), channel_id=1, source_target_pairs={{0,2},{1,3},{2,0},{3,1},{4,6},{5,7},{6,4},{7,5},{8,10},{9,11},{10,... | collective-permute-start | bytes 387080 | tf_op jit(solution)/shard_map/ppermute | solution.py:29
  18.8 8.2 %collective-permute-start.4 = (bf16[2,56,1152]{2,1,0:T(8,128)(2,1)S(1)}, bf16[2,56,1152]{2,1,0:T(8,128)(2,1)S(1)}, u32[]{:S(2)}, u32[]{:S(2)}) collective-permute-start(bf16[2,56,1152]{2,1,0:T(8,128)(2,1)S(1)} %pad_maximum_fusion.10), channel_id=1, source_target_pairs={{0,16},{1,17},{2,18},{3,19},{4,20},{5,21},{6,22},{7,23},{8,9},{9,8... | collective-permute-start | bytes 774152 | tf_op jit(solution)/shard_map/ppermute | solution.py:33
  20.2 5.3 %collective-permute-start.9 = (bf16[1,56,1152]{2,1,0:T(8,128)(2,1)S(1)}, bf16[1,56,1152]{2,1,0:T(8,128)(2,1)S(1)}, u32[]{:S(2)}, u32[]{:S(2)}) collective-permute-start(bf16[1,56,1152]{2,1,0:T(8,128)(2,1)S(1)} %collective-permute-done.6), channel_id=1, source_target_pairs={{0,2},{1,3},{2,0},{3,1},{4,6},{5,7},{6,4},{7,5},{8,10},{9,11},{10,... | collective-permute-start | bytes 387080 | tf_op jit(solution)/shard_map/ppermute | solution.py:29
  20.7 7.2 %collective-permute-start.7 = (bf16[2,56,1152]{2,1,0:T(8,128)(2,1)S(1)}, bf16[2,56,1152]{2,1,0:T(8,128)(2,1)S(1)}, u32[]{:S(2)}, u32[]{:S(2)}) collective-permute-start(bf16[2,56,1152]{2,1,0:T(8,128)(2,1)S(1)} %pad_maximum_fusion.11), channel_id=1, source_target_pairs={{0,16},{1,17},{2,18},{3,19},{4,20},{5,21},{6,22},{7,23},{8,9},{9,8... | collective-permute-start | bytes 774152 | tf_op jit(solution)/shard_map/ppermute | solution.py:33
  22.4 17.6 %collective-permute-start.15 = (bf16[768,256]{1,0:T(8,128)(2,1)S(1)}, bf16[768,256]{1,0:T(8,128)(2,1)S(1)}, u32[]{:S(2)}, u32[]{:S(2)}) collective-permute-start(bf16[768,256]{1,0:T(8,128)(2,1)S(1)} %bitcast.108), channel_id=1, source_target_pairs={{0,8},{1,9},{2,10},{3,11},{4,12},{5,13},{6,14},{7,15},{8,0},{9,1},... | collective-permute-start | bytes 1179656 | tf_op jit(solution)/shard_map/ppermute | solution.py:29
  25.5 6.4 %collective-permute-start.10 = (bf16[2,56,1152]{2,1,0:T(8,128)(2,1)S(1)}, bf16[2,56,1152]{2,1,0:T(8,128)(2,1)S(1)}, u32[]{:S(2)}, u32[]{:S(2)}) collective-permute-start(bf16[2,56,1152]{2,1,0:T(8,128)(2,1)S(1)} %pad_maximum_fusion.12), channel_id=1, source_target_pairs={{0,16},{1,17},{2,18},{3,19},{4,20},{5,21},{6,22},{7,23},{8,9},{9,8... | collective-permute-start | bytes 774152 | tf_op jit(solution)/shard_map/ppermute | solution.py:33
  26.0 6.1 %collective-permute-start.11 = (bf16[4,56,1152]{2,1,0:T(8,128)(2,1)S(1)}, bf16[4,56,1152]{2,1,0:T(8,128)(2,1)S(1)}, u32[]{:S(2)}, u32[]{:S(2)}) collective-permute-start(bf16[4,56,1152]{2,1,0:T(8,128)(2,1)S(1)} %pad_maximum_fusion.5), channel_id=1, source_target_pairs={{0,8},{1,9},{2,10},{3,11},{4,12},{5,13},{6,14},{7,15},{8,0},{9,1},... | collective-permute-start | bytes 1548296 | tf_op jit(solution)/shard_map/ppermute | solution.py:29
  27.1 5.1 %collective-permute-start.12 = (bf16[4,56,1152]{2,1,0:T(8,128)(2,1)S(1)}, bf16[4,56,1152]{2,1,0:T(8,128)(2,1)S(1)}, u32[]{:S(2)}, u32[]{:S(2)}) collective-permute-start(bf16[4,56,1152]{2,1,0:T(8,128)(2,1)S(1)} %pad_maximum_fusion.6), channel_id=1, source_target_pairs={{0,8},{1,9},{2,10},{3,11},{4,12},{5,13},{6,14},{7,15},{8,0},{9,1},... | collective-permute-start | bytes 1548296 | tf_op jit(solution)/shard_map/ppermute | solution.py:29
  28.0 4.2 %collective-permute-start.13 = (bf16[4,56,1152]{2,1,0:T(8,128)(2,1)S(1)}, bf16[4,56,1152]{2,1,0:T(8,128)(2,1)S(1)}, u32[]{:S(2)}, u32[]{:S(2)}) collective-permute-start(bf16[4,56,1152]{2,1,0:T(8,128)(2,1)S(1)} %pad_maximum_fusion.7), channel_id=1, source_target_pairs={{0,8},{1,9},{2,10},{3,11},{4,12},{5,13},{6,14},{7,15},{8,0},{9,1},... | collective-permute-start | bytes 1548296 | tf_op jit(solution)/shard_map/ppermute | solution.py:29
  32.0 2.0 %collective-permute-start.14 = (bf16[4,56,1152]{2,1,0:T(8,128)(2,1)S(1)}, bf16[4,56,1152]{2,1,0:T(8,128)(2,1)S(1)}, u32[]{:S(2)}, u32[]{:S(2)}) collective-permute-start(bf16[4,56,1152]{2,1,0:T(8,128)(2,1)S(1)} %pad_maximum_fusion.8), channel_id=1, source_target_pairs={{0,8},{1,9},{2,10},{3,11},{4,12},{5,13},{6,14},{7,15},{8,0},{9,1},... | collective-permute-start | bytes 1548296 | tf_op jit(solution)/shard_map/ppermute | solution.py:29
  35.6 0.7 copy-start.2
  35.9 3.8 %collective-permute-start.18 = (bf16[256,1152]{1,0:T(8,128)(2,1)S(1)}, bf16[256,1152]{1,0:T(8,128)(2,1)S(1)}, u32[]{:S(2)}, u32[]{:S(2)}) collective-permute-start(bf16[256,1152]{1,0:T(8,128)(2,1)S(1)} %multiply_convert_fusion.1), channel_id=1, source_target_pairs={{0,8},{1,9},{2,10},{3,11},{4,12},{5,13},{6,14},{7,15},{8,0},{9,1},... | collective-permute-start | bytes 1769480 | tf_op jit(solution)/shard_map/ppermute | solution.py:29
  37.6 2.5 %collective-permute-start.16 = (bf16[256,1152]{1,0:T(8,128)(2,1)S(1)}, bf16[256,1152]{1,0:T(8,128)(2,1)S(1)}, u32[]{:S(2)}, u32[]{:S(2)}) collective-permute-start(bf16[256,1152]{1,0:T(8,128)(2,1)S(1)} %multiply_convert_fusion), channel_id=1, source_target_pairs={{0,8},{1,9},{2,10},{3,11},{4,12},{5,13},{6,14},{7,15},{8,0},{9,1},... | collective-permute-start | bytes 1769480 | tf_op jit(solution)/shard_map/ppermute | solution.py:29
  38.2 1.5 %collective-permute-start.17 = (bf16[256,128]{1,0:T(8,128)(2,1)S(1)}, bf16[256,128]{1,0:T(8,128)(2,1)S(1)}, u32[]{:S(2)}, u32[]{:S(2)}) collective-permute-start(bf16[256,128]{1,0:T(8,128)(2,1)S(1)} %slice.188), channel_id=1, source_target_pairs={{0,8},{1,9},{2,10},{3,11},{4,12},{5,13},{6,14},{7,15},{8,0},{9,1},... | collective-permute-start | bytes 196616 | tf_op jit(solution)/shard_map/ppermute | solution.py:29
  40.4 6.4 %collective-permute-start.22 = (bf16[2,56,1152]{2,1,0:T(8,128)(2,1)S(1)}, bf16[2,56,1152]{2,1,0:T(8,128)(2,1)S(1)}, u32[]{:S(2)}, u32[]{:S(2)}) collective-permute-start(bf16[2,56,1152]{2,1,0:T(8,128)(2,1)S(1)} %fusion.15), channel_id=1, source_target_pairs={{0,16},{1,17},{2,18},{3,19},{4,20},{5,21},{6,22},{7,23},{8,9},{9,8... | collective-permute-start | bytes 774152 | tf_op jit(solution)/shard_map/ppermute | solution.py:33
  41.2 8.3 %collective-permute-start.19 = (bf16[2,56,1152]{2,1,0:T(8,128)(2,1)S(1)}, bf16[2,56,1152]{2,1,0:T(8,128)(2,1)S(1)}, u32[]{:S(2)}, u32[]{:S(2)}) collective-permute-start(bf16[2,56,1152]{2,1,0:T(8,128)(2,1)S(1)} %fusion.19), channel_id=1, source_target_pairs={{0,16},{1,17},{2,18},{3,19},{4,20},{5,21},{6,22},{7,23},{8,9},{9,8... | collective-permute-start | bytes 774152 | tf_op jit(solution)/shard_map/ppermute | solution.py:33
  46.8 8.8 %collective-permute-start.23 = (bf16[2,56,1152]{2,1,0:T(8,128)(2,1)S(1)}, bf16[2,56,1152]{2,1,0:T(8,128)(2,1)S(1)}, u32[]{:S(2)}, u32[]{:S(2)}) collective-permute-start(bf16[2,56,1152]{2,1,0:T(8,128)(2,1)S(1)} %fusion.24), channel_id=1, source_target_pairs={{0,16},{1,17},{2,18},{3,19},{4,20},{5,21},{6,22},{7,23},{8,9},{9,8... | collective-permute-start | bytes 774152 | tf_op jit(solution)/shard_map/ppermute | solution.py:33
  47.3 6.5 %collective-permute-start.27 = (bf16[56,1152]{1,0:T(8,128)(2,1)S(1)}, bf16[56,1152]{1,0:T(8,128)(2,1)S(1)}, u32[]{:S(2)}, u32[]{:S(2)}) collective-permute-start(bf16[56,1152]{1,0:T(8,128)(2,1)S(1)} %fusion.45), channel_id=1, source_target_pairs={{0,1},{1,0},{2,3},{3,2},{4,5},{5,4},{6,7},{7,6},{8,24},{9,25},{10,... | collective-permute-start | bytes 387080 | tf_op jit(solution)/shard_map/ppermute | solution.py:33
  49.7 7.6 %collective-permute-start.26 = (bf16[56,1152]{1,0:T(8,128)(2,1)S(1)}, bf16[56,1152]{1,0:T(8,128)(2,1)S(1)}, u32[]{:S(2)}, u32[]{:S(2)}) collective-permute-start(bf16[56,1152]{1,0:T(8,128)(2,1)S(1)} %fusion.44), channel_id=1, source_target_pairs={{0,1},{1,0},{2,3},{3,2},{4,5},{5,4},{6,7},{7,6},{8,24},{9,25},{10,... | collective-permute-start | bytes 387080 | tf_op jit(solution)/shard_map/ppermute | solution.py:33
  52.3 7.8 %collective-permute-start.20 = (bf16[2,56,1152]{2,1,0:T(8,128)(2,1)S(1)}, bf16[2,56,1152]{2,1,0:T(8,128)(2,1)S(1)}, u32[]{:S(2)}, u32[]{:S(2)}) collective-permute-start(bf16[2,56,1152]{2,1,0:T(8,128)(2,1)S(1)} %fusion.25), channel_id=1, source_target_pairs={{0,16},{1,17},{2,18},{3,19},{4,20},{5,21},{6,22},{7,23},{8,9},{9,8... | collective-permute-start | bytes 774152 | tf_op jit(solution)/shard_map/ppermute | solution.py:33
  53.8 5.2 %collective-permute-start.28 = (bf16[56,1152]{1,0:T(8,128)(2,1)S(1)}, bf16[56,1152]{1,0:T(8,128)(2,1)S(1)}, u32[]{:S(2)}, u32[]{:S(2)}) collective-permute-start(bf16[56,1152]{1,0:T(8,128)(2,1)S(1)} %fusion.27), channel_id=1, source_target_pairs={{0,2},{1,3},{2,0},{3,1},{4,6},{5,7},{6,4},{7,5},{8,10},{9,11},{10,... | collective-permute-start | bytes 387080 | tf_op jit(solution)/shard_map/ppermute | solution.py:29
  55.7 7.6 %copy-start = (bf16[32,1152]{1,0:T(8,128)(2,1)S(1)}, bf16[32,1152]{1,0:T(8,128)(2,1)}, u32[]{:S(2)}) copy-start(bf16[32,1152]{1,0:T(8,128)(2,1)} %param.7) | copy-start | bytes 221188
  55.8 5.6 %collective-permute-start.24 = (bf16[56,1152]{1,0:T(8,128)(2,1)S(1)}, bf16[56,1152]{1,0:T(8,128)(2,1)S(1)}, u32[]{:S(2)}, u32[]{:S(2)}) collective-permute-start(bf16[56,1152]{1,0:T(8,128)(2,1)S(1)} %fusion.43), channel_id=1, source_target_pairs={{0,1},{1,0},{2,3},{3,2},{4,5},{5,4},{6,7},{7,6},{8,24},{9,25},{10,... | collective-permute-start | bytes 387080 | tf_op jit(solution)/shard_map/ppermute | solution.py:33
  59.0 7.6 %collective-permute-start.29 = (bf16[56,1152]{1,0:T(8,128)(2,1)S(1)}, bf16[56,1152]{1,0:T(8,128)(2,1)S(1)}, u32[]{:S(2)}, u32[]{:S(2)}) collective-permute-start(bf16[56,1152]{1,0:T(8,128)(2,1)S(1)} %fusion.30), channel_id=1, source_target_pairs={{0,4},{1,5},{2,6},{3,7},{4,0},{5,1},{6,2},{7,3},{8,12},{9,13},{10,... | collective-permute-start | bytes 387080 | tf_op jit(solution)/shard_map/ppermute | solution.py:29
  60.1 6.5 %collective-permute-start.21 = (bf16[56,1152]{1,0:T(8,128)(2,1)S(1)}, bf16[56,1152]{1,0:T(8,128)(2,1)S(1)}, u32[]{:S(2)}, u32[]{:S(2)}) collective-permute-start(bf16[56,1152]{1,0:T(8,128)(2,1)S(1)} %fusion.42), channel_id=1, source_target_pairs={{0,1},{1,0},{2,3},{3,2},{4,5},{5,4},{6,7},{7,6},{8,24},{9,25},{10,... | collective-permute-start | bytes 387080 | tf_op jit(solution)/shard_map/ppermute | solution.py:33
  61.4 6.1 %collective-permute-start.25 = (bf16[56,1152]{1,0:T(8,128)(2,1)S(1)}, bf16[56,1152]{1,0:T(8,128)(2,1)S(1)}, u32[]{:S(2)}, u32[]{:S(2)}) collective-permute-start(bf16[56,1152]{1,0:T(8,128)(2,1)S(1)} %fusion.32), channel_id=1, source_target_pairs={{0,2},{1,3},{2,0},{3,1},{4,6},{5,7},{6,4},{7,5},{8,10},{9,11},{10,... | collective-permute-start | bytes 387080 | tf_op jit(solution)/shard_map/ppermute | solution.py:29
  67.6 3.4 %collective-permute-start.30 = (f32[8,1152]{1,0:T(8,128)S(1)}, f32[8,1152]{1,0:T(8,128)S(1)}, u32[]{:S(2)}, u32[]{:S(2)}) collective-permute-start(f32[8,1152]{1,0:T(8,128)S(1)} %slice.216), channel_id=1, source_target_pairs={{0,24},{1,25},{2,26},{3,27},{4,28},{5,29},{6,30},{7,31},{8,16},{9,... | collective-permute-start | bytes 110600 | tf_op jit(solution)/shard_map/ppermute | solution.py:29
  67.7 4.2 %collective-permute-start.31 = (f32[8,1152]{1,0:T(8,128)S(1)}, f32[8,1152]{1,0:T(8,128)S(1)}, u32[]{:S(2)}, u32[]{:S(2)}) collective-permute-start(f32[8,1152]{1,0:T(8,128)S(1)} %slice.216), channel_id=1, source_target_pairs={{0,16},{1,17},{2,18},{3,19},{4,20},{5,21},{6,22},{7,23},{8,24},{9,... | collective-permute-start | bytes 110600 | tf_op jit(solution)/shard_map/ppermute | solution.py:29
  68.3 3.6 %collective-permute-start.32 = (f32[8,1152]{1,0:T(8,128)S(1)}, f32[8,1152]{1,0:T(8,128)S(1)}, u32[]{:S(2)}, u32[]{:S(2)}) collective-permute-start(f32[8,1152]{1,0:T(8,128)S(1)} %slice.216), channel_id=1, source_target_pairs={{0,8},{1,9},{2,10},{3,11},{4,12},{5,13},{6,14},{7,15},{8,0},{9,1},... | collective-permute-start | bytes 110600 | tf_op jit(solution)/shard_map/ppermute | solution.py:29
